TPU v7x, 32 devices: a whole 2x2x4 slice. The times are simulated.
32 devices in a mesh: ctx: 8 (over y, x, core), fsdp: 4 (over z).
Axes of the slice: x: 2, y: 2, z: 4, core: 2. Of those that a mesh axis runs over, the one named last changes fastest.
Arguments:
- hidden_in: bfloat16 [4, 1536, 2048], P('fsdp', 'ctx'), may hold values from -6 to 6
- cotangent: bfloat16 [4, 1536, 2048], P('fsdp', 'ctx'), may hold values from -6 to 6
- routes: int32 [4, 1536, 8], P('fsdp', 'ctx'), may hold values from 0 to 31, all different within a row; in each aligned block of 192 rows (0 to 191, 192 to 383, ..., all dimensions but the last counted through in order) at most 64 rows name the same one
- attn_gain: bfloat16 [2048], P(('ctx', 'fsdp')), may hold values from 0.25 to 1.75
- query_gain: bfloat16 [2048], P(('ctx', 'fsdp')), may hold values from 0.25 to 1.75
- key_gain: bfloat16 [2048], P(('ctx', 'fsdp')), may hold values from 0.25 to 1.75
- ffn_gain: bfloat16 [2048], P(('ctx', 'fsdp')), may hold values from 0.25 to 1.75
- w_query: bfloat16 [2048, 2048], P(('ctx', 'fsdp')), may hold values from -0.125 to 0.125
- w_key: bfloat16 [2048, 2048], P(('ctx', 'fsdp')), may hold values from -0.125 to 0.125
- w_value: bfloat16 [2048, 2048], P(('ctx', 'fsdp')), may hold values from -0.125 to 0.125
- w_out: bfloat16 [2048, 2048], P(('ctx', 'fsdp')), may hold values from -0.5 to 0.5
- w_router: bfloat16 [2048, 32], P(('ctx', 'fsdp')), may hold values from -0.0625 to 0.0625
- w_gate: bfloat16 [32, 2048, 1024], P('ctx', 'fsdp'), may hold values from -0.125 to 0.125
- w_up: bfloat16 [32, 2048, 1024], P('ctx', 'fsdp'), may hold values from -0.125 to 0.125
- w_down: bfloat16 [32, 1024, 2048], P('ctx', 'fsdp'), may hold values from -0.75 to 0.75
Outputs:
- out_hidden: bfloat16 [4, 1536, 2048], P('fsdp', 'ctx')
- grad_hidden: float32 [4, 1536, 2048], P('fsdp', 'ctx')
- grad_attn_gain: float32 [2048], P(('ctx', 'fsdp'))
- grad_query_gain: float32 [2048], P(('ctx', 'fsdp'))
- grad_key_gain: float32 [2048], P(('ctx', 'fsdp'))
- grad_ffn_gain: float32 [2048], P(('ctx', 'fsdp'))
- grad_query: float32 [2048, 2048], P(('ctx', 'fsdp'))
- grad_key: float32 [2048, 2048], P(('ctx', 'fsdp'))
- grad_value: float32 [2048, 2048], P(('ctx', 'fsdp'))
- grad_out: float32 [2048, 2048], P(('ctx', 'fsdp'))
- grad_router: float32 [2048, 32], P(('ctx', 'fsdp'))
- grad_gate: float32 [32, 2048, 1024], P('ctx', 'fsdp')
- grad_up: float32 [32, 2048, 1024], P('ctx', 'fsdp')
- grad_down: float32 [32, 1024, 2048], P('ctx', 'fsdp')
Inputs may be any that keep to these rules, and one draw needn't show every extreme that they name: `routes`: each row names 8 different experts. In each aligned block of 192 tokens (the tokens of one device), no expert is named by more than 64 tokens, a bound that some block reaches.
All inputs are finite; a program needn't handle non-finite values.
Results may differ from a plain program's by a relative error of at most 0.018.
Values may be sent and summed in bfloat16 or wider, within the bound.
A program may use at most 384 MiB of HBM per device.

v0:
```python
import jax
import jax.numpy as jnp
from jax import lax
from jax.sharding import PartitionSpec as P

HEADS = 16


epsilon = 1e-05
neg_large = -1e30


def from_behind(x, axis, by):
    length = lax.axis_size(axis)
    return lax.ppermute(x, axis, [(i, (i + by) % length) for i in range(length)])


def rms_apply(vector, gain):
    scale = lax.rsqrt(jnp.mean(vector * vector, axis=-1, keepdims=True) + epsilon)
    normed = vector * scale
    return (normed * gain, normed, scale)


def rms_back(grad, normed, scale, gain):
    dnormed = grad * gain
    gain_grad = jnp.sum(grad * normed, axis=0)
    inner = jnp.mean(dnormed * normed, axis=-1, keepdims=True)
    return (scale * (dnormed - normed * inner), gain_grad)


def token_position(index, tokens, ctx_count):
    half = tokens // 2
    device = index // tokens
    local = index % tokens
    return jnp.where(
        local < half, device * half + local, (2 * ctx_count - 1 - device) * half + local - half
    )


def rotation(positions, head_size):
    half = head_size // 2
    freq = 10000.0 ** (-jnp.arange(half, dtype=jnp.float32) * (2.0 / head_size))
    angle = positions.astype(jnp.float32)[:, None] * freq[None, :]
    return (jnp.cos(angle)[:, None, :], jnp.sin(angle)[:, None, :])


def rotate(vector, cosine, sine):
    half = vector.shape[-1] // 2
    first = vector[..., :half]
    second = vector[..., half:]
    return jnp.concatenate(
        [first * cosine - second * sine, second * cosine + first * sine], axis=-1
    )


def contract_rows(left, right):
    return lax.dot_general(
        left, right, (((0,), (0,)), ((), ())), preferred_element_type=jnp.float32
    )


def contract_cols(left, right):
    return lax.dot_general(
        left, right, (((1,), (1,)), ((), ())), preferred_element_type=jnp.float32
    )


def body(
    hidden_in,
    cotangent,
    routes,
    attn_gain,
    query_gain,
    key_gain,
    ffn_gain,
    w_query,
    w_key,
    w_value,
    w_out,
    w_router,
    w_gate,
    w_up,
    w_down,
):
    tokens = hidden_in.shape[1]
    width = hidden_in.shape[2]
    heads = HEADS
    head_size = width // heads
    ctx_count = lax.axis_size("ctx")
    top = routes.shape[2]
    exp_local = w_gate.shape[0]
    experts = exp_local * ctx_count
    capacity = tokens * top * 4 // (3 * experts)
    scale = head_size ** (-0.5)
    (
        query_full,
        key_full,
        value_full,
        out_full,
        router_full,
        attn_scale,
        query_scale,
        key_scale,
        ffn_scale,
    ) = (
        lax.all_gather(w_query, ("ctx", "fsdp"), axis=0, tiled=True),
        lax.all_gather(w_key, ("ctx", "fsdp"), axis=0, tiled=True),
        lax.all_gather(w_value, ("ctx", "fsdp"), axis=0, tiled=True),
        lax.all_gather(w_out, ("ctx", "fsdp"), axis=0, tiled=True),
        lax.all_gather(w_router, ("ctx", "fsdp"), axis=0, tiled=True),
        lax.all_gather(attn_gain, ("ctx", "fsdp"), axis=0, tiled=True),
        lax.all_gather(query_gain, ("ctx", "fsdp"), axis=0, tiled=True),
        lax.all_gather(key_gain, ("ctx", "fsdp"), axis=0, tiled=True),
        lax.all_gather(ffn_gain, ("ctx", "fsdp"), axis=0, tiled=True),
    )
    gate_full, up_full, down_full = (
        lax.all_gather(w_gate, "fsdp", axis=1, tiled=True),
        lax.all_gather(w_up, "fsdp", axis=1, tiled=True),
        lax.all_gather(w_down, "fsdp", axis=1, tiled=True),
    )
    rows_in = hidden_in[0].astype(jnp.float32)
    hidden_one, normed_one, scale_one = rms_apply(rows_in, attn_scale.astype(jnp.float32))
    attn_input = hidden_one.astype(jnp.bfloat16)
    queries = jnp.dot(attn_input, query_full, preferred_element_type=jnp.float32)
    keys_proj = jnp.dot(attn_input, key_full, preferred_element_type=jnp.float32)
    values_proj = jnp.dot(attn_input, value_full, preferred_element_type=jnp.float32)
    query_normed_gain, query_normed, query_rms = rms_apply(queries, query_scale.astype(jnp.float32))
    key_normed_gain, key_normed, key_rms = rms_apply(keys_proj, key_scale.astype(jnp.float32))
    ctx_index = lax.axis_index("ctx")
    positions = token_position(
        ctx_index * tokens + jnp.arange(tokens, dtype=jnp.int32), tokens, ctx_count
    )
    cosine, sine = rotation(positions, head_size)
    query_rot = rotate(query_normed_gain.reshape(tokens, heads, head_size), cosine, sine).astype(
        jnp.bfloat16
    )
    key_rot = (
        rotate(key_normed_gain.reshape(tokens, heads, head_size), cosine, sine)
        .astype(jnp.bfloat16)
        .reshape(tokens, width)
    )
    value_low = values_proj.astype(jnp.bfloat16)

    def masked_scores(key_flat, start):
        key_piece = key_flat.reshape(-1, heads, head_size)
        count = key_piece.shape[0]
        scores = (
            jnp.einsum("qhd,khd->hqk", query_rot, key_piece, preferred_element_type=jnp.float32)
            * scale
        )
        key_pos = token_position(start + jnp.arange(count, dtype=jnp.int32), tokens, ctx_count)
        allowed = (key_pos[None, :] <= positions[:, None])[None]
        return (scores, allowed)

    run_max = jnp.full((heads, tokens), neg_large, jnp.float32)
    scores, allowed = masked_scores(
        lax.all_gather(key_rot, "ctx", axis=0, tiled=True), jnp.int32(0)
    )
    new_max = jnp.maximum(run_max, jnp.max(jnp.where(allowed, scores, neg_large), axis=-1))
    weights = jnp.where(allowed, jnp.exp(scores - new_max[..., None]), 0.0)
    run_sum = jnp.sum(weights, axis=-1)
    run_max, run_sum = (new_max, run_sum)
    log_total = run_max + jnp.log(run_sum)
    scores, allowed = masked_scores(
        lax.all_gather(key_rot, "ctx", axis=0, tiled=True), jnp.int32(0)
    )
    value_piece = lax.all_gather(value_low, "ctx", axis=0, tiled=True).reshape(-1, heads, head_size)
    probs = jnp.where(allowed, jnp.exp(scores - log_total[..., None]), 0.0)
    acc_low = jnp.einsum(
        "hqk,khd->qhd", probs.astype(jnp.bfloat16), value_piece, preferred_element_type=jnp.float32
    )
    acc_exact = jnp.einsum(
        "hqk,khd->qhd", probs, value_piece.astype(jnp.float32), preferred_element_type=jnp.float32
    )
    out_low = acc_low.reshape(tokens, width).astype(jnp.bfloat16)
    resid_one = rows_in + jnp.dot(out_low, out_full, preferred_element_type=jnp.float32)
    hidden_two, normed_two, scale_two = rms_apply(resid_one, ffn_scale.astype(jnp.float32))
    ffn_input = hidden_two.astype(jnp.bfloat16)
    logits = jnp.dot(ffn_input, router_full, preferred_element_type=jnp.float32)
    route_ids = routes[0]
    picks = (route_ids[:, :, None] == jnp.arange(experts, dtype=jnp.int32)).astype(jnp.float32)
    chosen = jnp.sum(picks * logits[:, None, :], axis=-1)
    gates = jax.nn.softmax(chosen, axis=-1)
    flat_ids = route_ids.reshape(-1)
    onehot_int = (flat_ids[:, None] == jnp.arange(experts, dtype=jnp.int32)).astype(jnp.int32)
    rank = jnp.sum(jnp.cumsum(onehot_int, axis=0) * onehot_int, axis=1) - 1
    slot = flat_ids * capacity + rank
    entries = tokens * top
    slot_entry = (
        jnp.full((experts * capacity,), entries, jnp.int32)
        .at[slot]
        .set(jnp.arange(entries, dtype=jnp.int32))
    )
    slot_token = slot_entry // top
    input_padded = jnp.concatenate([ffn_input, jnp.zeros((1, width), jnp.bfloat16)], axis=0)
    outgoing = input_padded[slot_token].reshape(ctx_count, exp_local * capacity, width)
    arrived = lax.all_to_all(outgoing, "ctx", split_axis=0, concat_axis=0, tiled=True).reshape(
        ctx_count, exp_local, capacity, width
    )
    gate_pre = jnp.einsum("secd,edf->secf", arrived, gate_full, preferred_element_type=jnp.float32)
    up_pre = jnp.einsum("secd,edf->secf", arrived, up_full, preferred_element_type=jnp.float32)
    activated = jax.nn.silu(gate_pre)
    inner_low = (activated * up_pre).astype(jnp.bfloat16)
    produced = jnp.einsum(
        "secf,efd->secd", inner_low, down_full, preferred_element_type=jnp.float32
    ).astype(jnp.bfloat16)
    returned = lax.all_to_all(
        produced.reshape(ctx_count, exp_local * capacity, width),
        "ctx",
        split_axis=0,
        concat_axis=0,
        tiled=True,
    ).reshape(experts * capacity, width)
    picked = returned[slot].reshape(tokens, top, width).astype(jnp.float32)
    resid_two = resid_one + jnp.sum(gates[:, :, None] * picked, axis=1)
    out_hidden = resid_two.astype(jnp.bfloat16)[None]
    grad_two = cotangent[0].astype(jnp.float32)
    gate_grad = jnp.sum(picked * grad_two[:, None, :], axis=-1)
    chosen_grad = gates * (gate_grad - jnp.sum(gates * gate_grad, axis=-1, keepdims=True))
    logit_grad = jnp.sum(picks * chosen_grad[:, :, None], axis=1).astype(jnp.bfloat16)
    router_grad = contract_rows(ffn_input, logit_grad)
    input_grad = contract_cols(logit_grad, router_full)
    route_grad = (
        (gates[:, :, None] * grad_two[:, None, :]).astype(jnp.bfloat16).reshape(entries, width)
    )
    route_padded = jnp.concatenate([route_grad, jnp.zeros((1, width), jnp.bfloat16)], axis=0)
    grad_out_rows = route_padded[slot_entry].reshape(ctx_count, exp_local * capacity, width)
    arrived_grad = lax.all_to_all(
        grad_out_rows, "ctx", split_axis=0, concat_axis=0, tiled=True
    ).reshape(ctx_count, exp_local, capacity, width)
    inner_grad = jnp.einsum(
        "secd,efd->secf", arrived_grad, down_full, preferred_element_type=jnp.float32
    )
    down_grad = jnp.einsum(
        "secf,secd->efd", inner_low, arrived_grad, preferred_element_type=jnp.float32
    )
    sigmoid_gate = jax.nn.sigmoid(gate_pre)
    gate_pre_grad = (
        inner_grad * up_pre * sigmoid_gate * (1.0 + gate_pre * (1.0 - sigmoid_gate))
    ).astype(jnp.bfloat16)
    up_pre_grad = (inner_grad * activated).astype(jnp.bfloat16)
    gate_grad_full = jnp.einsum(
        "secd,secf->edf", arrived, gate_pre_grad, preferred_element_type=jnp.float32
    )
    up_grad_full = jnp.einsum(
        "secd,secf->edf", arrived, up_pre_grad, preferred_element_type=jnp.float32
    )
    rows_grad = jnp.einsum(
        "secf,edf->secd", gate_pre_grad, gate_full, preferred_element_type=jnp.float32
    )
    rows_grad = rows_grad + jnp.einsum(
        "secf,edf->secd", up_pre_grad, up_full, preferred_element_type=jnp.float32
    )
    came_back = lax.all_to_all(
        rows_grad.astype(jnp.bfloat16).reshape(ctx_count, exp_local * capacity, width),
        "ctx",
        split_axis=0,
        concat_axis=0,
        tiled=True,
    ).reshape(experts * capacity, width)
    input_grad = input_grad + jnp.sum(
        came_back[slot].reshape(tokens, top, width).astype(jnp.float32), axis=1
    )
    grad_gate, grad_up, grad_down = (
        lax.psum_scatter(
            gate_grad_full.astype(jnp.bfloat16), "fsdp", scatter_dimension=1, tiled=True
        ).astype(jnp.float32),
        lax.psum_scatter(
            up_grad_full.astype(jnp.bfloat16), "fsdp", scatter_dimension=1, tiled=True
        ).astype(jnp.float32),
        lax.psum_scatter(
            down_grad.astype(jnp.bfloat16), "fsdp", scatter_dimension=1, tiled=True
        ).astype(jnp.float32),
    )
    resid_norm_grad, ffn_gain_grad = rms_back(
        input_grad, normed_two, scale_two, ffn_scale.astype(jnp.float32)
    )
    grad_one = grad_two + resid_norm_grad
    attn_grad_low = grad_one.astype(jnp.bfloat16)
    out_weight_grad = contract_rows(out_low, attn_grad_low)
    grad_attn_rows = (
        contract_cols(attn_grad_low, out_full)
        .astype(jnp.bfloat16)
        .reshape(tokens, heads, head_size)
    )
    delta = jnp.sum(grad_attn_rows.astype(jnp.float32) * acc_exact, axis=-1).T

    def back_terms(key_flat, value_flat, start):
        key_piece = key_flat.reshape(-1, heads, head_size)
        value_piece = value_flat.reshape(-1, heads, head_size)
        count = key_piece.shape[0]
        scores, allowed = masked_scores(key_flat, start)
        probs = jnp.where(allowed, jnp.exp(scores - log_total[..., None]), 0.0)
        value_term = jnp.einsum(
            "hqk,qhd->khd",
            probs.astype(jnp.bfloat16),
            grad_attn_rows,
            preferred_element_type=jnp.float32,
        ).reshape(count, width)
        prob_grad = jnp.einsum(
            "qhd,khd->hqk", grad_attn_rows, value_piece, preferred_element_type=jnp.float32
        )
        score_grad = (probs * (prob_grad - delta[..., None])).astype(jnp.bfloat16)
        query_term = scale * jnp.einsum(
            "hqk,khd->qhd", score_grad, key_piece, preferred_element_type=jnp.float32
        )
        key_term = scale * jnp.einsum(
            "hqk,qhd->khd", score_grad, query_rot, preferred_element_type=jnp.float32
        ).reshape(count, width)
        return (query_term, key_term, value_term)

    def cycle_turn(turn, carry):
        key_held, value_held, key_acc, value_acc, query_grad = carry
        anchor = jnp.mod(ctx_index - turn, ctx_count)
        query_term, key_term, value_term = back_terms(key_held, value_held, anchor * tokens)
        key_held, value_held = from_behind((key_held, value_held), "ctx", 1)
        key_acc, value_acc = from_behind((key_acc + key_term, value_acc + value_term), "ctx", 1)
        return (key_held, value_held, key_acc, value_acc, query_grad + query_term)

    cycle_state = (
        key_rot,
        value_low,
        jnp.zeros((tokens, width), jnp.float32),
        jnp.zeros((tokens, width), jnp.float32),
        jnp.zeros((tokens, heads, head_size), jnp.float32),
    )
    cycle_final = lax.fori_loop(0, ctx_count, cycle_turn, cycle_state)
    key_rot_grad = cycle_final[2]
    value_grad = cycle_final[3]
    query_rot_grad = cycle_final[4]
    query_back = rotate(query_rot_grad, cosine, -sine).reshape(tokens, width)
    key_back = rotate(key_rot_grad.reshape(tokens, heads, head_size), cosine, -sine).reshape(
        tokens, width
    )
    query_grad_pre, query_gain_grad = rms_back(
        query_back, query_normed, query_rms, query_scale.astype(jnp.float32)
    )
    key_grad_pre, key_gain_grad = rms_back(
        key_back, key_normed, key_rms, key_scale.astype(jnp.float32)
    )
    query_grad_low = query_grad_pre.astype(jnp.bfloat16)
    key_grad_low = key_grad_pre.astype(jnp.bfloat16)
    value_grad_low = value_grad.astype(jnp.bfloat16)
    query_weight_grad = contract_rows(attn_input, query_grad_low)
    key_weight_grad = contract_rows(attn_input, key_grad_low)
    value_weight_grad = contract_rows(attn_input, value_grad_low)
    attn_input_grad = (
        contract_cols(query_grad_low, query_full)
        + contract_cols(key_grad_low, key_full)
        + contract_cols(value_grad_low, value_full)
    )
    input_norm_grad, attn_gain_grad = rms_back(
        attn_input_grad, normed_one, scale_one, attn_scale.astype(jnp.float32)
    )
    grad_hidden = (grad_one + input_norm_grad)[None]
    (
        grad_query,
        grad_key,
        grad_value,
        grad_out,
        grad_router,
        grad_attn_gain,
        grad_query_gain,
        grad_key_gain,
        grad_ffn_gain,
    ) = (
        lax.psum_scatter(query_weight_grad, ("ctx", "fsdp"), scatter_dimension=0, tiled=True),
        lax.psum_scatter(key_weight_grad, ("ctx", "fsdp"), scatter_dimension=0, tiled=True),
        lax.psum_scatter(value_weight_grad, ("ctx", "fsdp"), scatter_dimension=0, tiled=True),
        lax.psum_scatter(out_weight_grad, ("ctx", "fsdp"), scatter_dimension=0, tiled=True),
        lax.psum_scatter(router_grad, ("ctx", "fsdp"), scatter_dimension=0, tiled=True),
        lax.psum_scatter(attn_gain_grad, ("ctx", "fsdp"), scatter_dimension=0, tiled=True),
        lax.psum_scatter(query_gain_grad, ("ctx", "fsdp"), scatter_dimension=0, tiled=True),
        lax.psum_scatter(key_gain_grad, ("ctx", "fsdp"), scatter_dimension=0, tiled=True),
        lax.psum_scatter(ffn_gain_grad, ("ctx", "fsdp"), scatter_dimension=0, tiled=True),
    )
    return (
        out_hidden,
        grad_hidden,
        grad_attn_gain,
        grad_query_gain,
        grad_key_gain,
        grad_ffn_gain,
        grad_query,
        grad_key,
        grad_value,
        grad_out,
        grad_router,
        grad_gate,
        grad_up,
        grad_down,
    )


def solution(mesh):
    in_specs = (
        P("fsdp", "ctx", None),
        P("fsdp", "ctx", None),
        P("fsdp", "ctx", None),
        P(("ctx", "fsdp")),
        P(("ctx", "fsdp")),
        P(("ctx", "fsdp")),
        P(("ctx", "fsdp")),
        P(("ctx", "fsdp"), None),
        P(("ctx", "fsdp"), None),
        P(("ctx", "fsdp"), None),
        P(("ctx", "fsdp"), None),
        P(("ctx", "fsdp"), None),
        P("ctx", "fsdp", None),
        P("ctx", "fsdp", None),
        P("ctx", "fsdp", None),
    )
    out_specs = (
        P("fsdp", "ctx", None),
        P("fsdp", "ctx", None),
        P(("ctx", "fsdp")),
        P(("ctx", "fsdp")),
        P(("ctx", "fsdp")),
        P(("ctx", "fsdp")),
        P(("ctx", "fsdp"), None),
        P(("ctx", "fsdp"), None),
        P(("ctx", "fsdp"), None),
        P(("ctx", "fsdp"), None),
        P(("ctx", "fsdp"), None),
        P("ctx", "fsdp", None),
        P("ctx", "fsdp", None),
        P("ctx", "fsdp", None),
    )
    return jax.shard_map(body, mesh=mesh, in_specs=in_specs, out_specs=out_specs, check_vma=False)
```

profile of v0, /device:TPU:0, one launch (start us, length us, event | category | flops | bytes accessed | tf_op | source)
XLA Modules:
  0.0 3912.5 jit_solution(9676272836625254248)
XLA Ops:
  12.9 42.6 %all-reduce.11 = (bf16[2048]{0:T(1024)(128)(2,1)S(1)}, bf16[2048]{0:T(1024)(128)(2,1)S(1)}, bf16[2048]{0:T(1024)(128)(2,1)S(1)}, bf16[2048]{0:T(1024)(128)(2,1)S(1)}) all-reduce(bf16[2048]{0:T(1024)(128)(2,1)S(1)} %dynamic-update-slice, bf16[2048]{0:T(1024)(128)(2,1)S(1)} %dynamic-update-slice.1, ...), channel_id=1, replica_groups=mesh['ctx'=8,'fsdp'=4] {'ctx','fsdp'}, use_global_device_ids=true, to_apply=%add.2 | all-reduce | flops 8192 | bytes 32768
  58.0 33.3 all-gather.15.cloned.1.call-done
  98.1 72.1 %all-gather.17.cloned.1.call-done = bf16[2048,2048]{1,0:T(8,128)(2,1)} async-done(((bf16[64,2048]{1,0:T(8,128)(2,1)}), bf16[2048,2048]{1,0:T(8,128)(2,1)}) %all-gather.17.cloned.1.call-update) | async-done | bytes 8388624 | tf_op jit(solution)/shard_map/all_gather | solution.py:107
  181.8 67.4 %all-gather.11.cloned.1.call-done = bf16[2048,2048]{1,0:T(8,128)(2,1)} async-done(((bf16[64,2048]{1,0:T(8,128)(2,1)}), bf16[2048,2048]{1,0:T(8,128)(2,1)}) %all-gather.11.cloned.1.call-update) | async-done | bytes 8388624 | tf_op jit(solution)/shard_map/all_gather | solution.py:108
  255.9 10.1 all-gather.23.cloned.1.call-start
  285.0 10.1 all-gather.19.cloned.1.call-done
  303.8 13.5 select_reduce_fusion.1
  317.3 11.7 select_reduce_fusion
  329.1 13.4 all-gather.13.cloned.1.call-done
  342.5 11.4 fusion.95
  353.9 68.8 %all-gather.21.cloned.1.call-done = bf16[2048,2048]{1,0:T(8,128)(2,1)} async-done(((bf16[64,2048]{1,0:T(8,128)(2,1)}), bf16[2048,2048]{1,0:T(8,128)(2,1)}) %all-gather.21.cloned.1.call-update) | async-done | bytes 8388624 | tf_op jit(solution)/shard_map/all_gather | solution.py:109
  429.1 10.8 gather_fusion
  445.2 98.8 %all-gather = bf16[32,64,32]{1,2,0:T(8,128)(2,1)S(1)} all-gather(bf16[1,64,32]{1,2,0:T(8,128)(2,1)S(1)} %bitcast.336), channel_id=1, replica_groups=mesh['ctx'=8,'fsdp'=4] {'ctx','fsdp'}, dimensions={0}, use_global_device_ids=true | all-gather | bytes 135168 | tf_op jit(solution)/shard_map/all_gather | solution.py:110
  550.0 19.9 gather_fusion.2
  569.9 19.4 all-to-all-start.2
  589.4 125.5 %all-gather.23.cloned.1.call-done = bf16[4,2048,1024]{2,1,0:T(8,128)(2,1)} async-done(((bf16[4,512,1024]{2,1,0:T(8,128)(2,1)}), bf16[4,2048,1024]{2,1,0:T(8,128)(2,1)}) %all-gather.23.cloned.1.call-update) | async-done | bytes 16777232 | tf_op jit(solution)/shard_map/all_gather | solution.py:117
  714.9 16.8 fusion.27
  731.7 270.0 %all-gather.25.cloned.1.call-done = bf16[4,2048,1024]{2,1,0:T(8,128)(2,1)} async-done(((bf16[4,512,1024]{2,1,0:T(8,128)(2,1)}), bf16[4,2048,1024]{2,1,0:T(8,128)(2,1)}) %all-gather.25.cloned.1.call-update) | async-done | bytes 16777232 | tf_op jit(solution)/shard_map/all_gather | solution.py:118
  1001.7 16.9 fusion.23
  1018.6 269.7 %all-gather.27.cloned.1.call-done = bf16[4,1024,2048]{2,1,0:T(8,128)(2,1)} async-done(((bf16[4,256,2048]{2,1,0:T(8,128)(2,1)}), bf16[4,1024,2048]{2,1,0:T(8,128)(2,1)}) %all-gather.27.cloned.1.call-update) | async-done | bytes 16777232 | tf_op jit(solution)/shard_map/all_gather | solution.py:119
  1288.3 22.8 fusion.51
  1311.1 17.6 convert_bitcast_fusion
  1342.4 94.0 %all-to-all-done.1 = bf16[8,256,2048]{2,1,0:T(8,128)(2,1)} async-done(((bf16[8,256,2048]{2,1,0:T(8,128)(2,1)}), bf16[8,256,2048]{2,1,0:T(8,128)(2,1)}, u32[]{:S(2)}, u32[]{:S(2)}) %all-to-all-start.1) | async-done | bytes 8388640 | tf_op jit(solution)/shard_map/all_to_all | solution.py:207
  1436.4 17.2 gather_fusion.1
  1463.6 16.6 bitcast_convert_fusion
  1480.3 15.9 bitcast_convert_fusion.2
  1496.3 16.3 bitcast_convert_fusion.1
  1512.7 17.1 fusion.21
  1529.8 18.2 fusion.48
  1556.5 101.3 %all_to_all.20 = bf16[8,256,2048]{2,1,0:T(8,128)(2,1)} all-to-all(bf16[8,256,2048]{2,1,0:T(8,128)(2,1)} %bitcast.324), channel_id=1, replica_groups=mesh['ctx'=8,'fsdp'=4] {'ctx'}, dimensions={0} | all-to-all | bytes 16777216 | tf_op jit(solution)/shard_map/all_to_all | solution.py:254
  1657.8 17.2 gather_fusion.3
  1702.1 10.7 fusion.86
  1715.4 525.3 %while.25 = (s32[]{:T(128)}, bf16[192,2048]{1,0:T(8,128)(2,1)}, bf16[192,2048]{1,0:T(8,128)(2,1)}, f32[192,2048]{1,0:T(8,128)}, f32[192,2048]{1,0:T(8,128)}, /*i...) while((s32[]{:T(128)}, bf16[192,2048]{1,0:T(8,128)(2,1)}, ...), condition=%wide.region_21.22_spmd.clone, body=%wide.region_20.21_spmd.clone.sunk | while | flops 763277184 | bytes 57167340 | solution.py:327
  1734.6 38.0 collective-permute-done
  1801.6 36.6 collective-permute-done
  1867.3 36.6 collective-permute-done
  1932.9 36.5 collective-permute-done
  1998.5 36.6 collective-permute-done
  2064.1 36.6 collective-permute-done
  2129.8 36.6 collective-permute-done
  2195.4 36.6 collective-permute-done
  2270.4 9.7 fusion.106
  2300.5 40.0 %all-reduce.10 = (f32[2048]{0:T(1024)S(1)}, f32[2048]{0:T(1024)S(1)}, f32[2048]{0:T(1024)S(1)}, f32[2048]{0:T(1024)S(1)}) all-reduce(f32[2048]{0:T(1024)S(1)} %get-tuple-element.460, f32[2048]{0:T(1024)S(1)} %get-tuple-element.458, f32[2048]{0:T(1024)S(1)} %get-tuple-element.456, ...), channel_id=2, replica_groups=mesh['ctx'=8,'fsdp'=4] {'ctx','fsdp'}, use_global_device_ids=true, to_apply=%region_26.27.clone | all-reduce | flops 8192 | bytes 65536
  2360.6 82.7 %reduce-scatter.21.cloned.1.call-done = bf16[4,512,1024]{2,1,0:T(8,128)(2,1)} async-done(((bf16[4,2048,1024]{2,1,0:T(8,128)(2,1)}), bf16[4,512,1024]{2,1,0:T(8,128)(2,1)}) %reduce-scatter.21.cloned.1.call-update) | async-done | bytes 4194320 | tf_op jit(solution)/shard_map/reduce_scatter | solution.py:268
  2450.0 361.0 %reduce-scatter.17.cloned.1.call-done = f32[64,2048]{1,0:T(8,128)} async-done(((f32[2048,2048]{1,0:T(8,128)}), f32[64,2048]{1,0:T(8,128)}) %reduce-scatter.17.cloned.1.call-update) | async-done | bytes 524304 | tf_op jit(solution)/shard_map/reduce_scatter | solution.py:370
  2811.0 364.9 %reduce-scatter.13.cloned.1.call-done = f32[64,2048]{1,0:T(8,128)} async-done(((f32[2048,2048]{1,0:T(8,128)}), f32[64,2048]{1,0:T(8,128)}) %reduce-scatter.13.cloned.1.call-update) | async-done | bytes 524304 | tf_op jit(solution)/shard_map/reduce_scatter | solution.py:368
  3175.9 364.9 %reduce-scatter.11.cloned.1.call-done = f32[64,2048]{1,0:T(8,128)} async-done(((f32[2048,2048]{1,0:T(8,128)}), f32[64,2048]{1,0:T(8,128)}) %reduce-scatter.11.cloned.1.call-update) | async-done | bytes 524304 | tf_op jit(solution)/shard_map/reduce_scatter | solution.py:367
  3540.8 364.9 %reduce-scatter.15.cloned.1.call-done = f32[64,2048]{1,0:T(8,128)} async-done(((f32[2048,2048]{1,0:T(8,128)}), f32[64,2048]{1,0:T(8,128)}) %reduce-scatter.15.cloned.1.call-update) | async-done | bytes 524304 | tf_op jit(solution)/shard_map/reduce_scatter | solution.py:369
  (435 shorter events, 446.8 us)
Async XLA Ops:
  7.2 84.1 %all-gather.15.cloned.1.call-start = ((), (), s32[]{:S(2)}) async-start(), calls=%async_computation.14 | async-start | bytes 8650752 | tf_op jit(solution)/shard_map/all_gather | solution.py:106
  7.9 162.3 %all-gather.17.cloned.1.call-start = ((), (), s32[]{:S(2)}) async-start(), calls=%async_computation.15 | async-start | bytes 8650752 | tf_op jit(solution)/shard_map/all_gather | solution.py:107
  8.7 240.6 %all-gather.11.cloned.1.call-start = ((), (), s32[]{:S(2)}) async-start(), calls=%async_computation.12 | async-start | bytes 8650752 | tf_op jit(solution)/shard_map/all_gather | solution.py:108
  9.4 285.7 %all-gather.19.cloned.1.call-start = ((), (), s32[]{:S(2)}) async-start(), calls=%async_computation.16 | async-start | bytes 7077888 | tf_op jit(solution)/shard_map/all_gather | solution.py:165
  181.7 160.7 %all-gather.13.cloned.1.call-start = ((), (), s32[]{:S(2)}) async-start(), calls=%async_computation.13 | async-start | bytes 7077888 | tf_op jit(solution)/shard_map/all_gather | solution.py:167
  255.4 167.3 %all-gather.21.cloned.1.call-start = ((), (), s32[]{:S(2)}) async-start(), calls=%async_computation.17 | async-start | bytes 8650752 | tf_op jit(solution)/shard_map/all_gather | solution.py:109
  255.9 459.0 %all-gather.23.cloned.1.call-start = ((), (), s32[]{:S(2)}) async-start(), calls=%async_computation.18 | async-start | bytes 20971520 | tf_op jit(solution)/shard_map/all_gather | solution.py:117
  266.1 735.6 %all-gather.25.cloned.1.call-start = ((), (), s32[]{:S(2)}) async-start(), calls=%async_computation.19 | async-start | bytes 20971520 | tf_op jit(solution)/shard_map/all_gather | solution.py:118
  266.9 1021.4 %all-gather.27.cloned.1.call-start = ((), (), s32[]{:S(2)}) async-start(), calls=%async_computation.20 | async-start | bytes 20971520 | tf_op jit(solution)/shard_map/all_gather | solution.py:119
  440.0 130.0 %all-to-all-start = ((bf16[8,256,2048]{2,1,0:T(8,128)(2,1)}), bf16[8,256,2048]{2,1,0:T(8,128)(2,1)}, u32[]{:S(2)}, u32[]{:S(2)}) async-start(bf16[8,256,2048]{2,1,0:T(8,128)(2,1)} %bitcast.321), calls=%async_computation | async-start | bytes 16777216 | tf_op jit(solution)/shard_map/all_to_all | solution.py:197
  569.9 718.3 %all-to-all-start.2 = ((bf16[8,256,2048]{2,1,0:T(8,128)(2,1)}), bf16[8,256,2048]{2,1,0:T(8,128)(2,1)}, u32[]{:S(2)}, u32[]{:S(2)}) async-start(bf16[8,256,2048]{2,1,0:T(8,128)(2,1)} %bitcast.322), calls=%async_computation.2 | async-start | bytes 16777216 | tf_op jit(solution)/shard_map/all_to_all | solution.py:228
  1337.2 99.2 %all-to-all-start.1 = ((bf16[8,256,2048]{2,1,0:T(8,128)(2,1)}), bf16[8,256,2048]{2,1,0:T(8,128)(2,1)}, u32[]{:S(2)}, u32[]{:S(2)}) async-start(bf16[8,256,2048]{2,1,0:T(8,128)(2,1)} %bitcast.323), calls=%async_computation.1 | async-start | bytes 16777216 | tf_op jit(solution)/shard_map/all_to_all | solution.py:207
  1342.3 1003.6 %reduce-scatter.25.cloned.1.call-start = ((), (), s32[]{:S(2)}) async-start(), calls=%async_computation.28 | async-start | bytes 1081344
  1463.6 883.8 %reduce-scatter.23.cloned.1.call-start = ((), (), s32[]{:S(2)}) async-start(), calls=%async_computation.27 | async-start | bytes 20971520 | tf_op jit(solution)/shard_map/reduce_scatter | solution.py:271
  1480.3 873.7 %reduce-scatter.19.cloned.1.call-start = ((), (), s32[]{:S(2)}) async-start(), calls=%async_computation.25 | async-start | bytes 20971520 | tf_op jit(solution)/shard_map/reduce_scatter | solution.py:265
  1496.3 947.1 %reduce-scatter.21.cloned.1.call-start = ((), (), s32[]{:S(2)}) async-start(), calls=%async_computation.26 | async-start | bytes 20971520 | tf_op jit(solution)/shard_map/reduce_scatter | solution.py:268
  1512.7 1298.4 %reduce-scatter.17.cloned.1.call-start = ((), (), s32[]{:S(2)}) async-start(), calls=%async_computation.24 | async-start | bytes 17301504 | tf_op jit(solution)/shard_map/reduce_scatter | solution.py:370
  1694.4 1481.5 %reduce-scatter.13.cloned.1.call-start = ((), (), s32[]{:S(2)}) async-start(), calls=%async_computation.22 | async-start | bytes 17301504 | tf_op jit(solution)/shard_map/reduce_scatter | solution.py:368
  1726.3 54.8 %collective-permute-start.2 = (f32[192,2048]{1,0:T(8,128)}, f32[192,2048]{1,0:T(8,128)}, u32[]{:S(2)}, u32[]{:S(2)}) collective-permute-start(f32[192,2048]{1,0:T(8,128)} %bitcast_add_fusion.6), channel_id=1, source_target_pairs={{0,4},{4,8},{8,12},{12,16},{16,20},{20,24},{24,28},{28,0},{1,5},{5... | collective-permute-start | bytes 4718600 | tf_op jit(solution)/shard_map/while/body/eval_jaxpr/ppermute | solution.py:15
  1730.9 50.2 %collective-permute-start.3 = (f32[192,2048]{1,0:T(8,128)}, f32[192,2048]{1,0:T(8,128)}, u32[]{:S(2)}, u32[]{:S(2)}) collective-permute-start(f32[192,2048]{1,0:T(8,128)} %bitcast_add_fusion.7), channel_id=1, source_target_pairs={{0,4},{4,8},{8,12},{12,16},{16,20},{20,24},{24,28},{28,0},{1,5},{5... | collective-permute-start | bytes 4718600 | tf_op jit(solution)/shard_map/while/body/eval_jaxpr/ppermute | solution.py:15
  1730.9 50.2 %collective-permute-start.1 = (bf16[192,2048]{1,0:T(8,128)(2,1)}, bf16[192,2048]{1,0:T(8,128)(2,1)}, u32[]{:S(2)}, u32[]{:S(2)}) collective-permute-start(bf16[192,2048]{1,0:T(8,128)(2,1)} %copy.331), channel_id=1, source_target_pairs={{0,4},{4,8},{8,12},{12,16},{16,20},{20,24},{24,28},{28,0},{1,5},{5... | collective-permute-start | bytes 2359304 | tf_op jit(solution)/shard_map/while/body/eval_jaxpr/ppermute | solution.py:15
  1791.9 54.8 %collective-permute-start.2 = (f32[192,2048]{1,0:T(8,128)}, f32[192,2048]{1,0:T(8,128)}, u32[]{:S(2)}, u32[]{:S(2)}) collective-permute-start(f32[192,2048]{1,0:T(8,128)} %bitcast_add_fusion.6), channel_id=1, source_target_pairs={{0,4},{4,8},{8,12},{12,16},{16,20},{20,24},{24,28},{28,0},{1,5},{5... | collective-permute-start | bytes 4718600 | tf_op jit(solution)/shard_map/while/body/eval_jaxpr/ppermute | solution.py:15
  1796.4 50.3 %collective-permute-start.3 = (f32[192,2048]{1,0:T(8,128)}, f32[192,2048]{1,0:T(8,128)}, u32[]{:S(2)}, u32[]{:S(2)}) collective-permute-start(f32[192,2048]{1,0:T(8,128)} %bitcast_add_fusion.7), channel_id=1, source_target_pairs={{0,4},{4,8},{8,12},{12,16},{16,20},{20,24},{24,28},{28,0},{1,5},{5... | collective-permute-start | bytes 4718600 | tf_op jit(solution)/shard_map/while/body/eval_jaxpr/ppermute | solution.py:15
  1796.4 41.9 %collective-permute-start = (bf16[192,2048]{1,0:T(8,128)(2,1)S(1)}, bf16[192,2048]{1,0:T(8,128)(2,1)}, u32[]{:S(2)}, u32[]{:S(2)}) collective-permute-start(bf16[192,2048]{1,0:T(8,128)(2,1)S(1)} %copy.330), channel_id=1, source_target_pairs={{0,4},{4,8},{8,12},{12,16},{16,20},{20,24},{24,28},{28,0},{1,5},{5... | collective-permute-start | bytes 2359304 | tf_op jit(solution)/shard_map/while/body/eval_jaxpr/ppermute | solution.py:15
  1796.4 50.3 %collective-permute-start.1 = (bf16[192,2048]{1,0:T(8,128)(2,1)}, bf16[192,2048]{1,0:T(8,128)(2,1)}, u32[]{:S(2)}, u32[]{:S(2)}) collective-permute-start(bf16[192,2048]{1,0:T(8,128)(2,1)} %copy.331), channel_id=1, source_target_pairs={{0,4},{4,8},{8,12},{12,16},{16,20},{20,24},{24,28},{28,0},{1,5},{5... | collective-permute-start | bytes 2359304 | tf_op jit(solution)/shard_map/while/body/eval_jaxpr/ppermute | solution.py:15
  1857.5 54.8 %collective-permute-start.2 = (f32[192,2048]{1,0:T(8,128)}, f32[192,2048]{1,0:T(8,128)}, u32[]{:S(2)}, u32[]{:S(2)}) collective-permute-start(f32[192,2048]{1,0:T(8,128)} %bitcast_add_fusion.6), channel_id=1, source_target_pairs={{0,4},{4,8},{8,12},{12,16},{16,20},{20,24},{24,28},{28,0},{1,5},{5... | collective-permute-start | bytes 4718600 | tf_op jit(solution)/shard_map/while/body/eval_jaxpr/ppermute | solution.py:15
  1862.0 50.3 %collective-permute-start.3 = (f32[192,2048]{1,0:T(8,128)}, f32[192,2048]{1,0:T(8,128)}, u32[]{:S(2)}, u32[]{:S(2)}) collective-permute-start(f32[192,2048]{1,0:T(8,128)} %bitcast_add_fusion.7), channel_id=1, source_target_pairs={{0,4},{4,8},{8,12},{12,16},{16,20},{20,24},{24,28},{28,0},{1,5},{5... | collective-permute-start | bytes 4718600 | tf_op jit(solution)/shard_map/while/body/eval_jaxpr/ppermute | solution.py:15
  1862.0 41.9 %collective-permute-start = (bf16[192,2048]{1,0:T(8,128)(2,1)S(1)}, bf16[192,2048]{1,0:T(8,128)(2,1)}, u32[]{:S(2)}, u32[]{:S(2)}) collective-permute-start(bf16[192,2048]{1,0:T(8,128)(2,1)S(1)} %copy.330), channel_id=1, source_target_pairs={{0,4},{4,8},{8,12},{12,16},{16,20},{20,24},{24,28},{28,0},{1,5},{5... | collective-permute-start | bytes 2359304 | tf_op jit(solution)/shard_map/while/body/eval_jaxpr/ppermute | solution.py:15
  1862.0 50.3 %collective-permute-start.1 = (bf16[192,2048]{1,0:T(8,128)(2,1)}, bf16[192,2048]{1,0:T(8,128)(2,1)}, u32[]{:S(2)}, u32[]{:S(2)}) collective-permute-start(bf16[192,2048]{1,0:T(8,128)(2,1)} %copy.331), channel_id=1, source_target_pairs={{0,4},{4,8},{8,12},{12,16},{16,20},{20,24},{24,28},{28,0},{1,5},{5... | collective-permute-start | bytes 2359304 | tf_op jit(solution)/shard_map/while/body/eval_jaxpr/ppermute | solution.py:15
  1923.1 54.8 %collective-permute-start.2 = (f32[192,2048]{1,0:T(8,128)}, f32[192,2048]{1,0:T(8,128)}, u32[]{:S(2)}, u32[]{:S(2)}) collective-permute-start(f32[192,2048]{1,0:T(8,128)} %bitcast_add_fusion.6), channel_id=1, source_target_pairs={{0,4},{4,8},{8,12},{12,16},{16,20},{20,24},{24,28},{28,0},{1,5},{5... | collective-permute-start | bytes 4718600 | tf_op jit(solution)/shard_map/while/body/eval_jaxpr/ppermute | solution.py:15
  1927.6 50.3 %collective-permute-start.3 = (f32[192,2048]{1,0:T(8,128)}, f32[192,2048]{1,0:T(8,128)}, u32[]{:S(2)}, u32[]{:S(2)}) collective-permute-start(f32[192,2048]{1,0:T(8,128)} %bitcast_add_fusion.7), channel_id=1, source_target_pairs={{0,4},{4,8},{8,12},{12,16},{16,20},{20,24},{24,28},{28,0},{1,5},{5... | collective-permute-start | bytes 4718600 | tf_op jit(solution)/shard_map/while/body/eval_jaxpr/ppermute | solution.py:15
  1927.6 50.3 %collective-permute-start.1 = (bf16[192,2048]{1,0:T(8,128)(2,1)}, bf16[192,2048]{1,0:T(8,128)(2,1)}, u32[]{:S(2)}, u32[]{:S(2)}) collective-permute-start(bf16[192,2048]{1,0:T(8,128)(2,1)} %copy.331), channel_id=1, source_target_pairs={{0,4},{4,8},{8,12},{12,16},{16,20},{20,24},{24,28},{28,0},{1,5},{5... | collective-permute-start | bytes 2359304 | tf_op jit(solution)/shard_map/while/body/eval_jaxpr/ppermute | solution.py:15
  1988.8 54.8 %collective-permute-start.2 = (f32[192,2048]{1,0:T(8,128)}, f32[192,2048]{1,0:T(8,128)}, u32[]{:S(2)}, u32[]{:S(2)}) collective-permute-start(f32[192,2048]{1,0:T(8,128)} %bitcast_add_fusion.6), channel_id=1, source_target_pairs={{0,4},{4,8},{8,12},{12,16},{16,20},{20,24},{24,28},{28,0},{1,5},{5... | collective-permute-start | bytes 4718600 | tf_op jit(solution)/shard_map/while/body/eval_jaxpr/ppermute | solution.py:15
  1993.3 50.3 %collective-permute-start.3 = (f32[192,2048]{1,0:T(8,128)}, f32[192,2048]{1,0:T(8,128)}, u32[]{:S(2)}, u32[]{:S(2)}) collective-permute-start(f32[192,2048]{1,0:T(8,128)} %bitcast_add_fusion.7), channel_id=1, source_target_pairs={{0,4},{4,8},{8,12},{12,16},{16,20},{20,24},{24,28},{28,0},{1,5},{5... | collective-permute-start | bytes 4718600 | tf_op jit(solution)/shard_map/while/body/eval_jaxpr/ppermute | solution.py:15
  1993.3 41.9 %collective-permute-start = (bf16[192,2048]{1,0:T(8,128)(2,1)S(1)}, bf16[192,2048]{1,0:T(8,128)(2,1)}, u32[]{:S(2)}, u32[]{:S(2)}) collective-permute-start(bf16[192,2048]{1,0:T(8,128)(2,1)S(1)} %copy.330), channel_id=1, source_target_pairs={{0,4},{4,8},{8,12},{12,16},{16,20},{20,24},{24,28},{28,0},{1,5},{5... | collective-permute-start | bytes 2359304 | tf_op jit(solution)/shard_map/while/body/eval_jaxpr/ppermute | solution.py:15
  1993.3 50.3 %collective-permute-start.1 = (bf16[192,2048]{1,0:T(8,128)(2,1)}, bf16[192,2048]{1,0:T(8,128)(2,1)}, u32[]{:S(2)}, u32[]{:S(2)}) collective-permute-start(bf16[192,2048]{1,0:T(8,128)(2,1)} %copy.331), channel_id=1, source_target_pairs={{0,4},{4,8},{8,12},{12,16},{16,20},{20,24},{24,28},{28,0},{1,5},{5... | collective-permute-start | bytes 2359304 | tf_op jit(solution)/shard_map/while/body/eval_jaxpr/ppermute | solution.py:15
  2054.4 54.8 %collective-permute-start.2 = (f32[192,2048]{1,0:T(8,128)}, f32[192,2048]{1,0:T(8,128)}, u32[]{:S(2)}, u32[]{:S(2)}) collective-permute-start(f32[192,2048]{1,0:T(8,128)} %bitcast_add_fusion.6), channel_id=1, source_target_pairs={{0,4},{4,8},{8,12},{12,16},{16,20},{20,24},{24,28},{28,0},{1,5},{5... | collective-permute-start | bytes 4718600 | tf_op jit(solution)/shard_map/while/body/eval_jaxpr/ppermute | solution.py:15
  2058.9 50.3 %collective-permute-start.3 = (f32[192,2048]{1,0:T(8,128)}, f32[192,2048]{1,0:T(8,128)}, u32[]{:S(2)}, u32[]{:S(2)}) collective-permute-start(f32[192,2048]{1,0:T(8,128)} %bitcast_add_fusion.7), channel_id=1, source_target_pairs={{0,4},{4,8},{8,12},{12,16},{16,20},{20,24},{24,28},{28,0},{1,5},{5... | collective-permute-start | bytes 4718600 | tf_op jit(solution)/shard_map/while/body/eval_jaxpr/ppermute | solution.py:15
  2058.9 41.9 %collective-permute-start = (bf16[192,2048]{1,0:T(8,128)(2,1)S(1)}, bf16[192,2048]{1,0:T(8,128)(2,1)}, u32[]{:S(2)}, u32[]{:S(2)}) collective-permute-start(bf16[192,2048]{1,0:T(8,128)(2,1)S(1)} %copy.330), channel_id=1, source_target_pairs={{0,4},{4,8},{8,12},{12,16},{16,20},{20,24},{24,28},{28,0},{1,5},{5... | collective-permute-start | bytes 2359304 | tf_op jit(solution)/shard_map/while/body/eval_jaxpr/ppermute | solution.py:15
  2058.9 50.3 %collective-permute-start.1 = (bf16[192,2048]{1,0:T(8,128)(2,1)}, bf16[192,2048]{1,0:T(8,128)(2,1)}, u32[]{:S(2)}, u32[]{:S(2)}) collective-permute-start(bf16[192,2048]{1,0:T(8,128)(2,1)} %copy.331), channel_id=1, source_target_pairs={{0,4},{4,8},{8,12},{12,16},{16,20},{20,24},{24,28},{28,0},{1,5},{5... | collective-permute-start | bytes 2359304 | tf_op jit(solution)/shard_map/while/body/eval_jaxpr/ppermute | solution.py:15
  2120.0 54.8 %collective-permute-start.2 = (f32[192,2048]{1,0:T(8,128)}, f32[192,2048]{1,0:T(8,128)}, u32[]{:S(2)}, u32[]{:S(2)}) collective-permute-start(f32[192,2048]{1,0:T(8,128)} %bitcast_add_fusion.6), channel_id=1, source_target_pairs={{0,4},{4,8},{8,12},{12,16},{16,20},{20,24},{24,28},{28,0},{1,5},{5... | collective-permute-start | bytes 4718600 | tf_op jit(solution)/shard_map/while/body/eval_jaxpr/ppermute | solution.py:15
  2124.5 50.3 %collective-permute-start.3 = (f32[192,2048]{1,0:T(8,128)}, f32[192,2048]{1,0:T(8,128)}, u32[]{:S(2)}, u32[]{:S(2)}) collective-permute-start(f32[192,2048]{1,0:T(8,128)} %bitcast_add_fusion.7), channel_id=1, source_target_pairs={{0,4},{4,8},{8,12},{12,16},{16,20},{20,24},{24,28},{28,0},{1,5},{5... | collective-permute-start | bytes 4718600 | tf_op jit(solution)/shard_map/while/body/eval_jaxpr/ppermute | solution.py:15
  2124.5 50.3 %collective-permute-start.1 = (bf16[192,2048]{1,0:T(8,128)(2,1)}, bf16[192,2048]{1,0:T(8,128)(2,1)}, u32[]{:S(2)}, u32[]{:S(2)}) collective-permute-start(bf16[192,2048]{1,0:T(8,128)(2,1)} %copy.331), channel_id=1, source_target_pairs={{0,4},{4,8},{8,12},{12,16},{16,20},{20,24},{24,28},{28,0},{1,5},{5... | collective-permute-start | bytes 2359304 | tf_op jit(solution)/shard_map/while/body/eval_jaxpr/ppermute | solution.py:15
  2185.6 54.8 %collective-permute-start.2 = (f32[192,2048]{1,0:T(8,128)}, f32[192,2048]{1,0:T(8,128)}, u32[]{:S(2)}, u32[]{:S(2)}) collective-permute-start(f32[192,2048]{1,0:T(8,128)} %bitcast_add_fusion.6), channel_id=1, source_target_pairs={{0,4},{4,8},{8,12},{12,16},{16,20},{20,24},{24,28},{28,0},{1,5},{5... | collective-permute-start | bytes 4718600 | tf_op jit(solution)/shard_map/while/body/eval_jaxpr/ppermute | solution.py:15
  2190.1 50.3 %collective-permute-start.3 = (f32[192,2048]{1,0:T(8,128)}, f32[192,2048]{1,0:T(8,128)}, u32[]{:S(2)}, u32[]{:S(2)}) collective-permute-start(f32[192,2048]{1,0:T(8,128)} %bitcast_add_fusion.7), channel_id=1, source_target_pairs={{0,4},{4,8},{8,12},{12,16},{16,20},{20,24},{24,28},{28,0},{1,5},{5... | collective-permute-start | bytes 4718600 | tf_op jit(solution)/shard_map/while/body/eval_jaxpr/ppermute | solution.py:15
  2190.1 50.3 %collective-permute-start.1 = (bf16[192,2048]{1,0:T(8,128)(2,1)}, bf16[192,2048]{1,0:T(8,128)(2,1)}, u32[]{:S(2)}, u32[]{:S(2)}) collective-permute-start(bf16[192,2048]{1,0:T(8,128)(2,1)} %copy.331), channel_id=1, source_target_pairs={{0,4},{4,8},{8,12},{12,16},{16,20},{20,24},{24,28},{28,0},{1,5},{5... | collective-permute-start | bytes 2359304 | tf_op jit(solution)/shard_map/while/body/eval_jaxpr/ppermute | solution.py:15
  2256.7 1284.1 %reduce-scatter.11.cloned.1.call-start = ((), (), s32[]{:S(2)}) async-start(), calls=%async_computation.21 | async-start | bytes 17301504 | tf_op jit(solution)/shard_map/reduce_scatter | solution.py:367
  2270.2 1635.5 %reduce-scatter.15.cloned.1.call-start = ((), (), s32[]{:S(2)}) async-start(), calls=%async_computation.23 | async-start | bytes 17301504 | tf_op jit(solution)/shard_map/reduce_scatter | solution.py:369
  (68 other events, 1734.6 us)
Sparse Core Ops, SparseCore 0:
  11.0 80.3 all-gather.14
  94.3 75.9 all-gather.16
  173.2 75.9 all-gather.10
  251.0 44.1 all-gather.18
  296.9 45.5 all-gather.12
  345.3 77.3 all-gather.20
  424.2 290.6 all-gather.22
  716.5 285.1 all-gather.24
  1003.3 284.9 all-gather.26
  1463.7 132.5 reduce-scatter.24
  1598.8 276.7 reduce-scatter.22
  1877.7 281.0 reduce-scatter.18
  2161.3 282.0 reduce-scatter.20
  2446.1 364.9 reduce-scatter.16
  2813.7 362.1 reduce-scatter.12
  3178.6 362.1 reduce-scatter.10
  3543.5 362.1 reduce-scatter.14
where the time goes:
time: 3920 us; the launch traced here: 3910 us
  waiting for transfers between devices  2930 us (75%)
  matrix products  348 us (9%)
  blocking collectives  283 us (7%)
  local copies, waits for them, and re-layouts  155 us (4%)
  other arithmetic  124 us (3%)
  starting transfers between devices  58 us (1%)
    reduce_scatter x1, waiting for transfers between devices, body(): lax.psum_scatter(value_weight_grad, ('ctx', 'fsdp'), scatter_dimension=0,...  365 us
    reduce_scatter x1, waiting for transfers between devices, body(): lax.psum_scatter(key_weight_grad, ('ctx', 'fsdp'), scatter_dimension=0, t...  365 us
    reduce_scatter x1, waiting for transfers between devices, body(): lax.psum_scatter(query_weight_grad, ('ctx', 'fsdp'), scatter_dimension=0,...  365 us
    ppermute x32, waiting for transfers between devices, from_behind(): lax.ppermute(x, axis, [(i, (i + by) % length) for i in range(length)])  362 us
    reduce_scatter x1, waiting for transfers between devices, body(): lax.psum_scatter(out_weight_grad, ('ctx', 'fsdp'), scatter_dimension=0, t...  361 us
    all_gather x1, waiting for transfers between devices, body(): lax.all_gather(w_up, 'fsdp', axis=1, tiled=True)  270 us
    all_gather x1, waiting for transfers between devices, body(): lax.all_gather(w_down, 'fsdp', axis=1, tiled=True)  270 us
    all_gather x1, waiting for transfers between devices, body(): lax.all_gather(w_gate, 'fsdp', axis=1, tiled=True)  126 us
  transfers between devices with their start and end apart: 52, of which 31 were waited for; matrix products, arithmetic and copies ran while one was open for 14% of the time, Pallas kernels for 0%

commit v1 on v0

v1 whole, which is shorter than its diff:
```python
import jax
import jax.numpy as jnp
from jax import lax
from jax.sharding import PartitionSpec as P

HEADS = 16


epsilon = 1e-05
neg_large = -1e30
low = jnp.bfloat16
exact = jnp.float32


def swap(x, axis, bit):
    length = lax.axis_size(axis)
    return lax.ppermute(x, axis, [(i, i ^ bit) for i in range(length)])


def bits_of(axis):
    length = lax.axis_size(axis)
    return [1 << i for i in range(length.bit_length() - 1)]


def doubled(x, axis, bits):
    index = lax.axis_index(axis)
    for bit in bits:
        other = swap(x, axis, bit)
        high = (index & bit) != 0
        x = jnp.stack([jnp.where(high, other, x), jnp.where(high, x, other)])
    count = len(bits)
    order = sorted(range(count), key=lambda i: -bits[count - 1 - i])
    x = x.transpose(order + list(range(count, x.ndim)))
    return x.reshape((1 << count,) + x.shape[count:])


def gather_ctx(x):
    bits = bits_of("ctx")
    half = x.shape[-1] // 2
    far = bits[1:]
    one = doubled(x[..., :half], "ctx", far + bits[:1])
    two = doubled(x[..., half:], "ctx", far[::-1] + bits[:1])
    return jnp.concatenate([one, two], axis=-1)


def halved(x, axis, bits):
    index = lax.axis_index(axis)
    count = len(bits)
    x = x.reshape((2,) * count + x.shape[1:])
    left = sorted(bits, reverse=True)
    for bit in bits:
        at = left.index(bit)
        left.remove(bit)
        zero = lax.index_in_dim(x, 0, at, keepdims=False)
        one = lax.index_in_dim(x, 1, at, keepdims=False)
        high = (index & bit) != 0
        got = swap(jnp.where(high, zero, one).astype(low), axis, bit)
        x = jnp.where(high, one, zero).astype(exact) + got.astype(exact)
    return x


def scatter_ctx(x):
    bits = bits_of("ctx")
    half = x.shape[-1] // 2
    far = bits[1:]
    one = halved(x[..., :half], "ctx", bits[:1] + far)
    two = halved(x[..., half:], "ctx", bits[:1] + far[::-1])
    return jnp.concatenate([one, two], axis=-1)


def near_first(x):
    blocks = {0: x}
    for bit in bits_of("fsdp")[::-1]:
        for key in sorted(blocks):
            blocks[key | bit] = swap(blocks[key], "fsdp", bit)
    return [blocks[key] for key in sorted(blocks)]


def back_home(parts):
    parts = [part.astype(exact) for part in parts]
    for bit in bits_of("fsdp"):
        for key in range(len(parts)):
            if key & bit and not key & (bit - 1):
                got = swap(parts[key].astype(low), "fsdp", bit)
                parts[key ^ bit] = parts[key ^ bit] + got.astype(exact)
    return parts[0]


def exchange(x, axis):
    return lax.all_to_all(x, axis, split_axis=0, concat_axis=0, tiled=True)


def rms_apply(vector, gain):
    scale = lax.rsqrt(jnp.mean(vector * vector, axis=-1, keepdims=True) + epsilon)
    normed = vector * scale
    return (normed * gain, normed, scale)


def rms_back(grad, normed, scale, gain):
    dnormed = grad * gain
    gain_grad = jnp.sum(grad * normed, axis=0)
    inner = jnp.mean(dnormed * normed, axis=-1, keepdims=True)
    return (scale * (dnormed - normed * inner), gain_grad)


def rotation(positions, head_size):
    half = head_size // 2
    freq = 10000.0 ** (-jnp.arange(half, dtype=jnp.float32) * (2.0 / head_size))
    angle = positions.astype(jnp.float32)[:, None] * freq[None, :]
    return (jnp.cos(angle)[:, None, :], jnp.sin(angle)[:, None, :])


def rotate(vector, cosine, sine):
    half = vector.shape[-1] // 2
    first = vector[..., :half]
    second = vector[..., half:]
    return jnp.concatenate(
        [first * cosine - second * sine, second * cosine + first * sine], axis=-1
    )


def dot(left, right):
    return jnp.dot(left, right, preferred_element_type=exact)


def contract_rows(left, right):
    return lax.dot_general(
        left, right, (((0,), (0,)), ((), ())), preferred_element_type=exact
    )


def contract_cols(left, right):
    return lax.dot_general(
        left, right, (((1,), (1,)), ((), ())), preferred_element_type=exact
    )


def ordered(x, ctx_count):
    x = x.reshape((ctx_count, 2, -1) + x.shape[1:])
    x = jnp.concatenate([x[:, 0], x[::-1, 1]], axis=0)
    return x.reshape((-1,) + x.shape[2:])


def placed(x, ctx_count):
    x = x.reshape((2 * ctx_count, -1) + x.shape[1:])
    x = jnp.stack([x[:ctx_count], x[ctx_count:][::-1]], axis=1)
    return x.reshape((-1,) + x.shape[3:])


def body(
    hidden_in,
    cotangent,
    routes,
    attn_gain,
    query_gain,
    key_gain,
    ffn_gain,
    w_query,
    w_key,
    w_value,
    w_out,
    w_router,
    w_gate,
    w_up,
    w_down,
):
    tokens = hidden_in.shape[1]
    width = hidden_in.shape[2]
    head_size = width // HEADS
    ctx_count = lax.axis_size("ctx")
    z_count = lax.axis_size("fsdp")
    both = ("ctx", "fsdp")
    top = routes.shape[2]
    exp_local = w_gate.shape[0]
    split = z_count // exp_local
    hidden = w_gate.shape[2]
    part = hidden // split
    experts = exp_local * ctx_count
    capacity = tokens * top * 4 // (3 * experts)
    heads = HEADS // ctx_count
    cols = heads * head_size
    length = tokens * ctx_count
    scale = head_size ** (-0.5)
    c_index = lax.axis_index("ctx")
    z_index = lax.axis_index("fsdp")
    rows_w = w_query.shape[0]

    qkv = jnp.stack([w_query, w_key, w_value], axis=1).reshape(rows_w, 3, ctx_count, cols)
    qkv = exchange(qkv.transpose(2, 0, 1, 3), "ctx")
    qkv = doubled(qkv, "fsdp", bits_of("fsdp")[::-1])
    qkv = qkv.transpose(1, 0, 2, 3, 4).reshape(width, 3 * cols)
    gains = jnp.stack([attn_gain, query_gain, key_gain, ffn_gain])
    small = jnp.concatenate([gains.reshape(-1), w_router.reshape(-1)])
    small = exchange(
        jnp.broadcast_to(small[None], (ctx_count * z_count, small.shape[0])), both
    )
    gains = small[:, : 4 * rows_w].reshape(-1, 4, rows_w).transpose(1, 0, 2).reshape(4, width)
    router_full = small[:, 4 * rows_w :].reshape(width, experts)
    gains = gains.astype(exact)
    attn_scale, query_scale, key_scale, ffn_scale = gains[0], gains[1], gains[2], gains[3]
    query_scale = lax.dynamic_slice_in_dim(query_scale, c_index * cols, cols)
    key_scale = lax.dynamic_slice_in_dim(key_scale, c_index * cols, cols)

    x_all = gather_ctx(hidden_in[0]).reshape(length, width)
    attn_all = rms_apply(x_all.astype(exact), attn_scale)[0].astype(low)

    routes_all = lax.all_gather(routes[0], both, axis=0)
    multi_all = jnp.sum(
        (routes_all[..., None] == jnp.arange(experts, dtype=jnp.int32)).astype(exact), axis=2
    ).reshape(ctx_count, z_count, tokens, experts)
    own_expert = c_index * exp_local + z_index // split
    lower = (
        jnp.arange(tokens)[:, None] >= jnp.arange(tokens)[None, :]
    ).astype(low)

    def slots(mask):
        rank = jnp.einsum("ts,bs->bt", lower, mask.astype(low), preferred_element_type=exact)
        rank = rank.astype(jnp.int32) - 1
        hit = rank[:, None, :] == jnp.arange(capacity, dtype=jnp.int32)[None, :, None]
        return (hit & (mask[:, None, :] > 0)).astype(low)

    multi_own = lax.dynamic_index_in_dim(multi_all, c_index, 0, False)
    sends = []
    metas = []
    for step in range(z_count):
        source = z_index ^ step
        multi = lax.dynamic_index_in_dim(multi_own, source, 0, False)
        plane = multi.reshape(tokens, ctx_count, exp_local)
        plane = lax.dynamic_index_in_dim(plane, z_index // split, 2, False)
        sends.append(slots(plane.T))
        there = lax.dynamic_index_in_dim(multi_all, source, 1, False)
        mine = lax.dynamic_index_in_dim(there, own_expert, 2, False)
        metas.append(
            jnp.einsum(
                "crt,cte->cre", slots(mine), there.astype(low), preferred_element_type=exact
            )
        )
    meta = jnp.stack(metas).reshape(-1, experts)

    def pick(hot, block):
        rows = jnp.einsum("crt,td->crd", hot, block, preferred_element_type=exact)
        return rows.astype(low)

    cot_near = near_first(cotangent[0])
    cot_sent = [pick(hot, block) for hot, block in zip(sends, cot_near)]
    cot_rows = jnp.stack([exchange(rows, "ctx") for rows in cot_sent]).reshape(-1, width)

    def whole_in(weight):
        rows = weight.shape[1]
        weight = weight.reshape(exp_local, rows, z_count, split, part // z_count)
        weight = weight.transpose(0, 3, 1, 2, 4).reshape(z_count, rows, part)
        return exchange(weight, "fsdp").reshape(z_count * rows, part)

    gate_full = whole_in(w_gate)
    up_full = whole_in(w_up)
    rows_d = w_down.shape[1]
    down_full = exchange(
        w_down.reshape(z_count, rows_d // split, width), "fsdp"
    ).reshape(part, width)

    projected = dot(attn_all, qkv)
    queries, keys, values = (
        projected[:, :cols],
        projected[:, cols : 2 * cols],
        projected[:, 2 * cols :],
    )

    def total_over_ctx(one, two):
        both_sums = jnp.stack([one, two])
        return jnp.sum(lax.all_gather(both_sums, "ctx", axis=0), axis=0)

    squares = total_over_ctx(jnp.sum(queries * queries, -1), jnp.sum(keys * keys, -1))
    rms_two = lax.rsqrt(squares / width + epsilon)
    query_rms, key_rms = rms_two[0][:, None], rms_two[1][:, None]
    query_normed, key_normed = queries * query_rms, keys * key_rms
    half = tokens // 2
    row = jnp.arange(length, dtype=jnp.int32)
    device, local = row // tokens, row % tokens
    positions = jnp.where(
        local < half, device * half + local, (2 * ctx_count - 1 - device) * half + local - half
    )
    cosine, sine = rotation(positions, head_size)

    def by_head(x):
        return x.reshape(length, heads, head_size)

    query_rot = ordered(rotate(by_head(query_normed * query_scale), cosine, sine).astype(low), ctx_count)
    key_rot = ordered(rotate(by_head(key_normed * key_scale), cosine, sine).astype(low), ctx_count)
    value_low = ordered(by_head(values.astype(low)), ctx_count)
    allowed = (row[None, :] <= row[:, None])[None]
    scores = (
        jnp.einsum("qhd,khd->hqk", query_rot, key_rot, preferred_element_type=exact) * scale
    )
    scores = jnp.where(allowed, scores, neg_large)
    log_total = jax.nn.logsumexp(scores, axis=-1, keepdims=True)
    probs = jnp.exp(scores - log_total)
    probs_low = probs.astype(low)
    mixed = jnp.einsum("hqk,khd->qhd", probs_low, value_low, preferred_element_type=exact)
    out_heads = placed(mixed.astype(low).reshape(length, cols), ctx_count)
    out_low = exchange(out_heads.reshape(ctx_count, tokens, cols), "ctx")
    out_low = out_low.transpose(1, 0, 2).reshape(tokens, width)
    out_full = doubled(w_out, "fsdp", bits_of("fsdp")[::-1]).reshape(cols, width)
    out_full = gather_ctx(out_full).reshape(width, width)
    rows_in = hidden_in[0].astype(exact)
    resid_one = rows_in + dot(out_low, out_full)
    hidden_two, normed_two, scale_two = rms_apply(resid_one, ffn_scale)
    ffn_input = hidden_two.astype(low)

    input_near = near_first(ffn_input)
    input_rows = jnp.stack(
        [exchange(pick(hot, block), "ctx") for hot, block in zip(sends, input_near)]
    ).reshape(-1, width)

    def routed_softmax(rows, multi):
        logits = jnp.where(multi > 0, dot(rows, router_full), neg_large)
        top_value = jnp.max(logits, axis=-1, keepdims=True)
        weight = jnp.exp(logits - top_value)
        return weight / jnp.sum(weight, axis=-1, keepdims=True)

    row_gates = routed_softmax(input_rows, meta)
    row_gate = lax.dynamic_slice_in_dim(row_gates, own_expert, 1, 1)
    deout = (row_gate * cot_rows.astype(exact)).astype(low)
    gate_pre = dot(input_rows, gate_full)
    up_pre = dot(input_rows, up_full)
    sigmoid_gate = jax.nn.sigmoid(gate_pre)
    activated = gate_pre * sigmoid_gate
    inner_low = (activated * up_pre).astype(low)
    produced = dot(inner_low, down_full).astype(low)
    inner_grad = contract_cols(deout, down_full)
    gate_pre_grad = (
        inner_grad * up_pre * sigmoid_gate * (1.0 + gate_pre * (1.0 - sigmoid_gate))
    ).astype(low)
    up_pre_grad = (inner_grad * activated).astype(low)
    droute = (
        contract_cols(gate_pre_grad, gate_full) + contract_cols(up_pre_grad, up_full)
    ).astype(low)
    down_grad = contract_rows(inner_low, deout).astype(low)
    gate_grad = contract_rows(input_rows, gate_pre_grad).astype(low)
    up_grad = contract_rows(input_rows, up_pre_grad).astype(low)

    def whole_out(grad):
        rows = grad.shape[0] // z_count
        grad = exchange(grad.reshape(z_count, rows, part), "fsdp")
        grad = grad.reshape(exp_local, split, rows, z_count, part // z_count)
        return grad.transpose(0, 2, 3, 1, 4).reshape(exp_local, rows, hidden).astype(exact)

    grad_down = (
        exchange(down_grad.reshape(z_count, rows_d // split, width), "fsdp")
        .reshape(exp_local, rows_d, width)
        .astype(exact)
    )
    grad_gate = whole_out(gate_grad)
    grad_up = whole_out(up_grad)

    shape = (z_count, ctx_count, capacity, width)
    produced = produced.reshape(shape)
    droute = droute.reshape(shape)
    out_parts = []
    in_parts = []
    gate_sums = []
    for step in range(z_count):
        source = z_index ^ step
        hot = sends[step]
        multi = lax.dynamic_index_in_dim(multi_own, source, 0, False)
        gates = routed_softmax(input_near[step], multi)
        if step == 0:
            gates_own, multi_here = gates, multi
        plane = gates.reshape(tokens, ctx_count, exp_local)
        plane = lax.dynamic_index_in_dim(plane, z_index // split, 2, False)
        back = exchange(produced[step], "ctx")
        weighted = (hot * plane.T[:, None, :]).astype(low)
        out_parts.append(
            jnp.einsum("crt,crd->td", weighted, back, preferred_element_type=exact)
        )
        slot_grad = jnp.sum(cot_sent[step].astype(exact) * back.astype(exact), axis=-1)
        gate_sums.append(jnp.sum(hot.astype(exact) * slot_grad[:, :, None], axis=1).T)
        in_back = exchange(droute[step], "ctx")
        in_parts.append(
            jnp.einsum("crt,crd->td", hot, in_back, preferred_element_type=exact)
        )
    resid_two = resid_one + back_home(out_parts)
    out_hidden = resid_two.astype(low)[None]
    gate_grads = jnp.zeros((tokens, ctx_count, exp_local), exact)
    for step in range(z_count):
        got = swap(gate_sums[step], "fsdp", step) if step else gate_sums[step]
        place = ((z_index ^ step) // split) == jnp.arange(exp_local)
        gate_grads = gate_grads + got[:, :, None] * place.astype(exact)
    gate_grads = gate_grads.reshape(tokens, experts)
    weighted_sum = jnp.sum(gates_own * gate_grads, axis=-1, keepdims=True)
    logit_grad = (gates_own * (gate_grads - weighted_sum)).astype(low)
    input_grad = contract_cols(logit_grad, router_full) + back_home(in_parts)
    router_grad = contract_rows(ffn_input, logit_grad)
    grad_two = cotangent[0].astype(exact)
    resid_norm_grad, ffn_gain_grad = rms_back(input_grad, normed_two, scale_two, ffn_scale)
    grad_one = grad_two + resid_norm_grad

    attn_grad_low = grad_one.astype(low)
    attn_grad_all = gather_ctx(attn_grad_low).reshape(length, width)
    out_weight_grad = contract_rows(out_heads, attn_grad_all)
    grad_heads = contract_cols(attn_grad_low, out_full).astype(low)
    grad_heads = exchange(grad_heads.reshape(tokens, ctx_count, cols).transpose(1, 0, 2), "ctx")
    grad_heads = ordered(by_head(grad_heads), ctx_count)
    value_grad = jnp.einsum("hqk,qhd->khd", probs_low, grad_heads, preferred_element_type=exact)
    prob_grad = jnp.einsum("qhd,khd->hqk", grad_heads, value_low, preferred_element_type=exact)
    delta = jnp.sum(probs * prob_grad, axis=-1, keepdims=True)
    score_grad = (probs * (prob_grad - delta)).astype(low)
    query_rot_grad = scale * jnp.einsum(
        "hqk,khd->qhd", score_grad, key_rot, preferred_element_type=exact
    )
    key_rot_grad = scale * jnp.einsum(
        "hqk,qhd->khd", score_grad, query_rot, preferred_element_type=exact
    )
    query_back = rotate(placed(query_rot_grad, ctx_count), cosine, -sine).reshape(length, cols)
    key_back = rotate(placed(key_rot_grad, ctx_count), cosine, -sine).reshape(length, cols)
    value_grad_low = placed(value_grad.astype(low), ctx_count).reshape(length, cols)
    query_gain_grad = jnp.sum(query_back * query_normed, axis=0)
    key_gain_grad = jnp.sum(key_back * key_normed, axis=0)
    query_d, key_d = query_back * query_scale, key_back * key_scale
    inner_two = total_over_ctx(
        jnp.sum(query_d * query_normed, -1), jnp.sum(key_d * key_normed, -1)
    ) / width
    query_grad_low = (query_rms * (query_d - query_normed * inner_two[0][:, None])).astype(low)
    key_grad_low = (key_rms * (key_d - key_normed * inner_two[1][:, None])).astype(low)
    qkv_grad_low = jnp.concatenate([query_grad_low, key_grad_low, value_grad_low], axis=1)
    attn_input_grad = contract_cols(qkv_grad_low, qkv)
    qkv_weight_grad = contract_rows(attn_all, qkv_grad_low)
    attn_input_grad = scatter_ctx(attn_input_grad.reshape(ctx_count, tokens, width))
    _, normed_one, scale_one = rms_apply(rows_in, attn_scale)
    input_norm_grad, attn_gain_grad = rms_back(
        attn_input_grad, normed_one, scale_one, attn_scale
    )
    grad_hidden = (grad_one + input_norm_grad)[None]

    z_bits = bits_of("fsdp")
    pieces = qkv_weight_grad.reshape(ctx_count, z_count, rows_w, 3 * cols).transpose(1, 0, 2, 3)
    pieces = halved(pieces, "fsdp", z_bits).astype(low)
    pieces = exchange(pieces, "ctx").reshape(ctx_count, rows_w, 3, cols).astype(exact)
    pieces = pieces.transpose(2, 1, 0, 3).reshape(3, rows_w, width)
    grad_out = halved(out_weight_grad.reshape(z_count, rows_w, width), "fsdp", z_bits)
    sums = jnp.concatenate(
        [
            router_grad.reshape(ctx_count * z_count, rows_w * experts),
            ffn_gain_grad.reshape(-1, rows_w),
        ],
        axis=1,
    )
    sums = jnp.sum(exchange(sums, both), axis=0)
    grad_router = sums[: rows_w * experts].reshape(rows_w, experts)
    grad_ffn_gain = sums[rows_w * experts :]
    grad_attn_gain = jnp.sum(exchange(attn_gain_grad.reshape(-1, rows_w), both), axis=0)
    head_gains = jnp.stack([query_gain_grad, key_gain_grad], axis=1)
    head_gains = head_gains.reshape(z_count, rows_w, 2)
    head_gains = jnp.sum(exchange(head_gains, "fsdp"), axis=0)
    return (
        out_hidden,
        grad_hidden,
        grad_attn_gain,
        head_gains[:, 0],
        head_gains[:, 1],
        grad_ffn_gain,
        pieces[0],
        pieces[1],
        pieces[2],
        grad_out,
        grad_router,
        grad_gate,
        grad_up,
        grad_down,
    )


def solution(mesh):
    in_specs = (
        P("fsdp", "ctx", None),
        P("fsdp", "ctx", None),
        P("fsdp", "ctx", None),
        P(("ctx", "fsdp")),
        P(("ctx", "fsdp")),
        P(("ctx", "fsdp")),
        P(("ctx", "fsdp")),
        P(("ctx", "fsdp"), None),
        P(("ctx", "fsdp"), None),
        P(("ctx", "fsdp"), None),
        P(("ctx", "fsdp"), None),
        P(("ctx", "fsdp"), None),
        P("ctx", "fsdp", None),
        P("ctx", "fsdp", None),
        P("ctx", "fsdp", None),
    )
    out_specs = (
        P("fsdp", "ctx", None),
        P("fsdp", "ctx", None),
        P(("ctx", "fsdp")),
        P(("ctx", "fsdp")),
        P(("ctx", "fsdp")),
        P(("ctx", "fsdp")),
        P(("ctx", "fsdp"), None),
        P(("ctx", "fsdp"), None),
        P(("ctx", "fsdp"), None),
        P(("ctx", "fsdp"), None),
        P(("ctx", "fsdp"), None),
        P("ctx", "fsdp", None),
        P("ctx", "fsdp", None),
        P("ctx", "fsdp", None),
    )
    return jax.shard_map(body, mesh=mesh, in_specs=in_specs, out_specs=out_specs, check_vma=False)
```

time: 3920 us -> 1720 us (0.44)
  waiting for transfers between devices: 2930 us -> 655 us
  starting transfers between devices: 58 us -> 165 us
  matrix products: 348 us -> 266 us
  other arithmetic: 124 us -> 202 us
  blocking collectives: 283 us -> 233 us
    reduce_scatter x7 -> x0, waiting for transfers between devices: 1540 us -> none  [the longest x1 365 us: body(): lax.psum_scatter(value_weight_grad, ('ctx', 'fsdp'), scatter_dimension=0,...]
    all_gather x9 -> x0, waiting for transfers between devices: 930 us -> none  [the longest x1 270 us: body(): lax.all_gather(w_up, 'fsdp', axis=1, tiled=True)]
    all_to_all x3 -> x26, waiting for transfers between devices: 94 us -> 342 us  [exchange(): return lax.all_to_all(x, axis, split_axis=0, concat_axis=0, tiled=True)]
    dot_general x57 -> x44, matrix products: 286 us -> 148 us  [the longest x10 57.7 us: dot(): return jnp.dot(left, right, preferred_element_type=exact)]
    all_to_all x3 -> x26, starting transfers between devices: 29.7 us -> 117 us  [exchange(): return lax.all_to_all(x, axis, split_axis=0, concat_axis=0, tiled=True)]
    unnamed x2 -> x0, blocking collectives: 82.6 us -> none
    gather x4 -> x0, local copies, waits for them, and re-layouts: 65.2 us -> none  [the longest x1 19.9 us: body(): route_padded[slot_entry].reshape(ctx_count, exp_local * capacity, width)]
    convert_element_type x14 -> x27, other arithmetic: 24.6 us -> 78.1 us  [the longest x3 25.5 us: body(): deout = (row_gate * cot_rows.astype(exact)).astype(low)]
  transfers between devices with their start and end apart: 52 -> 73, of which waited for: 31 -> 36; matrix products, arithmetic and copies ran while one was open for 14% -> 33% of each run, Pallas kernels for 0% -> 0%
where the time goes in v1:
time: 1720 us; the launch traced here: 1700 us
  waiting for transfers between devices  655 us (38%)
  matrix products  266 us (15%)
  blocking collectives  233 us (14%)
  other arithmetic  202 us (12%)
  local copies, waits for them, and re-layouts  179 us (10%)
  starting transfers between devices  165 us (10%)
    all_to_all x26, waiting for transfers between devices, exchange(): return lax.all_to_all(x, axis, split_axis=0, concat_axis=0, tiled=True)  342 us
    ppermute x47, waiting for transfers between devices, swap(): return lax.ppermute(x, axis, [(i, i ^ bit) for i in range(length)])  313 us
    all_to_all x4, blocking collectives, exchange(): return lax.all_to_all(x, axis, split_axis=0, concat_axis=0, tiled=True)  121 us
    all_to_all x26, starting transfers between devices, exchange(): return lax.all_to_all(x, axis, split_axis=0, concat_axis=0, tiled=True)  117 us
    all_gather x1, blocking collectives, body(): routes_all = lax.all_gather(routes[0], both, axis=0)  92.9 us
    dot_general x6, matrix products, contract_cols(): lax.dot_general(left, right, (((1,), (1,)), ((), ())), preferred_element_...  67.1 us
    dot_general x10, matrix products, dot(): return jnp.dot(left, right, preferred_element_type=exact)  57.7 us
    unnamed x406, local copies, waits for them, and re-layouts  54.7 us
  transfers between devices with their start and end apart: 73, of which 36 were waited for; matrix products, arithmetic and copies ran while one was open for 33% of the time, Pallas kernels for 0%

profile of v1, /device:TPU:0, one launch (start us, length us, event | category | flops | bytes accessed | tf_op | source)
XLA Modules:
  0.0 1703.8 jit_solution(2343223585701015822)
XLA Ops:
  20.6 92.9 %all_gather.17 = s32[32,192,8]{1,2,0:T(8,128)S(1)} all-gather(s32[1,192,8]{1,2,0:T(8,128)S(1)} %copy-done.171), channel_id=1, replica_groups=mesh['ctx'=8,'fsdp'=4] {'ctx','fsdp'}, dimensions={0}, use_global_device_ids=true | all-gather | bytes 202752 | tf_op jit(solution)/shard_map/all_gather | solution.py:207
  169.5 27.5 %collective-permute-done.10 = bf16[256,1024]{1,0:T(8,128)(2,1)S(1)} collective-permute-done((bf16[256,1024]{1,0:T(8,128)(2,1)S(1)}, bf16[256,1024]{1,0:T(8,128)(2,1)S(1)}, u32[]{:S(2)}, u32[]{:S(2)}) %collective-permute-start.10) | collective-permute-done | bytes 524320 | tf_op jit(solution)/shard_map/ppermute | solution.py:17
  206.8 16.5 collective-permute-done.14
  252.6 9.7 all-gather.2
  295.8 8.7 fusion.277
  311.8 8.9 exponential_reduce_fusion
  323.6 12.1 all-to-all-done.15
  340.1 9.9 fusion.34
  401.1 13.7 all-to-all-done.17
  414.8 30.9 %all_to_all.162 = bf16[8,64,2048]{2,1,0:T(8,128)(2,1)} all-to-all(bf16[8,64,2048]{2,1,0:T(8,128)(2,1)} %convolution_convert_fusion.11), channel_id=1, replica_groups=mesh['ctx'=8,'fsdp'=4] {'ctx'}, dimensions={0} | all-to-all | bytes 4194304 | tf_op jit(solution)/shard_map/all_to_all | solution.py:90
  452.5 82.1 %collective-permute-done.16 = bf16[192,2048]{1,0:T(8,128)(2,1)S(1)} collective-permute-done((bf16[192,2048]{1,0:T(8,128)(2,1)S(1)}, bf16[192,2048]{1,0:T(8,128)(2,1)S(1)}, u32[]{:S(2)}, u32[]{:S(2)}) %collective-permute-start.16) | collective-permute-done | bytes 786464 | tf_op jit(solution)/shard_map/ppermute | solution.py:17
  547.8 36.3 %collective-permute-done.17 = bf16[192,2048]{1,0:T(8,128)(2,1)S(1)} collective-permute-done((bf16[192,2048]{1,0:T(8,128)(2,1)S(1)}, bf16[192,2048]{1,0:T(8,128)(2,1)S(1)}, u32[]{:S(2)}, u32[]{:S(2)}) %collective-permute-start.17) | collective-permute-done | bytes 786464 | tf_op jit(solution)/shard_map/ppermute | solution.py:17
  591.7 19.7 %collective-permute-done.18 = bf16[192,2048]{1,0:T(8,128)(2,1)S(1)} collective-permute-done((bf16[192,2048]{1,0:T(8,128)(2,1)S(1)}, bf16[192,2048]{1,0:T(8,128)(2,1)S(1)}, u32[]{:S(2)}, u32[]{:S(2)}) %collective-permute-start.18) | collective-permute-done | bytes 786464 | tf_op jit(solution)/shard_map/ppermute | solution.py:17
  618.2 30.9 %all_to_all.163 = bf16[8,64,2048]{2,1,0:T(8,128)(2,1)} all-to-all(bf16[8,64,2048]{2,1,0:T(8,128)(2,1)} %convolution_convert_fusion.8), channel_id=1, replica_groups=mesh['ctx'=8,'fsdp'=4] {'ctx'}, dimensions={0} | all-to-all | bytes 4194304 | tf_op jit(solution)/shard_map/all_to_all | solution.py:90
  670.0 76.9 %all-to-all-done.8 = bf16[4,512,1024]{2,1,0:T(8,128)(2,1)} async-done(((bf16[4,512,1024]{2,1,0:T(8,128)(2,1)}), bf16[4,512,1024]{2,1,0:T(8,128)(2,1)}, u32[]{:S(2)}, u32[]{:S(2)}) %all-to-all-start.8) | async-done | bytes 4194336 | tf_op jit(solution)/shard_map/all_to_all | solution.py:90
  767.7 14.6 fusion.284
  782.3 12.7 fusion.283
  795.0 49.8 %all-to-all-done.9 = bf16[4,256,2048]{2,1,0:T(8,128)(2,1)} async-done(((bf16[4,256,2048]{2,1,0:T(8,128)(2,1)}), bf16[4,256,2048]{2,1,0:T(8,128)(2,1)}, u32[]{:S(2)}, u32[]{:S(2)}) %all-to-all-start.9) | async-done | bytes 4194336 | tf_op jit(solution)/shard_map/all_to_all | solution.py:90
  844.8 23.5 %multiply_convert_fusion.2 = (bf16[2048,1024]{1,0:T(8,128)(2,1)}, bf16[2048,1024]{1,0:T(8,128)(2,1)}, bf16[2048,1024]{1,0:T(8,128)(2,1)}) fusion(f32[2048,1024]{1,0:T(8,128)} %fusion.283, f32[2048,1024]{1,0:T(8,128)} %fusion.284, bf16[2048,2048]{1,0:T(8,128)(2,1)} %bitcast.724, bf16[1024,2048]{1,0:T(8,128)(2,1)} %bitcast.96), kind=kOutput, calls=%fused_computation.26 | convolution fusion | flops 8621391872 | bytes 41943040 | tf_op jit(solution)/shard_map/dot_general | solution.py:133
  868.4 11.9 convolution_convert_fusion
  882.8 29.8 %all_to_all.164 = bf16[8,64,2048]{2,1,0:T(8,128)(2,1)} all-to-all(bf16[8,64,2048]{2,1,0:T(8,128)(2,1)S(1)} %bitcast.734), channel_id=1, replica_groups=mesh['ctx'=8,'fsdp'=4] {'ctx'}, dimensions={0} | all-to-all | bytes 4194304 | tf_op jit(solution)/shard_map/all_to_all | solution.py:90
  912.6 29.8 %all_to_all.165 = bf16[8,64,2048]{2,1,0:T(8,128)(2,1)} all-to-all(bf16[8,64,2048]{2,1,0:T(8,128)(2,1)S(1)} %bitcast.733), channel_id=1, replica_groups=mesh['ctx'=8,'fsdp'=4] {'ctx'}, dimensions={0} | all-to-all | bytes 4194304 | tf_op jit(solution)/shard_map/all_to_all | solution.py:90
  946.2 15.4 fusion.286
  961.6 11.1 all-to-all-done.12
  977.7 16.4 add_convert_fusion
  1012.6 23.4 %all-to-all-done.21 = bf16[8,64,2048]{2,1,0:T(8,128)(2,1)S(1)} async-done(((bf16[8,64,2048]{2,1,0:T(8,128)(2,1)}), bf16[8,64,2048]{2,1,0:T(8,128)(2,1)S(1)}, u32[]{:S(2)}, u32[]{:S(2)}) %all-to-all-start.21) | async-done | bytes 2097184 | tf_op jit(solution)/shard_map/all_to_all | solution.py:90
  1047.8 8.7 copy.538
  1056.4 9.6 reshape.763
  1067.2 8.6 maximum_convert_fusion
  1089.0 19.0 %all-to-all-done.18 = bf16[8,64,2048]{2,1,0:T(8,128)(2,1)} async-done(((bf16[8,64,2048]{2,1,0:T(8,128)(2,1)}), bf16[8,64,2048]{2,1,0:T(8,128)(2,1)}, u32[]{:S(2)}, u32[]{:S(2)}) %all-to-all-start.18) | async-done | bytes 2097184 | tf_op jit(solution)/shard_map/all_to_all | solution.py:90
  1130.1 9.5 all-to-all-done.20
  1149.3 20.0 %collective-permute-done.28 = bf16[192,2048]{1,0:T(8,128)(2,1)} collective-permute-done((bf16[192,2048]{1,0:T(8,128)(2,1)}, bf16[192,2048]{1,0:T(8,128)(2,1)}, u32[]{:S(2)}, u32[]{:S(2)}) %collective-permute-start.28) | collective-permute-done | bytes 786464 | tf_op jit(solution)/shard_map/ppermute | solution.py:17
  1169.3 11.1 collective-permute-done.30
  1193.9 9.3 fusion
  1212.4 11.7 multiply_reduce_fusion
  1224.1 13.2 multiply_convert_fusion
  1275.5 14.0 convolution_convert_fusion.1
  1295.7 14.2 convolution_convert_fusion.2
  1310.0 13.0 convolution_convert_fusion.3
  1334.9 46.0 %collective-permute-done.20 = bf16[192,2048]{1,0:T(8,128)(2,1)} collective-permute-done((bf16[192,2048]{1,0:T(8,128)(2,1)}, bf16[192,2048]{1,0:T(8,128)(2,1)}, u32[]{:S(2)}, u32[]{:S(2)}) %collective-permute-start.20) | collective-permute-done | bytes 786464 | tf_op jit(solution)/shard_map/ppermute | solution.py:17
  1401.5 9.6 fusion.37
  1424.5 9.3 all-gather.3
  1464.7 21.8 %all-to-all-done.27 = bf16[4,512,1024]{2,1,0:T(8,128)(2,1)} async-done(((bf16[4,512,1024]{2,1,0:T(8,128)(2,1)}), bf16[4,512,1024]{2,1,0:T(8,128)(2,1)}, u32[]{:S(2)}, u32[]{:S(2)}) %all-to-all-start.27) | async-done | bytes 4194336 | tf_op jit(solution)/shard_map/all_to_all | solution.py:90
  1491.6 9.4 fusion.262
  1518.6 14.0 collective-permute-done.37
  1564.8 55.0 %all-to-all-done.28 = bf16[4,512,1024]{2,1,0:T(8,128)(2,1)} async-done(((bf16[4,512,1024]{2,1,0:T(8,128)(2,1)}), bf16[4,512,1024]{2,1,0:T(8,128)(2,1)}, u32[]{:S(2)}, u32[]{:S(2)}) %all-to-all-start.28) | async-done | bytes 4194336 | tf_op jit(solution)/shard_map/all_to_all | solution.py:90
  1632.2 18.3 %collective-permute-done.38 = bf16[8,64,768]{2,1,0:T(8,128)(2,1)} collective-permute-done((bf16[8,64,768]{2,1,0:T(8,128)(2,1)}, bf16[8,64,768]{2,1,0:T(8,128)(2,1)}, u32[]{:S(2)}, u32[]{:S(2)}) %collective-permute-start.38) | collective-permute-done | bytes 786464 | tf_op jit(solution)/shard_map/ppermute | solution.py:17
  1670.4 8.4 all-to-all-done.23
  (857 shorter events, 630.5 us)
Async XLA Ops:
  0.7 153.3 %collective-permute-start.24 = (bf16[192,2048]{1,0:T(8,128)(2,1)}, bf16[192,2048]{1,0:T(8,128)(2,1)}, u32[]{:S(2)}, u32[]{:S(2)}) collective-permute-start(bf16[192,2048]{1,0:T(8,128)(2,1)} %bitcast.741), channel_id=1, source_target_pairs={{0,2},{1,3},{2,0},{3,1},{4,6},{5,7},{6,4},{7,5},{8,10},{9,11},{10,... | collective-permute-start | bytes 2359304 | tf_op jit(solution)/shard_map/ppermute | solution.py:17
  4.8 193.2 %collective-permute-start.22 = (bf16[192,2048]{1,0:T(8,128)(2,1)}, bf16[192,2048]{1,0:T(8,128)(2,1)}, u32[]{:S(2)}, u32[]{:S(2)}) collective-permute-start(bf16[192,2048]{1,0:T(8,128)(2,1)} %bitcast.742), channel_id=1, source_target_pairs={{0,1},{1,0},{2,3},{3,2},{4,5},{5,4},{6,7},{7,6},{8,9},{9,8},{10,11... | collective-permute-start | bytes 2359304 | tf_op jit(solution)/shard_map/ppermute | solution.py:17
  6.3 123.1 %collective-permute-start.8 = (bf16[64,2048]{1,0:T(8,128)(2,1)}, bf16[64,2048]{1,0:T(8,128)(2,1)S(1)}, u32[]{:S(2)}, u32[]{:S(2)}) collective-permute-start(bf16[64,2048]{1,0:T(8,128)(2,1)} %param.25), channel_id=1, source_target_pairs={{0,2},{1,3},{2,0},{3,1},{4,6},{5,7},{6,4},{7,5},{8,10},{9,11},{10,... | collective-permute-start | bytes 786440 | tf_op jit(solution)/shard_map/ppermute | solution.py:17
  11.2 119.9 %all-to-all-start = ((bf16[32,2,1152]{2,1,0:T(2,128)(2,1)}), bf16[32,2,1152]{2,1,0:T(2,128)(2,1)S(1)}, u32[]{:S(2)}, u32[]{:S(2)}) async-start(bf16[32,2,1152]{2,1,0:T(2,128)(2,1)} %reshape.801), calls=%async_computation | async-start | bytes 294912 | tf_op jit(solution)/shard_map/all_to_all | solution.py:90
  17.3 119.4 %collective-permute-start = (bf16[192,1024]{1,0:T(8,128)(2,1)S(1)}, bf16[192,1024]{1,0:T(8,128)(2,1)}, u32[]{:S(2)}, u32[]{:S(2)}) collective-permute-start(bf16[192,1024]{1,0:T(8,128)(2,1)S(1)} %get-tuple-element.246), channel_id=1, source_target_pairs={{0,8},{4,12},{8,0},{12,4},{16,24},{20,28},{24,16},{28,20},{1,9},{5... | collective-permute-start | bytes 1179656 | tf_op jit(solution)/shard_map/ppermute | solution.py:17
  19.1 117.6 %collective-permute-start.3 = (bf16[192,1024]{1,0:T(8,128)(2,1)S(1)}, bf16[192,1024]{1,0:T(8,128)(2,1)}, u32[]{:S(2)}, u32[]{:S(2)}) collective-permute-start(bf16[192,1024]{1,0:T(8,128)(2,1)S(1)} %get-tuple-element.247), channel_id=1, source_target_pairs={{0,16},{4,20},{8,24},{12,28},{16,0},{20,4},{24,8},{28,12},{1,17},{... | collective-permute-start | bytes 1179656 | tf_op jit(solution)/shard_map/ppermute | solution.py:17
  148.7 155.8 %all-to-all-start.14 = ((bf16[8,64,2048]{2,1,0:T(8,128)(2,1)}), bf16[8,64,2048]{2,1,0:T(8,128)(2,1)S(1)}, u32[]{:S(2)}, u32[]{:S(2)}) async-start(bf16[8,64,2048]{2,1,0:T(8,128)(2,1)} %convolution_convert_fusion.7), calls=%async_computation.14 | async-start | bytes 4194304 | tf_op jit(solution)/shard_map/all_to_all | solution.py:90
  152.5 46.4 %collective-permute-start.6 = (bf16[8,64,3,256]{3,1,2,0:T(8,128)(2,1)}, bf16[8,64,3,256]{3,1,2,0:T(8,128)(2,1)S(1)}, u32[]{:S(2)}, u32[]{:S(2)}) collective-permute-start(bf16[8,64,3,256]{3,1,2,0:T(8,128)(2,1)} %copy-done.89), channel_id=1, source_target_pairs={{0,2},{1,3},{2,0},{3,1},{4,6},{5,7},{6,4},{7,5},{8,10},{9,11},{10,... | collective-permute-start | bytes 2359304 | tf_op jit(solution)/shard_map/ppermute | solution.py:17
  154.0 43.0 %collective-permute-start.10 = (bf16[256,1024]{1,0:T(8,128)(2,1)S(1)}, bf16[256,1024]{1,0:T(8,128)(2,1)S(1)}, u32[]{:S(2)}, u32[]{:S(2)}) collective-permute-start(bf16[256,1024]{1,0:T(8,128)(2,1)S(1)} %get-tuple-element.228), channel_id=1, source_target_pairs={{0,8},{4,12},{8,0},{12,4},{16,24},{20,28},{24,16},{28,20},{1,9},{5... | collective-permute-start | bytes 1572872 | tf_op jit(solution)/shard_map/ppermute | solution.py:17
  163.8 33.4 %collective-permute-start.13 = (bf16[256,1024]{1,0:T(8,128)(2,1)S(1)}, bf16[256,1024]{1,0:T(8,128)(2,1)S(1)}, u32[]{:S(2)}, u32[]{:S(2)}) collective-permute-start(bf16[256,1024]{1,0:T(8,128)(2,1)S(1)} %get-tuple-element.229), channel_id=1, source_target_pairs={{0,16},{4,20},{8,24},{12,28},{16,0},{20,4},{24,8},{28,12},{1,17},{... | collective-permute-start | bytes 1572872 | tf_op jit(solution)/shard_map/ppermute | solution.py:17
  166.7 36.8 %collective-permute-start.26 = (bf16[192,2048]{1,0:T(8,128)(2,1)}, bf16[192,2048]{1,0:T(8,128)(2,1)S(1)}, u32[]{:S(2)}, u32[]{:S(2)}) collective-permute-start(bf16[192,2048]{1,0:T(8,128)(2,1)} %collective-permute-done.24), channel_id=1, source_target_pairs={{0,1},{1,0},{2,3},{3,2},{4,5},{5,4},{6,7},{7,6},{8,9},{9,8},{10,11... | collective-permute-start | bytes 2359304 | tf_op jit(solution)/shard_map/ppermute | solution.py:17
  197.0 31.5 %collective-permute-start.5 = (bf16[2,2,192,1024]{3,2,1,0:T(8,128)(2,1)S(1)}, bf16[2,2,192,1024]{3,2,1,0:T(8,128)(2,1)S(1)}, u32[]{:S(2)}, u32[]{:S(2)}) collective-permute-start(bf16[2,2,192,1024]{3,2,1,0:T(8,128)(2,1)S(1)} %pad_maximum_fusion.6), channel_id=1, source_target_pairs={{0,4},{4,0},{8,12},{12,8},{16,20},{20,16},{24,28},{28,24},{1,5},{5... | collective-permute-start | bytes 4718600 | tf_op jit(solution)/shard_map/ppermute | solution.py:17
  197.2 31.3 %collective-permute-start.2 = (bf16[2,2,192,1024]{3,2,1,0:T(8,128)(2,1)S(1)}, bf16[2,2,192,1024]{3,2,1,0:T(8,128)(2,1)S(1)}, u32[]{:S(2)}, u32[]{:S(2)}) collective-permute-start(bf16[2,2,192,1024]{3,2,1,0:T(8,128)(2,1)S(1)} %pad_maximum_fusion.5), channel_id=1, source_target_pairs={{0,4},{4,0},{8,12},{12,8},{16,20},{20,16},{24,28},{28,24},{1,5},{5... | collective-permute-start | bytes 4718600 | tf_op jit(solution)/shard_map/ppermute | solution.py:17
  203.5 35.8 %collective-permute-start.7 = (bf16[2,8,64,3,256]{4,2,3,1,0:T(8,128)(2,1)S(1)}, bf16[2,8,64,3,256]{4,2,3,1,0:T(8,128)(2,1)S(1)}, u32[]{:S(2)}, u32[]{:S(2)}) collective-permute-start(bf16[2,8,64,3,256]{4,2,3,1,0:T(8,128)(2,1)S(1)} %pad_maximum_fusion.7), channel_id=1, source_target_pairs={{0,1},{1,0},{2,3},{3,2},{4,5},{5,4},{6,7},{7,6},{8,9},{9,8},{10,11... | collective-permute-start | bytes 4718600 | tf_op jit(solution)/shard_map/ppermute | solution.py:17
  226.4 144.6 %collective-permute-start.12 = (bf16[2,2,256,1024]{3,2,1,0:T(8,128)(2,1)}, bf16[2,2,256,1024]{3,2,1,0:T(8,128)(2,1)}, u32[]{:S(2)}, u32[]{:S(2)}) collective-permute-start(bf16[2,2,256,1024]{3,2,1,0:T(8,128)(2,1)} %pad_maximum_fusion.3), channel_id=1, source_target_pairs={{0,4},{4,0},{8,12},{12,8},{16,20},{20,16},{24,28},{28,24},{1,5},{5... | collective-permute-start | bytes 6291464 | tf_op jit(solution)/shard_map/ppermute | solution.py:17
  228.5 147.7 %collective-permute-start.15 = (bf16[2,2,256,1024]{3,2,1,0:T(8,128)(2,1)}, bf16[2,2,256,1024]{3,2,1,0:T(8,128)(2,1)}, u32[]{:S(2)}, u32[]{:S(2)}) collective-permute-start(bf16[2,2,256,1024]{3,2,1,0:T(8,128)(2,1)} %pad_maximum_fusion.4), channel_id=1, source_target_pairs={{0,4},{4,0},{8,12},{12,8},{16,20},{20,16},{24,28},{28,24},{1,5},{5... | collective-permute-start | bytes 6291464 | tf_op jit(solution)/shard_map/ppermute | solution.py:17
  304.5 31.2 %all-to-all-start.15 = ((bf16[8,64,2048]{2,1,0:T(8,128)(2,1)}), bf16[8,64,2048]{2,1,0:T(8,128)(2,1)}, u32[]{:S(2)}, u32[]{:S(2)}) async-start(bf16[8,64,2048]{2,1,0:T(8,128)(2,1)} %convolution_convert_fusion.6), calls=%async_computation.15 | async-start | bytes 4194304 | tf_op jit(solution)/shard_map/all_to_all | solution.py:90
  383.6 31.2 %all-to-all-start.17 = ((bf16[8,64,2048]{2,1,0:T(8,128)(2,1)}), bf16[8,64,2048]{2,1,0:T(8,128)(2,1)}, u32[]{:S(2)}, u32[]{:S(2)}) async-start(bf16[8,64,2048]{2,1,0:T(8,128)(2,1)} %convolution_convert_fusion.4), calls=%async_computation.17 | async-start | bytes 4194304 | tf_op jit(solution)/shard_map/all_to_all | solution.py:90
  445.7 97.7 %all-to-all-start.7 = ((bf16[4,512,1024]{2,1,0:T(8,128)(2,1)}), bf16[4,512,1024]{2,1,0:T(8,128)(2,1)}, u32[]{:S(2)}, u32[]{:S(2)}) async-start(bf16[4,512,1024]{2,1,0:T(8,128)(2,1)} %param.27), calls=%async_computation.7 | async-start | bytes 8388608 | tf_op jit(solution)/shard_map/all_to_all | solution.py:90
  450.6 84.1 %collective-permute-start.16 = (bf16[192,2048]{1,0:T(8,128)(2,1)S(1)}, bf16[192,2048]{1,0:T(8,128)(2,1)S(1)}, u32[]{:S(2)}, u32[]{:S(2)}) collective-permute-start(bf16[192,2048]{1,0:T(8,128)(2,1)S(1)} %multiply_convert_fusion.7), channel_id=1, source_target_pairs={{0,1},{1,0},{2,3},{3,2},{4,5},{5,4},{6,7},{7,6},{8,9},{9,8},{10,11... | collective-permute-start | bytes 2359304 | tf_op jit(solution)/shard_map/ppermute | solution.py:17
  543.4 43.7 %all-to-all-start.4 = ((bf16[8,64,2048]{2,1,0:T(8,128)(2,1)}), bf16[8,64,2048]{2,1,0:T(8,128)(2,1)}, u32[]{:S(2)}, u32[]{:S(2)}) async-start(bf16[8,64,2048]{2,1,0:T(8,128)(2,1)} %convolution_convert_fusion.10), calls=%async_computation.4 | async-start | bytes 4194304 | tf_op jit(solution)/shard_map/all_to_all | solution.py:90
  547.8 36.4 %collective-permute-start.17 = (bf16[192,2048]{1,0:T(8,128)(2,1)S(1)}, bf16[192,2048]{1,0:T(8,128)(2,1)S(1)}, u32[]{:S(2)}, u32[]{:S(2)}) collective-permute-start(bf16[192,2048]{1,0:T(8,128)(2,1)S(1)} %multiply_convert_fusion.7), channel_id=1, source_target_pairs={{0,2},{1,3},{2,0},{3,1},{4,6},{5,7},{6,4},{7,5},{8,10},{9,11},{10,... | collective-permute-start | bytes 2359304 | tf_op jit(solution)/shard_map/ppermute | solution.py:17
  587.1 31.2 %all-to-all-start.5 = ((bf16[8,64,2048]{2,1,0:T(8,128)(2,1)}), bf16[8,64,2048]{2,1,0:T(8,128)(2,1)}, u32[]{:S(2)}, u32[]{:S(2)}) async-start(bf16[8,64,2048]{2,1,0:T(8,128)(2,1)} %convolution_convert_fusion.9), calls=%async_computation.5 | async-start | bytes 4194304 | tf_op jit(solution)/shard_map/all_to_all | solution.py:90
  649.2 97.7 %all-to-all-start.8 = ((bf16[4,512,1024]{2,1,0:T(8,128)(2,1)}), bf16[4,512,1024]{2,1,0:T(8,128)(2,1)}, u32[]{:S(2)}, u32[]{:S(2)}) async-start(bf16[4,512,1024]{2,1,0:T(8,128)(2,1)} %param.28), calls=%async_computation.8 | async-start | bytes 8388608 | tf_op jit(solution)/shard_map/all_to_all | solution.py:90
  746.9 97.9 %all-to-all-start.9 = ((bf16[4,256,2048]{2,1,0:T(8,128)(2,1)}), bf16[4,256,2048]{2,1,0:T(8,128)(2,1)}, u32[]{:S(2)}, u32[]{:S(2)}) async-start(bf16[4,256,2048]{2,1,0:T(8,128)(2,1)} %param.29), calls=%async_computation.9 | async-start | bytes 8388608 | tf_op jit(solution)/shard_map/all_to_all | solution.py:90
  1037.3 39.5 %all-to-all-start.19 = ((bf16[8,64,2048]{2,1,0:T(8,128)(2,1)}), bf16[8,64,2048]{2,1,0:T(8,128)(2,1)}, u32[]{:S(2)}, u32[]{:S(2)}) async-start(bf16[8,64,2048]{2,1,0:T(8,128)(2,1)} %bitcast.729), calls=%async_computation.19 | async-start | bytes 4194304 | tf_op jit(solution)/shard_map/all_to_all | solution.py:90
  1076.8 31.2 %all-to-all-start.18 = ((bf16[8,64,2048]{2,1,0:T(8,128)(2,1)}), bf16[8,64,2048]{2,1,0:T(8,128)(2,1)}, u32[]{:S(2)}, u32[]{:S(2)}) async-start(bf16[8,64,2048]{2,1,0:T(8,128)(2,1)} %bitcast.727), calls=%async_computation.18 | async-start | bytes 4194304 | tf_op jit(solution)/shard_map/all_to_all | solution.py:90
  1089.0 59.0 %collective-permute-start.25 = (f32[192,8]{0,1:T(8,128)}, f32[192,8]{0,1:T(8,128)}, u32[]{:S(2)}, u32[]{:S(2)}) collective-permute-start(f32[192,8]{0,1:T(8,128)} %bitcast.118), channel_id=1, source_target_pairs={{0,2},{1,3},{2,0},{3,1},{4,6},{5,7},{6,4},{7,5},{8,10},{9,11},{10,... | collective-permute-start | bytes 18440 | tf_op jit(solution)/shard_map/ppermute | solution.py:17
  1108.0 31.6 %all-to-all-start.20 = ((bf16[8,64,2048]{2,1,0:T(8,128)(2,1)}), bf16[8,64,2048]{2,1,0:T(8,128)(2,1)}, u32[]{:S(2)}, u32[]{:S(2)}) async-start(bf16[8,64,2048]{2,1,0:T(8,128)(2,1)} %bitcast.725), calls=%async_computation.20 | async-start | bytes 4194304 | tf_op jit(solution)/shard_map/all_to_all | solution.py:90
  1124.8 44.5 %collective-permute-start.28 = (bf16[192,2048]{1,0:T(8,128)(2,1)}, bf16[192,2048]{1,0:T(8,128)(2,1)}, u32[]{:S(2)}, u32[]{:S(2)}) collective-permute-start(bf16[192,2048]{1,0:T(8,128)(2,1)} %fusion.30), channel_id=1, source_target_pairs={{0,1},{1,0},{2,3},{3,2},{4,5},{5,4},{6,7},{7,6},{8,9},{9,8},{10,11... | collective-permute-start | bytes 2359304 | tf_op jit(solution)/shard_map/ppermute | solution.py:17
  1144.3 36.1 %collective-permute-start.30 = (bf16[192,2048]{1,0:T(8,128)(2,1)}, bf16[192,2048]{1,0:T(8,128)(2,1)}, u32[]{:S(2)}, u32[]{:S(2)}) collective-permute-start(bf16[192,2048]{1,0:T(8,128)(2,1)} %add_convert_fusion.1), channel_id=1, source_target_pairs={{0,2},{1,3},{2,0},{3,1},{4,6},{5,7},{6,4},{7,5},{8,10},{9,11},{10,... | collective-permute-start | bytes 2359304 | tf_op jit(solution)/shard_map/ppermute | solution.py:17
  1206.5 63.6 %all-to-all-start.25 = ((f32[32,1,2112]{2,1,0:T(1,128)}), f32[32,1,2112]{2,1,0:T(1,128)S(1)}, u32[]{:S(2)}, u32[]{:S(2)}) async-start(f32[32,1,2112]{2,1,0:T(1,128)} %copy.537), calls=%async_computation.25 | async-start | bytes 557056 | tf_op jit(solution)/shard_map/all_to_all | solution.py:90
  1290.1 98.5 %all-to-all-start.29 = ((bf16[4,256,2048]{2,1,0:T(8,128)(2,1)}), bf16[4,256,2048]{2,1,0:T(8,128)(2,1)}, u32[]{:S(2)}, u32[]{:S(2)}) async-start(bf16[4,256,2048]{2,1,0:T(8,128)(2,1)} %bitcast.754), calls=%async_computation.29 | async-start | bytes 8388608 | tf_op jit(solution)/shard_map/all_to_all | solution.py:90
  1324.5 56.4 %collective-permute-start.20 = (bf16[192,2048]{1,0:T(8,128)(2,1)}, bf16[192,2048]{1,0:T(8,128)(2,1)}, u32[]{:S(2)}, u32[]{:S(2)}) collective-permute-start(bf16[192,2048]{1,0:T(8,128)(2,1)} %fusion.29), channel_id=1, source_target_pairs={{0,1},{1,0},{2,3},{3,2},{4,5},{5,4},{6,7},{7,6},{8,9},{9,8},{10,11... | collective-permute-start | bytes 2359304 | tf_op jit(solution)/shard_map/ppermute | solution.py:17
  1328.1 354.8 %collective-permute-start.19 = (bf16[192,2048]{1,0:T(8,128)(2,1)}, bf16[192,2048]{1,0:T(8,128)(2,1)}, u32[]{:S(2)}, u32[]{:S(2)}) collective-permute-start(bf16[192,2048]{1,0:T(8,128)(2,1)} %fusion.28), channel_id=1, source_target_pairs={{0,1},{1,0},{2,3},{3,2},{4,5},{5,4},{6,7},{7,6},{8,9},{9,8},{10,11... | collective-permute-start | bytes 2359304 | tf_op jit(solution)/shard_map/ppermute | solution.py:17
  1330.1 63.7 %collective-permute-start.39 = (bf16[192,1024]{1,0:T(8,128)(2,1)}, bf16[192,1024]{1,0:T(8,128)(2,1)}, u32[]{:S(2)}, u32[]{:S(2)}) collective-permute-start(bf16[192,1024]{1,0:T(8,128)(2,1)} %get-tuple-element.234), channel_id=1, source_target_pairs={{0,8},{4,12},{8,0},{12,4},{16,24},{20,28},{24,16},{28,20},{1,9},{5... | collective-permute-start | bytes 1179656 | tf_op jit(solution)/shard_map/ppermute | solution.py:17
  1331.6 62.2 %collective-permute-start.42 = (bf16[192,1024]{1,0:T(8,128)(2,1)S(1)}, bf16[192,1024]{1,0:T(8,128)(2,1)}, u32[]{:S(2)}, u32[]{:S(2)}) collective-permute-start(bf16[192,1024]{1,0:T(8,128)(2,1)S(1)} %get-tuple-element.235), channel_id=1, source_target_pairs={{0,16},{4,20},{8,24},{12,28},{16,0},{20,4},{24,8},{28,12},{1,17},{... | collective-permute-start | bytes 1179656 | tf_op jit(solution)/shard_map/ppermute | solution.py:17
  1388.6 97.9 %all-to-all-start.27 = ((bf16[4,512,1024]{2,1,0:T(8,128)(2,1)}), bf16[4,512,1024]{2,1,0:T(8,128)(2,1)}, u32[]{:S(2)}, u32[]{:S(2)}) async-start(bf16[4,512,1024]{2,1,0:T(8,128)(2,1)} %bitcast.753), calls=%async_computation.27 | async-start | bytes 8388608 | tf_op jit(solution)/shard_map/all_to_all | solution.py:90
  1396.0 119.5 %collective-permute-start.43 = (bf16[2,192,1024]{2,1,0:T(8,128)(2,1)}, bf16[2,192,1024]{2,1,0:T(8,128)(2,1)}, u32[]{:S(2)}, u32[]{:S(2)}) collective-permute-start(bf16[2,192,1024]{2,1,0:T(8,128)(2,1)} %pad_maximum_fusion.27), channel_id=1, source_target_pairs={{0,8},{4,12},{8,0},{12,4},{16,24},{20,28},{24,16},{28,20},{1,9},{5... | collective-permute-start | bytes 2359304 | tf_op jit(solution)/shard_map/ppermute | solution.py:17
  1398.5 112.7 %collective-permute-start.40 = (bf16[2,192,1024]{2,1,0:T(8,128)(2,1)}, bf16[2,192,1024]{2,1,0:T(8,128)(2,1)}, u32[]{:S(2)}, u32[]{:S(2)}) collective-permute-start(bf16[2,192,1024]{2,1,0:T(8,128)(2,1)} %pad_maximum_fusion.26), channel_id=1, source_target_pairs={{0,16},{4,20},{8,24},{12,28},{16,0},{20,4},{24,8},{28,12},{1,17},{... | collective-permute-start | bytes 2359304 | tf_op jit(solution)/shard_map/ppermute | solution.py:17
  1454.4 78.1 %collective-permute-start.37 = (bf16[2,8,64,768]{3,2,1,0:T(8,128)(2,1)}, bf16[2,8,64,768]{3,2,1,0:T(8,128)(2,1)}, u32[]{:S(2)}, u32[]{:S(2)}) collective-permute-start(bf16[2,8,64,768]{3,2,1,0:T(8,128)(2,1)} %fusion.63), channel_id=1, source_target_pairs={{0,1},{1,0},{2,3},{3,2},{4,5},{5,4},{6,7},{7,6},{8,9},{9,8},{10,11... | collective-permute-start | bytes 4718600 | tf_op jit(solution)/shard_map/ppermute | solution.py:17
  1486.5 133.3 %all-to-all-start.28 = ((bf16[4,512,1024]{2,1,0:T(8,128)(2,1)}), bf16[4,512,1024]{2,1,0:T(8,128)(2,1)}, u32[]{:S(2)}, u32[]{:S(2)}) async-start(bf16[4,512,1024]{2,1,0:T(8,128)(2,1)} %bitcast.752), calls=%async_computation.28 | async-start | bytes 8388608 | tf_op jit(solution)/shard_map/all_to_all | solution.py:90
  1511.2 171.7 %collective-permute-start.21 = (bf16[192,2048]{1,0:T(8,128)(2,1)}, bf16[192,2048]{1,0:T(8,128)(2,1)}, u32[]{:S(2)}, u32[]{:S(2)}) collective-permute-start(bf16[192,2048]{1,0:T(8,128)(2,1)} %add_convert_fusion.3), channel_id=1, source_target_pairs={{0,2},{1,3},{2,0},{3,1},{4,6},{5,7},{6,4},{7,5},{8,10},{9,11},{10,... | collective-permute-start | bytes 2359304 | tf_op jit(solution)/shard_map/ppermute | solution.py:17
  1540.4 110.2 %collective-permute-start.38 = (bf16[8,64,768]{2,1,0:T(8,128)(2,1)}, bf16[8,64,768]{2,1,0:T(8,128)(2,1)}, u32[]{:S(2)}, u32[]{:S(2)}) collective-permute-start(bf16[8,64,768]{2,1,0:T(8,128)(2,1)} %fusion.84), channel_id=1, source_target_pairs={{0,2},{1,3},{2,0},{3,1},{4,6},{5,7},{6,4},{7,5},{8,10},{9,11},{10,... | collective-permute-start | bytes 2359304 | tf_op jit(solution)/shard_map/ppermute | solution.py:17
  1542.8 83.8 %collective-permute-start.32 = (bf16[2,192,1024]{2,1,0:T(8,128)(2,1)}, bf16[2,192,1024]{2,1,0:T(8,128)(2,1)}, u32[]{:S(2)}, u32[]{:S(2)}) collective-permute-start(bf16[2,192,1024]{2,1,0:T(8,128)(2,1)} %fusion.82), channel_id=1, source_target_pairs={{0,8},{4,12},{8,0},{12,4},{16,24},{20,28},{24,16},{28,20},{1,9},{5... | collective-permute-start | bytes 2359304 | tf_op jit(solution)/shard_map/ppermute | solution.py:17
  1545.1 83.8 %collective-permute-start.35 = (bf16[2,192,1024]{2,1,0:T(8,128)(2,1)}, bf16[2,192,1024]{2,1,0:T(8,128)(2,1)}, u32[]{:S(2)}, u32[]{:S(2)}) collective-permute-start(bf16[2,192,1024]{2,1,0:T(8,128)(2,1)} %fusion.83), channel_id=1, source_target_pairs={{0,16},{4,20},{8,24},{12,28},{16,0},{20,4},{24,8},{28,12},{1,17},{... | collective-permute-start | bytes 2359304 | tf_op jit(solution)/shard_map/ppermute | solution.py:17
  1626.6 35.0 %collective-permute-start.45 = (bf16[2,64,2048]{2,1,0:T(8,128)(2,1)S(1)}, bf16[2,64,2048]{2,1,0:T(8,128)(2,1)S(1)}, u32[]{:S(2)}, u32[]{:S(2)}) collective-permute-start(bf16[2,64,2048]{2,1,0:T(8,128)(2,1)S(1)} %copy-done.109), channel_id=1, source_target_pairs={{0,1},{1,0},{2,3},{3,2},{4,5},{5,4},{6,7},{7,6},{8,9},{9,8},{10,11... | collective-permute-start | bytes 1572872 | tf_op jit(solution)/shard_map/ppermute | solution.py:17
  1628.9 33.8 %collective-permute-start.33 = (bf16[192,1024]{1,0:T(8,128)(2,1)S(1)}, bf16[192,1024]{1,0:T(8,128)(2,1)S(1)}, u32[]{:S(2)}, u32[]{:S(2)}) collective-permute-start(bf16[192,1024]{1,0:T(8,128)(2,1)S(1)} %fusion.133), channel_id=1, source_target_pairs={{0,16},{4,20},{8,24},{12,28},{16,0},{20,4},{24,8},{28,12},{1,17},{... | collective-permute-start | bytes 1179656 | tf_op jit(solution)/shard_map/ppermute | solution.py:17
  (213 other events, 3274.4 us)

commit v2 on v1

--- a/solution.py
+++ b/solution.py
@@ -1,6 +1,12 @@
+import functools
+import math
+
 import jax
 import jax.numpy as jnp
+import numpy as np
 from jax import lax
+from jax.experimental import pallas as pl
+from jax.experimental.pallas import tpu as pltpu
 from jax.sharding import PartitionSpec as P
 
 HEADS = 16
@@ -41,6 +47,20 @@
     one = doubled(x[..., :half], "ctx", far + bits[:1])
     two = doubled(x[..., half:], "ctx", far[::-1] + bits[:1])
     return jnp.concatenate([one, two], axis=-1)
+
+
+def everywhere(x):
+    x = doubled(x, "fsdp", bits_of("fsdp")[::-1])
+    return doubled(x, "ctx", bits_of("ctx"))
+
+
+def spread(x):
+    index = lax.axis_index("fsdp")
+    out = x
+    for step in range(1, x.shape[0]):
+        piece = lax.dynamic_index_in_dim(x, index ^ step, 0, True)
+        out = lax.dynamic_update_slice_in_dim(out, swap(piece, "fsdp", step), index ^ step, 0)
+    return out
 
 
 def halved(x, axis, bits):
@@ -145,6 +165,463 @@
     x = x.reshape((2 * ctx_count, -1) + x.shape[1:])
     x = jnp.stack([x[:ctx_count], x[ctx_count:][::-1]], axis=1)
     return x.reshape((-1,) + x.shape[3:])
+
+
+def bits_down(count):
+    return [1 << i for i in range(count.bit_length() - 1)][::-1]
+
+
+class Links:
+    def __init__(self, sends, recvs, locals_):
+        self.sends, self.recvs, self.locals = sends, recvs, locals_
+        self.count = self.local_count = 0
+        self.open = {}
+        self.seen = {}
+
+    def send(self, src, dst, **to):
+        copy = pltpu.make_async_remote_copy(
+            src_ref=src,
+            dst_ref=dst,
+            send_sem=self.sends.at[self.count],
+            recv_sem=self.recvs.at[self.count],
+            device_id=to,
+            device_id_type=pl.DeviceIdType.MESH,
+        )
+        self.count += 1
+        copy.start()
+        self.open[id(copy)] = (copy, True)
+        return copy
+
+    def move(self, src, dst):
+        copy = pltpu.make_async_copy(src, dst, self.locals.at[self.local_count])
+        self.local_count += 1
+        copy.start()
+        self.open[id(copy)] = (copy, False)
+        return copy
+
+    def left(self, copy):
+        if id(copy) in self.open:
+            copy, remote = self.open.pop(id(copy))
+            self.seen[id(copy), "left"] = copy
+            copy.wait_send() if remote else copy.wait()
+
+    def arrived(self, copy):
+        if (id(copy), "in") not in self.seen:
+            self.seen[id(copy), "in"] = copy
+            copy.wait_recv()
+
+    def close(self):
+        for copy, _ in list(self.open.values()):
+            self.left(copy)
+
+
+def greet(c, z, nc, nz):
+    barrier = pltpu.get_barrier_semaphore()
+    for d in range(1, nc):
+        pl.semaphore_signal(
+            barrier, inc=1, device_id={"ctx": c ^ d}, device_id_type=pl.DeviceIdType.MESH
+        )
+    for s in range(1, nz):
+        pl.semaphore_signal(
+            barrier, inc=1, device_id={"fsdp": z ^ s}, device_id_type=pl.DeviceIdType.MESH
+        )
+    pl.semaphore_wait(barrier, nc - 1 + nz - 1)
+
+
+def kdot(left, right, dims=((1,), (0,)), precision=None):
+    return lax.dot_general(
+        left, right, (dims, ((), ())), preferred_element_type=exact, precision=precision
+    )
+
+
+def slots_of(cfg, mask_rows, upper):
+    rank = kdot(mask_rows.astype(low), upper)
+    return jnp.where(mask_rows > 0, rank, 0.0)
+
+
+def plane_ranks(cfg, routes, z):
+    nc, tokens = cfg["nc"], cfg["tokens"]
+    expert = lax.broadcasted_iota(jnp.int32, (nc, tokens), 0) * cfg["exp_local"] + z // cfg["split"]
+    mask = jnp.zeros((nc, tokens), exact)
+    for k in range(cfg["top"]):
+        mask = jnp.where(routes[k : k + 1, :] == expert, 1.0, mask)
+    upper = jnp.where(
+        lax.broadcasted_iota(jnp.int32, (tokens, tokens), 0)
+        <= lax.broadcasted_iota(jnp.int32, (tokens, tokens), 1),
+        1.0,
+        0.0,
+    ).astype(low)
+    return slots_of(cfg, mask, upper)
+
+
+def fill_hot(cfg, ranks, hot_ref):
+    cap, tokens = cfg["cap"], cfg["tokens"]
+    number = lax.broadcasted_iota(jnp.int32, (cap, tokens), 0).astype(exact) + 1.0
+    for k in range(cfg["nc"]):
+        hit = jnp.where(ranks[k : k + 1, :] == number, 1.0, 0.0)
+        hot_ref[k * cap : (k + 1) * cap, :] = hit.astype(low)
+
+
+def front_kernel(
+    cfg,
+    x_ref, wq_ref, wk_ref, wv_ref, wo_ref, gt_ref, rt_ref, ro_ref, cot_ref, gp_ref, up_ref, cos_ref, sin_ref,
+    a1_out, w_full, raw_out, stat_out, rot_out, ob_out, wo_full, r1_out, a2_out, r_all, g_all, t_all,
+    gate_full, up_full, cot_rows, cot_near,
+    xbuf, wbuf, obw, gbuf, gfull, rbuf, tbuf, raw, stat, total, rq, rk, rot, opos, odev, orecv, r1, a2, cbuf, hot, cs,
+    sends, recvs, locals_,
+):
+    nc, nz, tokens, width = cfg["nc"], cfg["nz"], cfg["tokens"], cfg["width"]
+    cols, rows_w, length, cap = cfg["cols"], cfg["rows_w"], cfg["length"], cfg["cap"]
+    hs = 128
+    heads = cols // hs
+    half = tokens // 2
+    block = cfg["block"]
+    blocks = length // block
+    c, z = lax.axis_index("ctx"), lax.axis_index("fsdp")
+    links = Links(sends, recvs, locals_)
+    ds = pl.ds
+    same = [d for d in range(2, nc, 2)]
+
+    own = []
+    own.append(links.move(x_ref, xbuf.at[ds(c * tokens, tokens)]))
+    for j, ref in enumerate((wq_ref, wk_ref, wv_ref)):
+        at = pl.multiple_of(c * cols, 128)
+        own.append(links.move(ref.at[:, ds(at, cols)], wbuf.at[j, c, z]))
+    own.append(links.move(wo_ref, obw.at[c, z]))
+    own.append(links.move(gt_ref, gbuf.at[c, z]))
+    own.append(links.move(rt_ref, rbuf.at[c, z]))
+    own.append(links.move(ro_ref, tbuf.at[c, z]))
+    own.append(links.move(cot_ref, cbuf.at[0]))
+    mine = links.move(gp_ref.at[z], gate_full.at[z])
+    mine_up = links.move(up_ref.at[z], up_full.at[z])
+    greet(c, z, nc, nz)
+
+    slices = []
+    for d in range(1, nc):
+        peer = c ^ d
+        at = pl.multiple_of(peer * cols, 128)
+        for j, ref in enumerate((wq_ref, wk_ref, wv_ref)):
+            slices.append(links.send(ref.at[:, ds(at, cols)], wbuf.at[j, c, z], ctx=peer))
+    small_z = []
+    for s in range(1, nz):
+        for src, dst in ((gt_ref, gbuf), (rt_ref, rbuf), (ro_ref, tbuf)):
+            small_z.append(links.send(src, dst.at[c, z], fsdp=z ^ s))
+    x_at = xbuf.at[ds(c * tokens, tokens)]
+    x_same = {d: links.send(x_ref, x_at, ctx=c ^ d) for d in same}
+    x_side = [links.send(x_ref, x_at, ctx=c ^ 1)]
+    for copy in own:
+        links.left(copy)
+
+    for copy in slices:
+        links.arrived(copy)
+    w_near = {}
+
+    def w_send(s, bit):
+        place = wbuf.at[:, :, z ^ s]
+        w_near[s | bit] = links.send(place, place, fsdp=z ^ bit)
+
+    steps = bits_down(nz)
+    for bit in steps:
+        w_send(0, bit)
+    wo_near, cot_copies = {}, {}
+
+    def wo_send(s, bit):
+        place = obw.at[c, z ^ s]
+        wo_near[s | bit] = links.send(place, place, fsdp=z ^ bit)
+
+    def cot_send(s, bit):
+        cot_copies[s | bit] = links.send(cbuf.at[s], cbuf.at[s | bit], fsdp=z ^ bit)
+
+    for copy in small_z:
+        links.arrived(copy)
+    small_c = []
+    for d in range(1, nc):
+        for buf in (gbuf, rbuf, tbuf):
+            small_c.append(links.send(buf.at[c], buf.at[c], ctx=c ^ d))
+    for d in same:
+        links.arrived(x_same[d])
+        place = xbuf.at[ds((c ^ d) * tokens, tokens)]
+        x_side.append(links.send(place, place, ctx=c ^ 1))
+
+    def forward(waits, send):
+        for at, bit in enumerate(steps):
+            held = [0]
+            for earlier in steps[:at]:
+                held += [s | earlier for s in held]
+            for s in held[1:]:
+                links.arrived(waits[s])
+                send(s, bit)
+
+    forward(w_near, w_send)
+    for bit in steps:
+        wo_send(0, bit)
+    for bit in steps:
+        cot_send(0, bit)
+    for copy in small_c:
+        links.arrived(copy)
+    per = 128 // rows_w
+    groups = nz // per
+    for k in range(nc):
+        for g in range(groups):
+            tile = gbuf[k, g * per]
+            for p in range(1, per):
+                tile = tile + gbuf[k, g * per + p]
+            at = (k * groups + g) * 128
+            gfull[:, at : at + 128] = tile
+    for copy in x_side:
+        links.arrived(copy)
+    for copy in list(x_same.values()) + x_side:
+        links.left(copy)
+
+    chunk = cfg["chunk"]
+
+    def norm_rows(i, _):
+        at = pl.multiple_of(i * chunk, chunk)
+        v = xbuf[ds(at, chunk), :].astype(exact)
+        v = v * lax.rsqrt(jnp.mean(v * v, axis=-1, keepdims=True) + epsilon) * gfull[0:1, :]
+        xbuf[ds(at, chunk), :] = v.astype(low)
+        return 0
+
+    lax.fori_loop(0, length // chunk, norm_rows, 0)
+    a1_copy = links.move(xbuf, a1_out)
+
+    last = steps[-1]
+    for s in range(1, nz):
+        if s & last:
+            links.arrived(w_near[s])
+    experts_in = []
+    for s in range(1, nz):
+        experts_in.append(links.send(gp_ref.at[z ^ s], gate_full.at[z], fsdp=z ^ s))
+    if cfg["carry_up"]:
+        for s in range(1, nz):
+            experts_in.append(links.send(up_ref.at[z ^ s], up_full.at[z], fsdp=z ^ s))
+    w_copy = links.move(wbuf, w_full)
+
+    one_row = lax.broadcasted_iota(jnp.int32, (8, cols), 0)
+    pick_q = jnp.where(one_row == 0, 1.0, 0.0)
+    pick_k = jnp.where(one_row == 1, 1.0, 0.0)
+    best = lax.Precision.HIGHEST
+
+    def project(i, _):
+        at = pl.multiple_of(i * block, block)
+        rows = xbuf[ds(at, block), :]
+        sums = jnp.zeros((8, block), exact)
+        for j in range(3):
+            weight = wbuf[j].reshape(width, cols)
+            v = kdot(rows, weight)
+            raw[ds(at, block), j * cols : (j + 1) * cols] = v
+            if j < 2:
+                sums += kdot(pick_k if j else pick_q, v * v, ((1,), (1,)), best)
+        stat[c, :, ds(at, block)] = sums
+        return 0
+
+    lax.fori_loop(0, blocks, project, 0)
+    raw_copy = links.move(raw, raw_out)
+    stats = [links.send(stat.at[c], stat.at[c], ctx=c ^ d) for d in range(1, nc)]
+    forward(wo_near, wo_send)
+    for s in range(1, nz):
+        if s & last:
+            links.arrived(wo_near[s])
+    wo_same = {d: links.send(obw.at[c], obw.at[c], ctx=c ^ d) for d in same}
+    wo_side = [links.send(obw.at[c], obw.at[c], ctx=c ^ 1)]
+    for copy in stats:
+        links.arrived(copy)
+    summed = stat[0]
+    for k in range(1, nc):
+        summed += stat[k]
+    total[...] = summed
+    row8 = lax.broadcasted_iota(jnp.int32, (8, hs), 0)
+
+    def columns(i, _):
+        at = pl.multiple_of(i * block, block)
+        part = total[:, ds(at, block)]
+        for row, dst in ((0, rq), (1, rk)):
+            sel = jnp.where(row8 == row, 1.0, 0.0)
+            ms = kdot(part, sel, ((0,), (0,)), best)
+            dst[ds(at, block), :] = lax.rsqrt(ms / width + epsilon)
+        return 0
+
+    lax.fori_loop(0, blocks, columns, 0)
+    stat_copy = links.move(total, stat_out)
+
+    def turn(i, _):
+        d, side = i // 2, i % 2
+        at = pl.multiple_of(d * tokens + side * half, half)
+        to = pl.multiple_of(jnp.where(side == 0, d, 2 * nc - 1 - d) * half, half)
+        cosine, sine = cos_ref[ds(at, half), :], sin_ref[ds(at, half), :]
+        for h in range(heads):
+            for j, scale in ((0, rq), (1, rk)):
+                lane = j * cols + h * hs
+                gain = gfull[1 + j : 2 + j, ds(pl.multiple_of(c * cols + h * hs, hs), hs)]
+                v = raw[ds(at, half), lane : lane + hs] * scale[ds(at, half), :] * gain
+                v = v * cosine + pltpu.roll(v, hs // 2, 1) * sine
+                rot[j, ds(to, half), h * hs : (h + 1) * hs] = v.astype(low)
+        rot[2, ds(to, half), :] = raw[ds(at, half), 2 * cols : 3 * cols].astype(low)
+        return 0
+
+    lax.fori_loop(0, 2 * nc, turn, 0)
+    rot_copy = links.move(rot, rot_out)
+    forward(cot_copies, cot_send)
+
+    scale = hs ** -0.5
+    for h in range(heads):
+        lanes = slice(h * hs, (h + 1) * hs)
+        for i in range(blocks):
+            count = (i + 1) * block
+            q = rot[0, i * block : count, lanes]
+            s = kdot(q, rot[1, :count, lanes], ((1,), (1,))) * scale
+            row = lax.broadcasted_iota(jnp.int32, (block, count), 0) + i * block
+            col = lax.broadcasted_iota(jnp.int32, (block, count), 1)
+            s = jnp.where(col <= row, s, neg_large)
+            p = jnp.exp(s - jnp.max(s, axis=-1, keepdims=True))
+            p = p * (1.0 / jnp.sum(p, axis=-1, keepdims=True))
+            opos[i * block : count, lanes] = kdot(p.astype(low), rot[2, :count, lanes]).astype(low)
+
+    def place(i, _):
+        d, side = i // 2, i % 2
+        to = pl.multiple_of(d * tokens + side * half, half)
+        at = pl.multiple_of(jnp.where(side == 0, d, 2 * nc - 1 - d) * half, half)
+        odev[ds(to, half), :] = opos[ds(at, half), :]
+        return 0
+
+    lax.fori_loop(0, 2 * nc, place, 0)
+    ob_copy = links.move(odev, ob_out)
+    mixed = []
+    for d in range(1, nc):
+        src = odev.at[ds((c ^ d) * tokens, tokens)]
+        mixed.append(links.send(src, orecv.at[c], ctx=c ^ d))
+    own_mixed = links.move(odev.at[ds(c * tokens, tokens)], orecv.at[c])
+    for d in same:
+        links.arrived(wo_same[d])
+        place_at = obw.at[c ^ d]
+        wo_side.append(links.send(place_at, place_at, ctx=c ^ 1))
+
+    for s in range(1, nz):
+        if s & last:
+            links.arrived(cot_copies[s])
+    near_copy = links.move(cbuf, cot_near)
+    rows_sent = []
+    slot_busy = [[], []]
+    for s in range(nz):
+        slot = s % 2
+        for copy in slot_busy[slot]:
+            links.left(copy)
+        fill_hot(cfg, plane_ranks(cfg, tbuf[c, z ^ s], z), hot)
+        cs[slot] = kdot(hot[...], cbuf[s]).astype(low)
+        busy = []
+        for d in range(1, nc):
+            src = cs.at[slot, ds((c ^ d) * cap, cap)]
+            copy = links.send(src, cot_rows.at[s, c], ctx=c ^ d)
+            rows_sent.append(copy)
+            busy.append(copy)
+        busy.append(links.move(cs.at[slot, ds(c * cap, cap)], cot_rows.at[s, c]))
+        slot_busy[slot] = busy
+
+    for copy in wo_side:
+        links.arrived(copy)
+    wo_copy = links.move(obw, wo_full)
+    for copy in mixed:
+        links.arrived(copy)
+    links.left(own_mixed)
+    r1[...] = jnp.zeros_like(r1)
+
+    def mix(k, _):
+        r1[...] += kdot(orecv[k], obw[k].reshape(cols, width))
+        return 0
+
+    lax.fori_loop(0, nc, mix, 0)
+    xin = links.move(x_ref, a2)
+    links.left(xin)
+    v = r1[...] + a2[...].astype(exact)
+    r1[...] = v
+    n2 = v * lax.rsqrt(jnp.mean(v * v, axis=-1, keepdims=True) + epsilon)
+    a2[...] = (n2 * gfull[3:4, :]).astype(low)
+    links.move(r1, r1_out)
+    links.move(a2, a2_out)
+    links.move(rbuf, r_all)
+    links.move(gfull, g_all)
+    links.move(tbuf, t_all)
+    for copy in experts_in + rows_sent:
+        links.arrived(copy)
+    links.close()
+
+
+def front(cfg, x, w_query, w_key, w_value, w_out, gains, router, routes, cot, gate_pieces, up_pieces, cosine, sine):
+    nc, nz, tokens, width = cfg["nc"], cfg["nz"], cfg["tokens"], cfg["width"]
+    cols, rows_w, length, cap = cfg["cols"], cfg["rows_w"], cfg["length"], cfg["cap"]
+    rows, part = gate_pieces.shape[1:]
+    shape = jax.ShapeDtypeStruct
+    any_, vmem = pl.BlockSpec(memory_space=pl.ANY), pl.BlockSpec(memory_space=pltpu.VMEM)
+    top_rows = routes.shape[0]
+    outs = [
+        shape((length, width), low),
+        shape((3, nc, nz, rows_w, cols), low),
+        shape((length, 3 * cols), exact),
+        shape((8, length), exact),
+        shape((3, length, cols), low),
+        shape((length, cols), low),
+        shape((nc, nz, rows_w, width), low),
+        shape((tokens, width), exact),
+        shape((tokens, width), low),
+        shape((nc, nz, rows_w, 128), low),
+        shape((8, width), exact),
+        shape((nc, nz, top_rows, tokens), jnp.int32),
+        shape((nz, rows, part), low),
+        shape((nz, rows, part), low),
+        shape((nz, nc, cap, width), low),
+        shape((nz, tokens, width), low),
+    ]
+    scratch = [
+        pltpu.VMEM((length, width), low),
+        pltpu.VMEM((3, nc, nz, rows_w, cols), low),
+        pltpu.VMEM((nc, nz, rows_w, width), low),
+        pltpu.VMEM((nc, nz, 8, 128), exact),
+        pltpu.VMEM((8, width), exact),
+        pltpu.VMEM((nc, nz, rows_w, 128), low),
+        pltpu.VMEM((nc, nz, top_rows, tokens), jnp.int32),
+        pltpu.VMEM((length, 3 * cols), exact),
+        pltpu.VMEM((nc, 8, length), exact),
+        pltpu.VMEM((8, length), exact),
+        pltpu.VMEM((length, 128), exact),
+        pltpu.VMEM((length, 128), exact),
+        pltpu.VMEM((3, length, cols), low),
+        pltpu.VMEM((length, cols), low),
+        pltpu.VMEM((length, cols), low),
+        pltpu.VMEM((nc, tokens, cols), low),
+        pltpu.VMEM((tokens, width), exact),
+        pltpu.VMEM((tokens, width), low),
+        pltpu.VMEM((nz, tokens, width), low),
+        pltpu.VMEM((nc * cap, tokens), low),
+        pltpu.VMEM((2, nc * cap, width), low),
+        pltpu.SemaphoreType.DMA((cfg["copies"],)),
+        pltpu.SemaphoreType.DMA((cfg["copies"],)),
+        pltpu.SemaphoreType.DMA((64,)),
+    ]
+    return pl.pallas_call(
+        functools.partial(front_kernel, cfg),
+        out_shape=outs,
+        in_specs=[any_] * 11 + [vmem] * 2,
+        out_specs=[any_] * len(outs),
+        scratch_shapes=scratch,
+        compiler_params=pltpu.CompilerParams(
+            collective_id=0, has_side_effects=True, vmem_limit_bytes=cfg["vmem"]
+        ),
+        name="front",
+    )(x, w_query, w_key, w_value, w_out, gains, router, routes, cot, gate_pieces, up_pieces, cosine, sine)
+
+
+def tables(nc, tokens, head_size):
+    half = tokens // 2
+    local = np.arange(tokens)
+    device = np.arange(nc)[:, None]
+    position = np.where(
+        local < half, device * half + local, (2 * nc - 1 - device) * half + local - half
+    ).reshape(-1)
+    freq = np.float32(10000.0) ** (-np.arange(head_size // 2, dtype=np.float32) * (2.0 / head_size))
+    angle = position.astype(np.float32)[:, None] * freq.astype(np.float32)
+    cosine = np.concatenate([np.cos(angle), np.cos(angle)], axis=1)
+    sine = np.concatenate([-np.sin(angle), np.sin(angle)], axis=1)
+    return jnp.asarray(cosine, exact), jnp.asarray(sine, exact)
 
 
 def body(
@@ -185,28 +662,58 @@
     z_index = lax.axis_index("fsdp")
     rows_w = w_query.shape[0]
 
-    qkv = jnp.stack([w_query, w_key, w_value], axis=1).reshape(rows_w, 3, ctx_count, cols)
-    qkv = exchange(qkv.transpose(2, 0, 1, 3), "ctx")
-    qkv = doubled(qkv, "fsdp", bits_of("fsdp")[::-1])
-    qkv = qkv.transpose(1, 0, 2, 3, 4).reshape(width, 3 * cols)
-    gains = jnp.stack([attn_gain, query_gain, key_gain, ffn_gain])
-    small = jnp.concatenate([gains.reshape(-1), w_router.reshape(-1)])
-    small = exchange(
-        jnp.broadcast_to(small[None], (ctx_count * z_count, small.shape[0])), both
-    )
-    gains = small[:, : 4 * rows_w].reshape(-1, 4, rows_w).transpose(1, 0, 2).reshape(4, width)
-    router_full = small[:, 4 * rows_w :].reshape(width, experts)
-    gains = gains.astype(exact)
-    attn_scale, query_scale, key_scale, ffn_scale = gains[0], gains[1], gains[2], gains[3]
-    query_scale = lax.dynamic_slice_in_dim(query_scale, c_index * cols, cols)
-    key_scale = lax.dynamic_slice_in_dim(key_scale, c_index * cols, cols)
-
-    x_all = gather_ctx(hidden_in[0]).reshape(length, width)
-    attn_all = rms_apply(x_all.astype(exact), attn_scale)[0].astype(low)
-
-    routes_all = lax.all_gather(routes[0], both, axis=0)
+    cfg = dict(
+        nc=ctx_count,
+        nz=z_count,
+        tokens=tokens,
+        width=width,
+        cols=cols,
+        rows_w=rows_w,
+        length=length,
+        cap=capacity,
+        top=top,
+        exp_local=exp_local,
+        split=split,
+        block=math.gcd(length, 256),
+        chunk=math.gcd(length, 64),
+        copies=(ctx_count - 1) * (8 + z_count) + (z_count - 1) * 8 + 2 * ctx_count + 8,
+        carry_up=True,
+        vmem=60 * 2**20,
+    )
+    index = c_index * z_count + z_index
+    per = 128 // rows_w
+    gains = jnp.stack([attn_gain, query_gain, key_gain, ffn_gain]).astype(exact)
+    gains = lax.dynamic_update_slice(
+        jnp.zeros((8, 128), exact), gains, (0, jnp.mod(index, per) * rows_w)
+    )
+    router_tile = jnp.pad(w_router, ((0, 0), (0, 128 - experts)))
+    route_tile = jnp.pad(routes[0].T, ((0, 8 - top), (0, 0)), constant_values=-1)
+
+    def pieces_of(weight):
+        rows = weight.shape[1]
+        weight = weight.reshape(exp_local, rows, z_count, split, part // z_count)
+        return weight.transpose(0, 3, 1, 2, 4).reshape(z_count, rows, part)
+
+    (
+        attn_all, w_full, raw, squares, rot, out_heads, wo_full, resid_one, ffn_input,
+        router_full, gains, routes_all, gate_full, up_full, cot_rows, cot_near,
+    ) = front(
+        cfg, hidden_in[0], w_query, w_key, w_value, w_out, gains, router_tile, route_tile,
+        cotangent[0], pieces_of(w_gate), pieces_of(w_up), *tables(ctx_count, tokens, head_size),
+    )
+    gate_full = gate_full.reshape(-1, part)
+    up_full = up_full.reshape(-1, part)
+    w_full = w_full.reshape(3, width, cols)
+    out_full = wo_full.reshape(width, width)
+    router_full = router_full.reshape(width, 128)[:, :experts]
+    cot_rows = cot_rows.reshape(-1, width)
+    attn_scale, ffn_scale = gains[0], gains[3]
+    query_scale = lax.dynamic_slice_in_dim(gains[1], c_index * cols, cols)
+    key_scale = lax.dynamic_slice_in_dim(gains[2], c_index * cols, cols)
+    routes_all = routes_all[:, :, :top].swapaxes(2, 3)
+
     multi_all = jnp.sum(
-        (routes_all[..., None] == jnp.arange(experts, dtype=jnp.int32)).astype(exact), axis=2
+        (routes_all[..., None] == jnp.arange(experts, dtype=jnp.int32)).astype(exact), axis=-2
     ).reshape(ctx_count, z_count, tokens, experts)
     own_expert = c_index * exp_local + z_index // split
     lower = (
@@ -241,36 +748,16 @@
         rows = jnp.einsum("crt,td->crd", hot, block, preferred_element_type=exact)
         return rows.astype(low)
 
-    cot_near = near_first(cotangent[0])
-    cot_sent = [pick(hot, block) for hot, block in zip(sends, cot_near)]
-    cot_rows = jnp.stack([exchange(rows, "ctx") for rows in cot_sent]).reshape(-1, width)
-
-    def whole_in(weight):
-        rows = weight.shape[1]
-        weight = weight.reshape(exp_local, rows, z_count, split, part // z_count)
-        weight = weight.transpose(0, 3, 1, 2, 4).reshape(z_count, rows, part)
-        return exchange(weight, "fsdp").reshape(z_count * rows, part)
-
-    gate_full = whole_in(w_gate)
-    up_full = whole_in(w_up)
+    cot_sent = [pick(hot, cot_near[step]) for step, hot in enumerate(sends)]
     rows_d = w_down.shape[1]
-    down_full = exchange(
-        w_down.reshape(z_count, rows_d // split, width), "fsdp"
-    ).reshape(part, width)
-
-    projected = dot(attn_all, qkv)
-    queries, keys, values = (
-        projected[:, :cols],
-        projected[:, cols : 2 * cols],
-        projected[:, 2 * cols :],
-    )
+    down_full = spread(w_down.reshape(z_count, rows_d // split, width)).reshape(part, width)
 
     def total_over_ctx(one, two):
         both_sums = jnp.stack([one, two])
         return jnp.sum(lax.all_gather(both_sums, "ctx", axis=0), axis=0)
 
-    squares = total_over_ctx(jnp.sum(queries * queries, -1), jnp.sum(keys * keys, -1))
-    rms_two = lax.rsqrt(squares / width + epsilon)
+    queries, keys = raw[:, :cols], raw[:, cols : 2 * cols]
+    rms_two = lax.rsqrt(squares[:2] / width + epsilon)
     query_rms, key_rms = rms_two[0][:, None], rms_two[1][:, None]
     query_normed, key_normed = queries * query_rms, keys * key_rms
     half = tokens // 2
@@ -284,9 +771,7 @@
     def by_head(x):
         return x.reshape(length, heads, head_size)
 
-    query_rot = ordered(rotate(by_head(query_normed * query_scale), cosine, sine).astype(low), ctx_count)
-    key_rot = ordered(rotate(by_head(key_normed * key_scale), cosine, sine).astype(low), ctx_count)
-    value_low = ordered(by_head(values.astype(low)), ctx_count)
+    query_rot, key_rot, value_low = by_head(rot[0]), by_head(rot[1]), by_head(rot[2])
     allowed = (row[None, :] <= row[:, None])[None]
     scores = (
         jnp.einsum("qhd,khd->hqk", query_rot, key_rot, preferred_element_type=exact) * scale
@@ -295,16 +780,9 @@
     log_total = jax.nn.logsumexp(scores, axis=-1, keepdims=True)
     probs = jnp.exp(scores - log_total)
     probs_low = probs.astype(low)
-    mixed = jnp.einsum("hqk,khd->qhd", probs_low, value_low, preferred_element_type=exact)
-    out_heads = placed(mixed.astype(low).reshape(length, cols), ctx_count)
-    out_low = exchange(out_heads.reshape(ctx_count, tokens, cols), "ctx")
-    out_low = out_low.transpose(1, 0, 2).reshape(tokens, width)
-    out_full = doubled(w_out, "fsdp", bits_of("fsdp")[::-1]).reshape(cols, width)
-    out_full = gather_ctx(out_full).reshape(width, width)
     rows_in = hidden_in[0].astype(exact)
-    resid_one = rows_in + dot(out_low, out_full)
-    hidden_two, normed_two, scale_two = rms_apply(resid_one, ffn_scale)
-    ffn_input = hidden_two.astype(low)
+    scale_two = lax.rsqrt(jnp.mean(resid_one * resid_one, axis=-1, keepdims=True) + epsilon)
+    normed_two = resid_one * scale_two
 
     input_near = near_first(ffn_input)
     input_rows = jnp.stack(
@@ -340,12 +818,12 @@
 
     def whole_out(grad):
         rows = grad.shape[0] // z_count
-        grad = exchange(grad.reshape(z_count, rows, part), "fsdp")
+        grad = spread(grad.reshape(z_count, rows, part))
         grad = grad.reshape(exp_local, split, rows, z_count, part // z_count)
         return grad.transpose(0, 2, 3, 1, 4).reshape(exp_local, rows, hidden).astype(exact)
 
     grad_down = (
-        exchange(down_grad.reshape(z_count, rows_d // split, width), "fsdp")
+        spread(down_grad.reshape(z_count, rows_d // split, width))
         .reshape(exp_local, rows_d, width)
         .astype(exact)
     )
@@ -422,7 +900,11 @@
     query_grad_low = (query_rms * (query_d - query_normed * inner_two[0][:, None])).astype(low)
     key_grad_low = (key_rms * (key_d - key_normed * inner_two[1][:, None])).astype(low)
     qkv_grad_low = jnp.concatenate([query_grad_low, key_grad_low, value_grad_low], axis=1)
-    attn_input_grad = contract_cols(qkv_grad_low, qkv)
+    attn_input_grad = (
+        contract_cols(query_grad_low, w_full[0])
+        + contract_cols(key_grad_low, w_full[1])
+        + contract_cols(value_grad_low, w_full[2])
+    )
     qkv_weight_grad = contract_rows(attn_all, qkv_grad_low)
     attn_input_grad = scatter_ctx(attn_input_grad.reshape(ctx_count, tokens, width))
     _, normed_one, scale_one = rms_apply(rows_in, attn_scale)

time: 1720 us -> 1490 us (0.87)
  Pallas kernels: 0 us -> 379 us
  waiting for transfers between devices: 655 us -> 380 us
  blocking collectives: 233 us -> 8.22 us
  other arithmetic: 202 us -> 121 us
  local copies, waits for them, and re-layouts: 179 us -> 113 us
  starting transfers between devices: 165 us -> 220 us
    pallas_call x0 -> x1, Pallas kernels: none -> 379 us  [front(): pl.pallas_call(functools.partial(front_kernel, cfg), out_shape=outs, in_s...]
    all_to_all x26 -> x17, waiting for transfers between devices: 342 us -> 75.9 us  [exchange(): return lax.all_to_all(x, axis, split_axis=0, concat_axis=0, tiled=True)]
    all_to_all x4 -> x0, blocking collectives: 121 us -> none  [exchange(): return lax.all_to_all(x, axis, split_axis=0, concat_axis=0, tiled=True)]
    ppermute x47 -> x40, starting transfers between devices: 48.7 us -> 148 us  [swap(): return lax.ppermute(x, axis, [(i, i ^ bit) for i in range(length)])]
    all_gather x1 -> x0, blocking collectives: 92.9 us -> none  [body(): routes_all = lax.all_gather(routes[0], both, axis=0)]
    all_to_all x26 -> x17, starting transfers between devices: 117 us -> 72.2 us  [exchange(): return lax.all_to_all(x, axis, split_axis=0, concat_axis=0, tiled=True)]
    unnamed x406 -> x269, local copies, waits for them, and re-layouts: 54.7 us -> 26.2 us
    dynamic_slice x1 -> x9, local copies, waits for them, and re-layouts: 0.54 us -> 20.5 us  [the longest x8 19.9 us: spread(): piece = lax.dynamic_index_in_dim(x, index ^ step, 0, True)]
  transfers between devices with their start and end apart: 73 -> 57, of which waited for: 36 -> 21; matrix products, arithmetic and copies ran while one was open for 33% -> 25% of each run, Pallas kernels for 0% -> 0%
where the time goes in v2:
time: 1490 us; the launch traced here: 1480 us
  waiting for transfers between devices  380 us (26%)
  Pallas kernels  379 us (25%)
  matrix products  258 us (17%)
  starting transfers between devices  220 us (15%)
  other arithmetic  121 us (8%)
  local copies, waits for them, and re-layouts  113 us (8%)
    pallas_call x1, Pallas kernels, front(): pl.pallas_call(functools.partial(front_kernel, cfg), out_shape=outs, in_s...  379 us
    ppermute x40, waiting for transfers between devices, swap(): return lax.ppermute(x, axis, [(i, i ^ bit) for i in range(length)])  304 us
    ppermute x40, starting transfers between devices, swap(): return lax.ppermute(x, axis, [(i, i ^ bit) for i in range(length)])  148 us
    dot_general x8, matrix products, contract_cols(): lax.dot_general(left, right, (((1,), (1,)), ((), ())), preferred_element_...  80.4 us
    all_to_all x17, waiting for transfers between devices, exchange(): return lax.all_to_all(x, axis, split_axis=0, concat_axis=0, tiled=True)  75.9 us
    all_to_all x17, starting transfers between devices, exchange(): return lax.all_to_all(x, axis, split_axis=0, concat_axis=0, tiled=True)  72.2 us
    dot_general x6, matrix products, contract_rows(): lax.dot_general(left, right, (((0,), (0,)), ((), ())), preferred_element_...  49.2 us
    dot_general x8, matrix products, dot(): return jnp.dot(left, right, preferred_element_type=exact)  44.6 us
  transfers between devices with their start and end apart: 57, of which 21 were waited for; matrix products, arithmetic and copies ran while one was open for 25% of the time, Pallas kernels for 0%

profile of v2, /device:TPU:0, one launch (start us, length us, event | category | flops | bytes accessed | tf_op | source)
XLA Modules:
  0.0 1483.1 jit_solution(10971449726719462015)
XLA Ops:
  0.7 4.8 copy.458
  7.2 378.9 %front.1 = (bf16[1536,2048]{1,0:T(8,128)(2,1)}, bf16[3,8,4,64,256]{4,3,2,1,0:T(8,128)(2,1)}, f32[1536,768]{1,0:T(8,128)}, f32[8,1536]{1,0:T(8,128)}, bf16[3,1536...) custom-call(bf16[192,2048]{1,0:T(8,128)(2,1)} %bitcast.623, ...), custom_call_target="tpu_custom_call" | custom-call | tf_op jit(solution)/shard_map/front/pallas_call | solution.py:600
  386.2 27.3 %collective-permute-start.1 = (bf16[192,2048]{1,0:T(8,128)(2,1)}, bf16[192,2048]{1,0:T(8,128)(2,1)}, u32[]{:S(2)}, u32[]{:S(2)}) collective-permute-start(bf16[192,2048]{1,0:T(8,128)(2,1)} %get-tuple-element.32), channel_id=1, source_target_pairs={{0,2},{1,3},{2,0},{3,1},{4,6},{5,7},{6,4},{7,5},{8,10},{9,11},{10,... | collective-permute-start | bytes 2359304 | tf_op jit(solution)/shard_map/ppermute | solution.py:23
  422.6 5.2 all-to-all-start
  447.0 8.6 fusion.253
  464.0 8.8 exponential_reduce_fusion
  476.8 13.8 all-to-all-done.1
  510.5 9.6 collective-permute-done.2
  535.8 65.7 %collective-permute-done.4 = bf16[1,256,2048]{2,1,0:T(8,128)(2,1)S(1)} collective-permute-done((bf16[1,256,2048]{2,1,0:T(8,128)(2,1)}, bf16[1,256,2048]{2,1,0:T(8,128)(2,1)S(1)}, u32[]{:S(2)}, u32[]{:S(2)}) %collective-permute-start.4) | collective-permute-done | bytes 1048608 | tf_op jit(solution)/shard_map/ppermute | solution.py:23
  612.6 8.1 multiply_convert_fusion.1
  620.7 8.3 fusion
  629.0 14.6 fusion.258
  643.6 11.5 fusion.257
  655.1 23.4 %multiply_convert_fusion.2 = (bf16[2048,1024]{1,0:T(8,128)(2,1)}, bf16[2048,1024]{1,0:T(8,128)(2,1)}, bf16[2048,1024]{1,0:T(8,128)(2,1)}) fusion(f32[2048,1024]{1,0:T(8,128)} %fusion.257, f32[2048,1024]{1,0:T(8,128)} %fusion.258, bf16[2048,2048]{1,0:T(8,128)(2,1)} %bitcast.624, bf16[1024,2048]{1,0:T(8,128)(2,1)} %bitcast.619), kind=kOutput, calls=%fused_computation.15 | convolution fusion | flops 8621391872 | bytes 41943040 | tf_op jit(solution)/shard_map/dot_general | solution.py:153
  678.5 12.1 convolution_convert_fusion
  698.0 12.7 convolution_convert_fusion.1
  713.7 21.9 %collective-permute-start.37 = (bf16[1,256,2048]{2,1,0:T(8,128)(2,1)}, bf16[1,256,2048]{2,1,0:T(8,128)(2,1)}, u32[]{:S(2)}, u32[]{:S(2)}) collective-permute-start(bf16[1,256,2048]{2,1,0:T(8,128)(2,1)} %constant_dynamic-slice_fusion.2), channel_id=1, source_target_pairs={{0,1},{1,0},{2,3},{3,2},{4,5},{5,4},{6,7},{7,6},{8,9},{9,8},{10,11... | collective-permute-start | bytes 3145736 | tf_op jit(solution)/shard_map/ppermute | solution.py:23
  740.2 15.4 %fusion.259 = f32[2048,2048]{1,0:T(8,128)} fusion(bf16[2048,1024]{1,0:T(8,128)(2,1)} %get-tuple-element.139, bf16[2048,1024]{1,0:T(8,128)(2,1)} %bitcast.711), kind=kOutput, calls=%fused_computation.491 | convolution fusion | flops 8589934592 | bytes 25165824 | tf_op jit(solution)/shard_map/dot_general | solution.py:153
  755.6 11.2 all-to-all-done.5
  771.2 14.4 add_convert_fusion
  789.1 8.8 all-to-all-done.6
  801.7 14.0 convolution_convert_fusion.2
  815.7 12.6 all-to-all-done.4
  832.7 12.7 convolution_convert_fusion.3
  846.5 10.9 collective-permute-start.31
  861.2 4.8 all-to-all-start.9
  871.8 8.6 collective-permute-start.38
  884.6 19.4 %collective-permute-done.34 = bf16[1,512,1024]{2,1,0:T(8,128)(2,1)} collective-permute-done((bf16[1,512,1024]{2,1,0:T(8,128)(2,1)}, bf16[1,512,1024]{2,1,0:T(8,128)(2,1)}, u32[]{:S(2)}, u32[]{:S(2)}) %collective-permute-start.34) | collective-permute-done | bytes 1048608 | tf_op jit(solution)/shard_map/ppermute | solution.py:23
  938.6 8.7 all-to-all-done.8
  957.7 39.2 %collective-permute-start.35 = (bf16[1,512,1024]{2,1,0:T(8,128)(2,1)}, bf16[1,512,1024]{2,1,0:T(8,128)(2,1)}, u32[]{:S(2)}, u32[]{:S(2)}) collective-permute-start(bf16[1,512,1024]{2,1,0:T(8,128)(2,1)} %get-tuple-element.157), channel_id=1, source_target_pairs={{0,2},{1,3},{2,0},{3,1},{4,6},{5,7},{6,4},{7,5},{8,10},{9,11},{10,... | collective-permute-start | bytes 3145736 | tf_op jit(solution)/shard_map/ppermute | solution.py:23
  1003.5 34.1 %collective-permute-done.13 = bf16[192,2048]{1,0:T(8,128)(2,1)} collective-permute-done((bf16[192,2048]{1,0:T(8,128)(2,1)}, bf16[192,2048]{1,0:T(8,128)(2,1)}, u32[]{:S(2)}, u32[]{:S(2)}) %collective-permute-start.13) | collective-permute-done | bytes 786464 | tf_op jit(solution)/shard_map/ppermute | solution.py:23
  1045.5 74.0 %collective-permute-done.35 = bf16[1,512,1024]{2,1,0:T(8,128)(2,1)} collective-permute-done((bf16[1,512,1024]{2,1,0:T(8,128)(2,1)}, bf16[1,512,1024]{2,1,0:T(8,128)(2,1)}, u32[]{:S(2)}, u32[]{:S(2)}) %collective-permute-start.35) | collective-permute-done | bytes 1048608 | tf_op jit(solution)/shard_map/ppermute | solution.py:23
  1134.8 37.9 %collective-permute-done.32 = bf16[1,512,1024]{2,1,0:T(8,128)(2,1)S(1)} collective-permute-done((bf16[1,512,1024]{2,1,0:T(8,128)(2,1)}, bf16[1,512,1024]{2,1,0:T(8,128)(2,1)S(1)}, u32[]{:S(2)}, u32[]{:S(2)}) %collective-permute-start.32) | collective-permute-done | bytes 1048608 | tf_op jit(solution)/shard_map/ppermute | solution.py:23
  1177.5 10.5 collective-permute-done.14
  1199.0 6.3 convolution_convert_fusion.12
  1229.1 9.7 fusion.19
  1238.8 11.8 multiply_reduce_fusion
  1250.6 13.6 multiply_convert_fusion
  1292.3 8.2 all-gather.1
  1305.0 7.6 fusion.22
  1321.6 6.4 fusion.261
  1328.0 11.0 add_add_fusion
  1339.0 9.2 fusion.239
  1385.2 11.3 collective-permute-done.16
  1401.3 28.6 %collective-permute-done.22 = bf16[8,64,768]{2,1,0:T(8,128)(2,1)S(1)} collective-permute-done((bf16[8,64,768]{2,1,0:T(8,128)(2,1)S(1)}, bf16[8,64,768]{2,1,0:T(8,128)(2,1)S(1)}, u32[]{:S(2)}, u32[]{:S(2)}) %collective-permute-start.22) | collective-permute-done | bytes 786464 | tf_op jit(solution)/shard_map/ppermute | solution.py:23
  1432.6 8.4 collective-permute-done.29
  1448.8 9.5 all-to-all-done.13
  1462.5 5.2 fusion.35
  (608 shorter events, 360.3 us)
Async XLA Ops:
  386.2 87.5 %collective-permute-start.1 = (bf16[192,2048]{1,0:T(8,128)(2,1)}, bf16[192,2048]{1,0:T(8,128)(2,1)}, u32[]{:S(2)}, u32[]{:S(2)}) collective-permute-start(bf16[192,2048]{1,0:T(8,128)(2,1)} %get-tuple-element.32), channel_id=1, source_target_pairs={{0,2},{1,3},{2,0},{3,1},{4,6},{5,7},{6,4},{7,5},{8,10},{9,11},{10,... | collective-permute-start | bytes 2359304 | tf_op jit(solution)/shard_map/ppermute | solution.py:23
  413.5 42.9 %collective-permute-start = (bf16[192,2048]{1,0:T(8,128)(2,1)}, bf16[192,2048]{1,0:T(8,128)(2,1)}, u32[]{:S(2)}, u32[]{:S(2)}) collective-permute-start(bf16[192,2048]{1,0:T(8,128)(2,1)} %get-tuple-element.32), channel_id=1, source_target_pairs={{0,1},{1,0},{2,3},{3,2},{4,5},{5,4},{6,7},{7,6},{8,9},{9,8},{10,11... | collective-permute-start | bytes 2359304 | tf_op jit(solution)/shard_map/ppermute | solution.py:23
  415.8 110.7 %collective-permute-start.3 = (bf16[1,256,2048]{2,1,0:T(8,128)(2,1)}, bf16[1,256,2048]{2,1,0:T(8,128)(2,1)}, u32[]{:S(2)}, u32[]{:S(2)}) collective-permute-start(bf16[1,256,2048]{2,1,0:T(8,128)(2,1)} %constant_dynamic-slice_fusion.21), channel_id=1, source_target_pairs={{0,1},{1,0},{2,3},{3,2},{4,5},{5,4},{6,7},{7,6},{8,9},{9,8},{10,11... | collective-permute-start | bytes 3145736 | tf_op jit(solution)/shard_map/ppermute | solution.py:23
  422.6 37.0 %all-to-all-start = ((bf16[8,64,2048]{2,1,0:T(8,128)(2,1)}), bf16[8,64,2048]{2,1,0:T(8,128)(2,1)}, u32[]{:S(2)}, u32[]{:S(2)}) async-start(bf16[8,64,2048]{2,1,0:T(8,128)(2,1)} %convolution_convert_fusion.11), calls=%async_computation | async-start | bytes 4194304 | tf_op jit(solution)/shard_map/all_to_all | solution.py:110
  459.6 31.0 %all-to-all-start.1 = ((bf16[8,64,2048]{2,1,0:T(8,128)(2,1)}), bf16[8,64,2048]{2,1,0:T(8,128)(2,1)}, u32[]{:S(2)}, u32[]{:S(2)}) async-start(bf16[8,64,2048]{2,1,0:T(8,128)(2,1)} %convolution_convert_fusion.10), calls=%async_computation.1 | async-start | bytes 4194304 | tf_op jit(solution)/shard_map/all_to_all | solution.py:110
  490.6 31.5 %all-to-all-start.2 = ((bf16[8,64,2048]{2,1,0:T(8,128)(2,1)}), bf16[8,64,2048]{2,1,0:T(8,128)(2,1)}, u32[]{:S(2)}, u32[]{:S(2)}) async-start(bf16[8,64,2048]{2,1,0:T(8,128)(2,1)} %convolution_convert_fusion.9), calls=%async_computation.2 | async-start | bytes 4194304 | tf_op jit(solution)/shard_map/all_to_all | solution.py:110
  500.0 20.1 %collective-permute-start.2 = (bf16[192,2048]{1,0:T(8,128)(2,1)}, bf16[192,2048]{1,0:T(8,128)(2,1)S(1)}, u32[]{:S(2)}, u32[]{:S(2)}) collective-permute-start(bf16[192,2048]{1,0:T(8,128)(2,1)} %collective-permute-done.1), channel_id=1, source_target_pairs={{0,1},{1,0},{2,3},{3,2},{4,5},{5,4},{6,7},{7,6},{8,9},{9,8},{10,11... | collective-permute-start | bytes 2359304 | tf_op jit(solution)/shard_map/ppermute | solution.py:23
  522.2 81.4 %all-to-all-start.3 = ((bf16[8,64,2048]{2,1,0:T(8,128)(2,1)}), bf16[8,64,2048]{2,1,0:T(8,128)(2,1)}, u32[]{:S(2)}, u32[]{:S(2)}) async-start(bf16[8,64,2048]{2,1,0:T(8,128)(2,1)} %convolution_convert_fusion.8), calls=%async_computation.3 | async-start | bytes 4194304 | tf_op jit(solution)/shard_map/all_to_all | solution.py:110
  530.2 71.2 %collective-permute-start.4 = (bf16[1,256,2048]{2,1,0:T(8,128)(2,1)}, bf16[1,256,2048]{2,1,0:T(8,128)(2,1)S(1)}, u32[]{:S(2)}, u32[]{:S(2)}) collective-permute-start(bf16[1,256,2048]{2,1,0:T(8,128)(2,1)} %get-tuple-element.164), channel_id=1, source_target_pairs={{0,2},{1,3},{2,0},{3,1},{4,6},{5,7},{6,4},{7,5},{8,10},{9,11},{10,... | collective-permute-start | bytes 3145736 | tf_op jit(solution)/shard_map/ppermute | solution.py:23
  530.8 71.7 %collective-permute-start.5 = (bf16[1,256,2048]{2,1,0:T(8,128)(2,1)}, bf16[1,256,2048]{2,1,0:T(8,128)(2,1)S(1)}, u32[]{:S(2)}, u32[]{:S(2)}) collective-permute-start(bf16[1,256,2048]{2,1,0:T(8,128)(2,1)} %get-tuple-element.162), channel_id=1, source_target_pairs={{0,3},{1,2},{2,1},{3,0},{4,7},{5,6},{6,5},{7,4},{8,11},{9,10},{10,... | collective-permute-start | bytes 3145736 | tf_op jit(solution)/shard_map/ppermute | solution.py:23
  694.1 41.5 %all-to-all-start.7 = ((bf16[8,64,2048]{2,1,0:T(8,128)(2,1)}), bf16[8,64,2048]{2,1,0:T(8,128)(2,1)S(1)}, u32[]{:S(2)}, u32[]{:S(2)}) async-start(bf16[8,64,2048]{2,1,0:T(8,128)(2,1)} %bitcast.40), calls=%async_computation.7 | async-start | bytes 4194304 | tf_op jit(solution)/shard_map/all_to_all | solution.py:110
  713.7 152.5 %collective-permute-start.37 = (bf16[1,256,2048]{2,1,0:T(8,128)(2,1)}, bf16[1,256,2048]{2,1,0:T(8,128)(2,1)}, u32[]{:S(2)}, u32[]{:S(2)}) collective-permute-start(bf16[1,256,2048]{2,1,0:T(8,128)(2,1)} %constant_dynamic-slice_fusion.2), channel_id=1, source_target_pairs={{0,1},{1,0},{2,3},{3,2},{4,5},{5,4},{6,7},{7,6},{8,9},{9,8},{10,11... | collective-permute-start | bytes 3145736 | tf_op jit(solution)/shard_map/ppermute | solution.py:23
  735.6 31.2 %all-to-all-start.5 = ((bf16[8,64,2048]{2,1,0:T(8,128)(2,1)}), bf16[8,64,2048]{2,1,0:T(8,128)(2,1)}, u32[]{:S(2)}, u32[]{:S(2)}) async-start(bf16[8,64,2048]{2,1,0:T(8,128)(2,1)} %bitcast.32), calls=%async_computation.5 | async-start | bytes 4194304 | tf_op jit(solution)/shard_map/all_to_all | solution.py:110
  766.8 31.0 %all-to-all-start.6 = ((bf16[8,64,2048]{2,1,0:T(8,128)(2,1)}), bf16[8,64,2048]{2,1,0:T(8,128)(2,1)}, u32[]{:S(2)}, u32[]{:S(2)}) async-start(bf16[8,64,2048]{2,1,0:T(8,128)(2,1)} %bitcast.36), calls=%async_computation.6 | async-start | bytes 4194304 | tf_op jit(solution)/shard_map/all_to_all | solution.py:110
  797.9 30.4 %all-to-all-start.4 = ((bf16[8,64,2048]{2,1,0:T(8,128)(2,1)}), bf16[8,64,2048]{2,1,0:T(8,128)(2,1)S(1)}, u32[]{:S(2)}, u32[]{:S(2)}) async-start(bf16[8,64,2048]{2,1,0:T(8,128)(2,1)} %bitcast.630), calls=%async_computation.4 | async-start | bytes 4194304 | tf_op jit(solution)/shard_map/all_to_all | solution.py:110
  828.3 32.9 %all-to-all-start.11 = ((bf16[8,64,2048]{2,1,0:T(8,128)(2,1)}), bf16[8,64,2048]{2,1,0:T(8,128)(2,1)}, u32[]{:S(2)}, u32[]{:S(2)}) async-start(bf16[8,64,2048]{2,1,0:T(8,128)(2,1)} %bitcast.631), calls=%async_computation.11 | async-start | bytes 4194304 | tf_op jit(solution)/shard_map/all_to_all | solution.py:110
  846.5 35.3 %collective-permute-start.31 = (bf16[1,512,1024]{2,1,0:T(8,128)(2,1)}, bf16[1,512,1024]{2,1,0:T(8,128)(2,1)}, u32[]{:S(2)}, u32[]{:S(2)}) collective-permute-start(bf16[1,512,1024]{2,1,0:T(8,128)(2,1)} %constant_dynamic-slice_fusion.8), channel_id=1, source_target_pairs={{0,1},{1,0},{2,3},{3,2},{4,5},{5,4},{6,7},{7,6},{8,9},{9,8},{10,11... | collective-permute-start | bytes 3145736 | tf_op jit(solution)/shard_map/ppermute | solution.py:23
  859.7 44.3 %collective-permute-start.34 = (bf16[1,512,1024]{2,1,0:T(8,128)(2,1)}, bf16[1,512,1024]{2,1,0:T(8,128)(2,1)}, u32[]{:S(2)}, u32[]{:S(2)}) collective-permute-start(bf16[1,512,1024]{2,1,0:T(8,128)(2,1)} %constant_dynamic-slice_fusion.5), channel_id=1, source_target_pairs={{0,1},{1,0},{2,3},{3,2},{4,5},{5,4},{6,7},{7,6},{8,9},{9,8},{10,11... | collective-permute-start | bytes 3145736 | tf_op jit(solution)/shard_map/ppermute | solution.py:23
  861.2 55.0 %all-to-all-start.9 = ((bf16[8,64,2048]{2,1,0:T(8,128)(2,1)}), bf16[8,64,2048]{2,1,0:T(8,128)(2,1)}, u32[]{:S(2)}, u32[]{:S(2)}) async-start(bf16[8,64,2048]{2,1,0:T(8,128)(2,1)} %bitcast.629), calls=%async_computation.9 | async-start | bytes 4194304 | tf_op jit(solution)/shard_map/all_to_all | solution.py:110
  870.0 175.4 %collective-permute-start.39 = (bf16[1,256,2048]{2,1,0:T(8,128)(2,1)}, bf16[1,256,2048]{2,1,0:T(8,128)(2,1)}, u32[]{:S(2)}, u32[]{:S(2)}) collective-permute-start(bf16[1,256,2048]{2,1,0:T(8,128)(2,1)} %get-tuple-element.153), channel_id=1, source_target_pairs={{0,3},{1,2},{2,1},{3,0},{4,7},{5,6},{6,5},{7,4},{8,11},{9,10},{10,... | collective-permute-start | bytes 3145736 | tf_op jit(solution)/shard_map/ppermute | solution.py:23
  871.8 129.8 %collective-permute-start.38 = (bf16[1,256,2048]{2,1,0:T(8,128)(2,1)}, bf16[1,256,2048]{2,1,0:T(8,128)(2,1)}, u32[]{:S(2)}, u32[]{:S(2)}) collective-permute-start(bf16[1,256,2048]{2,1,0:T(8,128)(2,1)} %get-tuple-element.154), channel_id=1, source_target_pairs={{0,2},{1,3},{2,0},{3,1},{4,6},{5,7},{6,4},{7,5},{8,10},{9,11},{10,... | collective-permute-start | bytes 3145736 | tf_op jit(solution)/shard_map/ppermute | solution.py:23
  911.0 85.9 %collective-permute-start.10 = (f32[192,8]{0,1:T(8,128)S(1)}, f32[192,8]{0,1:T(8,128)S(1)}, u32[]{:S(2)}, u32[]{:S(2)}) collective-permute-start(f32[192,8]{0,1:T(8,128)S(1)} %bitcast.701), channel_id=1, source_target_pairs={{0,2},{1,3},{2,0},{3,1},{4,6},{5,7},{6,4},{7,5},{8,10},{9,11},{10,... | collective-permute-start | bytes 18440 | tf_op jit(solution)/shard_map/ppermute | solution.py:23
  916.2 41.5 %collective-permute-start.9 = (f32[192,8]{0,1:T(8,128)S(1)}, f32[192,8]{0,1:T(8,128)S(1)}, u32[]{:S(2)}, u32[]{:S(2)}) collective-permute-start(f32[192,8]{0,1:T(8,128)S(1)} %bitcast.702), channel_id=1, source_target_pairs={{0,1},{1,0},{2,3},{3,2},{4,5},{5,4},{6,7},{7,6},{8,9},{9,8},{10,11... | collective-permute-start | bytes 18440 | tf_op jit(solution)/shard_map/ppermute | solution.py:23
  916.3 31.0 %all-to-all-start.8 = ((bf16[8,64,2048]{2,1,0:T(8,128)(2,1)}), bf16[8,64,2048]{2,1,0:T(8,128)(2,1)}, u32[]{:S(2)}, u32[]{:S(2)}) async-start(bf16[8,64,2048]{2,1,0:T(8,128)(2,1)} %bitcast.628), calls=%async_computation.8 | async-start | bytes 4194304 | tf_op jit(solution)/shard_map/all_to_all | solution.py:110
  923.5 32.1 %collective-permute-start.11 = (f32[192,8]{0,1:T(8,128)S(1)}, f32[192,8]{0,1:T(8,128)S(1)}, u32[]{:S(2)}, u32[]{:S(2)}) collective-permute-start(f32[192,8]{0,1:T(8,128)S(1)} %bitcast.703), channel_id=1, source_target_pairs={{0,3},{1,2},{2,1},{3,0},{4,7},{5,6},{6,5},{7,4},{8,11},{9,10},{10,... | collective-permute-start | bytes 18440 | tf_op jit(solution)/shard_map/ppermute | solution.py:23
  947.3 95.5 %all-to-all-start.10 = ((bf16[8,64,2048]{2,1,0:T(8,128)(2,1)}), bf16[8,64,2048]{2,1,0:T(8,128)(2,1)}, u32[]{:S(2)}, u32[]{:S(2)}) async-start(bf16[8,64,2048]{2,1,0:T(8,128)(2,1)} %bitcast.627), calls=%async_computation.10 | async-start | bytes 4194304 | tf_op jit(solution)/shard_map/all_to_all | solution.py:110
  955.5 171.1 %collective-permute-start.36 = (bf16[1,512,1024]{2,1,0:T(8,128)(2,1)}, bf16[1,512,1024]{2,1,0:T(8,128)(2,1)}, u32[]{:S(2)}, u32[]{:S(2)}) collective-permute-start(bf16[1,512,1024]{2,1,0:T(8,128)(2,1)} %get-tuple-element.156), channel_id=1, source_target_pairs={{0,3},{1,2},{2,1},{3,0},{4,7},{5,6},{6,5},{7,4},{8,11},{9,10},{10,... | collective-permute-start | bytes 3145736 | tf_op jit(solution)/shard_map/ppermute | solution.py:23
  957.7 161.8 %collective-permute-start.35 = (bf16[1,512,1024]{2,1,0:T(8,128)(2,1)}, bf16[1,512,1024]{2,1,0:T(8,128)(2,1)}, u32[]{:S(2)}, u32[]{:S(2)}) collective-permute-start(bf16[1,512,1024]{2,1,0:T(8,128)(2,1)} %get-tuple-element.157), channel_id=1, source_target_pairs={{0,2},{1,3},{2,0},{3,1},{4,6},{5,7},{6,4},{7,5},{8,10},{9,11},{10,... | collective-permute-start | bytes 3145736 | tf_op jit(solution)/shard_map/ppermute | solution.py:23
  996.9 40.7 %collective-permute-start.13 = (bf16[192,2048]{1,0:T(8,128)(2,1)}, bf16[192,2048]{1,0:T(8,128)(2,1)}, u32[]{:S(2)}, u32[]{:S(2)}) collective-permute-start(bf16[192,2048]{1,0:T(8,128)(2,1)} %fusion.18), channel_id=1, source_target_pairs={{0,1},{1,0},{2,3},{3,2},{4,5},{5,4},{6,7},{7,6},{8,9},{9,8},{10,11... | collective-permute-start | bytes 2359304 | tf_op jit(solution)/shard_map/ppermute | solution.py:23
  1001.6 171.2 %collective-permute-start.33 = (bf16[1,512,1024]{2,1,0:T(8,128)(2,1)S(1)}, bf16[1,512,1024]{2,1,0:T(8,128)(2,1)S(1)}, u32[]{:S(2)}, u32[]{:S(2)}) collective-permute-start(bf16[1,512,1024]{2,1,0:T(8,128)(2,1)S(1)} %copy-done.62), channel_id=1, source_target_pairs={{0,3},{1,2},{2,1},{3,0},{4,7},{5,6},{6,5},{7,4},{8,11},{9,10},{10,... | collective-permute-start | bytes 3145736 | tf_op jit(solution)/shard_map/ppermute | solution.py:23
  1037.6 135.1 %collective-permute-start.32 = (bf16[1,512,1024]{2,1,0:T(8,128)(2,1)}, bf16[1,512,1024]{2,1,0:T(8,128)(2,1)S(1)}, u32[]{:S(2)}, u32[]{:S(2)}) collective-permute-start(bf16[1,512,1024]{2,1,0:T(8,128)(2,1)} %get-tuple-element.160), channel_id=1, source_target_pairs={{0,2},{1,3},{2,0},{3,1},{4,6},{5,7},{6,4},{7,5},{8,10},{9,11},{10,... | collective-permute-start | bytes 3145736 | tf_op jit(solution)/shard_map/ppermute | solution.py:23
  1045.4 132.1 %collective-permute-start.12 = (bf16[192,2048]{1,0:T(8,128)(2,1)S(1)}, bf16[192,2048]{1,0:T(8,128)(2,1)S(1)}, u32[]{:S(2)}, u32[]{:S(2)}) collective-permute-start(bf16[192,2048]{1,0:T(8,128)(2,1)S(1)} %copy-done.113), channel_id=1, source_target_pairs={{0,1},{1,0},{2,3},{3,2},{4,5},{5,4},{6,7},{7,6},{8,9},{9,8},{10,11... | collective-permute-start | bytes 2359304 | tf_op jit(solution)/shard_map/ppermute | solution.py:23
  1119.5 68.5 %collective-permute-start.14 = (bf16[192,2048]{1,0:T(8,128)(2,1)S(1)}, bf16[192,2048]{1,0:T(8,128)(2,1)S(1)}, u32[]{:S(2)}, u32[]{:S(2)}) collective-permute-start(bf16[192,2048]{1,0:T(8,128)(2,1)S(1)} %add_convert_fusion.1), channel_id=1, source_target_pairs={{0,2},{1,3},{2,0},{3,1},{4,6},{5,7},{6,4},{7,5},{8,10},{9,11},{10,... | collective-permute-start | bytes 2359304 | tf_op jit(solution)/shard_map/ppermute | solution.py:23
  1126.6 335.9 %collective-permute-start.6 = (bf16[192,2048]{1,0:T(8,128)(2,1)}, bf16[192,2048]{1,0:T(8,128)(2,1)}, u32[]{:S(2)}, u32[]{:S(2)}) collective-permute-start(bf16[192,2048]{1,0:T(8,128)(2,1)} %fusion.15), channel_id=1, source_target_pairs={{0,1},{1,0},{2,3},{3,2},{4,5},{5,4},{6,7},{7,6},{8,9},{9,8},{10,11... | collective-permute-start | bytes 2359304 | tf_op jit(solution)/shard_map/ppermute | solution.py:23
  1172.8 41.8 %collective-permute-start.7 = (bf16[192,2048]{1,0:T(8,128)(2,1)}, bf16[192,2048]{1,0:T(8,128)(2,1)}, u32[]{:S(2)}, u32[]{:S(2)}) collective-permute-start(bf16[192,2048]{1,0:T(8,128)(2,1)} %fusion.16), channel_id=1, source_target_pairs={{0,1},{1,0},{2,3},{3,2},{4,5},{5,4},{6,7},{7,6},{8,9},{9,8},{10,11... | collective-permute-start | bytes 2359304 | tf_op jit(solution)/shard_map/ppermute | solution.py:23
  1190.1 20.7 %all-to-all-start.15 = ((f32[32,1,2112]{2,1,0:T(1,128)}), f32[32,1,2112]{2,1,0:T(1,128)S(1)}, u32[]{:S(2)}, u32[]{:S(2)}) async-start(f32[32,1,2112]{2,1,0:T(1,128)} %copy.302), calls=%async_computation.15 | async-start | bytes 557056 | tf_op jit(solution)/shard_map/all_to_all | solution.py:110
  1195.7 22.3 %collective-permute-start.23 = (bf16[192,1024]{1,0:T(8,128)(2,1)S(1)}, bf16[192,1024]{1,0:T(8,128)(2,1)S(1)}, u32[]{:S(2)}, u32[]{:S(2)}) collective-permute-start(bf16[192,1024]{1,0:T(8,128)(2,1)S(1)} %get-tuple-element.212), channel_id=1, source_target_pairs={{0,8},{4,12},{8,0},{12,4},{16,24},{20,28},{24,16},{28,20},{1,9},{5... | collective-permute-start | bytes 1179656 | tf_op jit(solution)/shard_map/ppermute | solution.py:23
  1197.5 20.5 %collective-permute-start.26 = (bf16[192,1024]{1,0:T(8,128)(2,1)S(1)}, bf16[192,1024]{1,0:T(8,128)(2,1)S(1)}, u32[]{:S(2)}, u32[]{:S(2)}) collective-permute-start(bf16[192,1024]{1,0:T(8,128)(2,1)S(1)} %get-tuple-element.213), channel_id=1, source_target_pairs={{0,16},{4,20},{8,24},{12,28},{16,0},{20,4},{24,8},{28,12},{1,17},{... | collective-permute-start | bytes 1179656 | tf_op jit(solution)/shard_map/ppermute | solution.py:23
  1219.8 142.5 %collective-permute-start.27 = (bf16[2,192,1024]{2,1,0:T(8,128)(2,1)}, bf16[2,192,1024]{2,1,0:T(8,128)(2,1)}, u32[]{:S(2)}, u32[]{:S(2)}) collective-permute-start(bf16[2,192,1024]{2,1,0:T(8,128)(2,1)} %pad_maximum_fusion.9), channel_id=1, source_target_pairs={{0,8},{4,12},{8,0},{12,4},{16,24},{20,28},{24,16},{28,20},{1,9},{5... | collective-permute-start | bytes 2359304 | tf_op jit(solution)/shard_map/ppermute | solution.py:23
  1222.8 135.7 %collective-permute-start.24 = (bf16[2,192,1024]{2,1,0:T(8,128)(2,1)}, bf16[2,192,1024]{2,1,0:T(8,128)(2,1)}, u32[]{:S(2)}, u32[]{:S(2)}) collective-permute-start(bf16[2,192,1024]{2,1,0:T(8,128)(2,1)} %pad_maximum_fusion.8), channel_id=1, source_target_pairs={{0,16},{4,20},{8,24},{12,28},{16,0},{20,4},{24,8},{28,12},{1,17},{... | collective-permute-start | bytes 2359304 | tf_op jit(solution)/shard_map/ppermute | solution.py:23
  1289.1 67.7 %all-to-all-start.14 = ((f32[4,1,128]{2,1,0:T(1,128)}), f32[4,1,128]{2,1,0:T(1,128)S(1)}, u32[]{:S(2)}, u32[]{:S(2)}) async-start(f32[4,1,128]{2,1,0:T(1,128)} %reshape.623), calls=%async_computation.14 | async-start | bytes 4096 | tf_op jit(solution)/shard_map/all_to_all | solution.py:110
  1317.7 47.9 %collective-permute-start.21 = (bf16[2,8,64,768]{3,2,1,0:T(8,128)(2,1)}, bf16[2,8,64,768]{3,2,1,0:T(8,128)(2,1)}, u32[]{:S(2)}, u32[]{:S(2)}) collective-permute-start(bf16[2,8,64,768]{3,2,1,0:T(8,128)(2,1)} %fusion.40), channel_id=1, source_target_pairs={{0,1},{1,0},{2,3},{3,2},{4,5},{5,4},{6,7},{7,6},{8,9},{9,8},{10,11... | collective-permute-start | bytes 4718600 | tf_op jit(solution)/shard_map/ppermute | solution.py:23
  1358.5 104.0 %collective-permute-start.8 = (bf16[192,2048]{1,0:T(8,128)(2,1)}, bf16[192,2048]{1,0:T(8,128)(2,1)}, u32[]{:S(2)}, u32[]{:S(2)}) collective-permute-start(bf16[192,2048]{1,0:T(8,128)(2,1)} %add_convert_fusion.3), channel_id=1, source_target_pairs={{0,2},{1,3},{2,0},{3,1},{4,6},{5,7},{6,4},{7,5},{8,10},{9,11},{10,... | collective-permute-start | bytes 2359304 | tf_op jit(solution)/shard_map/ppermute | solution.py:23
  1373.4 56.5 %collective-permute-start.22 = (bf16[8,64,768]{2,1,0:T(8,128)(2,1)S(1)}, bf16[8,64,768]{2,1,0:T(8,128)(2,1)S(1)}, u32[]{:S(2)}, u32[]{:S(2)}) collective-permute-start(bf16[8,64,768]{2,1,0:T(8,128)(2,1)S(1)} %fusion.60), channel_id=1, source_target_pairs={{0,2},{1,3},{2,0},{3,1},{4,6},{5,7},{6,4},{7,5},{8,10},{9,11},{10,... | collective-permute-start | bytes 2359304 | tf_op jit(solution)/shard_map/ppermute | solution.py:23
  1377.0 19.4 %collective-permute-start.16 = (bf16[2,192,1024]{2,1,0:T(8,128)(2,1)S(1)}, bf16[2,192,1024]{2,1,0:T(8,128)(2,1)S(1)}, u32[]{:S(2)}, u32[]{:S(2)}) collective-permute-start(bf16[2,192,1024]{2,1,0:T(8,128)(2,1)S(1)} %fusion.58), channel_id=1, source_target_pairs={{0,8},{4,12},{8,0},{12,4},{16,24},{20,28},{24,16},{28,20},{1,9},{5... | collective-permute-start | bytes 2359304 | tf_op jit(solution)/shard_map/ppermute | solution.py:23
  1396.4 44.6 %collective-permute-start.29 = (bf16[2,64,2048]{2,1,0:T(8,128)(2,1)S(1)}, bf16[2,64,2048]{2,1,0:T(8,128)(2,1)S(1)}, u32[]{:S(2)}, u32[]{:S(2)}) collective-permute-start(bf16[2,64,2048]{2,1,0:T(8,128)(2,1)S(1)} %fusion.83), channel_id=1, source_target_pairs={{0,1},{1,0},{2,3},{3,2},{4,5},{5,4},{6,7},{7,6},{8,9},{9,8},{10,11... | collective-permute-start | bytes 1572872 | tf_op jit(solution)/shard_map/ppermute | solution.py:23
  1400.2 42.6 %collective-permute-start.17 = (bf16[192,1024]{1,0:T(8,128)(2,1)S(1)}, bf16[192,1024]{1,0:T(8,128)(2,1)S(1)}, u32[]{:S(2)}, u32[]{:S(2)}) collective-permute-start(bf16[192,1024]{1,0:T(8,128)(2,1)S(1)} %fusion.114), channel_id=1, source_target_pairs={{0,16},{4,20},{8,24},{12,28},{16,0},{20,4},{24,8},{28,12},{1,17},{... | collective-permute-start | bytes 1179656 | tf_op jit(solution)/shard_map/ppermute | solution.py:23
  1442.1 26.1 %collective-permute-start.30 = (bf16[64,2048]{1,0:T(8,128)(2,1)}, bf16[64,2048]{1,0:T(8,128)(2,1)S(1)}, u32[]{:S(2)}, u32[]{:S(2)}) collective-permute-start(bf16[64,2048]{1,0:T(8,128)(2,1)} %fusion.116), channel_id=1, source_target_pairs={{0,2},{1,3},{2,0},{3,1},{4,6},{5,7},{6,4},{7,5},{8,10},{9,11},{10,... | collective-permute-start | bytes 786440 | tf_op jit(solution)/shard_map/ppermute | solution.py:23
  (133 other events, 1562.1 us)

commit v3 on v2

--- a/solution.py
+++ b/solution.py
@@ -47,11 +47,6 @@
     one = doubled(x[..., :half], "ctx", far + bits[:1])
     two = doubled(x[..., half:], "ctx", far[::-1] + bits[:1])
     return jnp.concatenate([one, two], axis=-1)
-
-
-def everywhere(x):
-    x = doubled(x, "fsdp", bits_of("fsdp")[::-1])
-    return doubled(x, "ctx", bits_of("ctx"))
 
 
 def spread(x):
@@ -88,24 +83,6 @@
     return jnp.concatenate([one, two], axis=-1)
 
 
-def near_first(x):
-    blocks = {0: x}
-    for bit in bits_of("fsdp")[::-1]:
-        for key in sorted(blocks):
-            blocks[key | bit] = swap(blocks[key], "fsdp", bit)
-    return [blocks[key] for key in sorted(blocks)]
-
-
-def back_home(parts):
-    parts = [part.astype(exact) for part in parts]
-    for bit in bits_of("fsdp"):
-        for key in range(len(parts)):
-            if key & bit and not key & (bit - 1):
-                got = swap(parts[key].astype(low), "fsdp", bit)
-                parts[key ^ bit] = parts[key ^ bit] + got.astype(exact)
-    return parts[0]
-
-
 def exchange(x, axis):
     return lax.all_to_all(x, axis, split_axis=0, concat_axis=0, tiled=True)
 
@@ -264,10 +241,10 @@
 
 def front_kernel(
     cfg,
-    x_ref, wq_ref, wk_ref, wv_ref, wo_ref, gt_ref, rt_ref, ro_ref, cot_ref, gp_ref, up_ref, cos_ref, sin_ref,
-    a1_out, w_full, raw_out, stat_out, rot_out, ob_out, wo_full, r1_out, a2_out, r_all, g_all, t_all,
-    gate_full, up_full, cot_rows, cot_near,
-    xbuf, wbuf, obw, gbuf, gfull, rbuf, tbuf, raw, stat, total, rq, rk, rot, opos, odev, orecv, r1, a2, cbuf, hot, cs,
+    x_ref, wq_ref, wk_ref, wv_ref, wo_ref, gt_ref, rt_ref, ro_ref, cot_ref, gp_ref, up_ref, dp_ref, cos_ref, sin_ref,
+    a1_out, w_full, raw_out, stat_out, rot_out, ob_out, wo_full, r1_out, r_all, g_all, t_all,
+    gate_full, up_full, down_full, cot_rows, cot_near, in_rows, in_near,
+    xbuf, wbuf, obw, gbuf, gfull, rbuf, tbuf, raw, stat, total, rq, rk, rot, opos, odev, orecv, r1, a2, cbuf, abuf, hot, cs,
     sends, recvs, locals_,
 ):
     nc, nz, tokens, width = cfg["nc"], cfg["nz"], cfg["tokens"], cfg["width"]
@@ -294,6 +271,7 @@
     own.append(links.move(cot_ref, cbuf.at[0]))
     mine = links.move(gp_ref.at[z], gate_full.at[z])
     mine_up = links.move(up_ref.at[z], up_full.at[z])
+    mine_down = links.move(dp_ref.at[z], down_full.at[z])
     greet(c, z, nc, nz)
 
     slices = []
@@ -392,9 +370,6 @@
     experts_in = []
     for s in range(1, nz):
         experts_in.append(links.send(gp_ref.at[z ^ s], gate_full.at[z], fsdp=z ^ s))
-    if cfg["carry_up"]:
-        for s in range(1, nz):
-            experts_in.append(links.send(up_ref.at[z ^ s], up_full.at[z], fsdp=z ^ s))
     w_copy = links.move(wbuf, w_full)
 
     one_row = lax.broadcasted_iota(jnp.int32, (8, cols), 0)
@@ -462,6 +437,8 @@
     lax.fori_loop(0, 2 * nc, turn, 0)
     rot_copy = links.move(rot, rot_out)
     forward(cot_copies, cot_send)
+    for s in range(1, nz):
+        experts_in.append(links.send(up_ref.at[z ^ s], up_full.at[z], fsdp=z ^ s))
 
     scale = hs ** -0.5
     for h in range(heads):
@@ -502,20 +479,24 @@
     near_copy = links.move(cbuf, cot_near)
     rows_sent = []
     slot_busy = [[], []]
-    for s in range(nz):
+
+    def dispatch(s, near, landing):
         slot = s % 2
         for copy in slot_busy[slot]:
             links.left(copy)
         fill_hot(cfg, plane_ranks(cfg, tbuf[c, z ^ s], z), hot)
-        cs[slot] = kdot(hot[...], cbuf[s]).astype(low)
+        cs[slot] = kdot(hot[...], near[s]).astype(low)
         busy = []
         for d in range(1, nc):
             src = cs.at[slot, ds((c ^ d) * cap, cap)]
-            copy = links.send(src, cot_rows.at[s, c], ctx=c ^ d)
+            copy = links.send(src, landing.at[s, c], ctx=c ^ d)
             rows_sent.append(copy)
             busy.append(copy)
-        busy.append(links.move(cs.at[slot, ds(c * cap, cap)], cot_rows.at[s, c]))
+        busy.append(links.move(cs.at[slot, ds(c * cap, cap)], landing.at[s, c]))
         slot_busy[slot] = busy
+
+    for s in range(nz):
+        dispatch(s, cbuf, cot_rows)
 
     for copy in wo_side:
         links.arrived(copy)
@@ -535,21 +516,36 @@
     v = r1[...] + a2[...].astype(exact)
     r1[...] = v
     n2 = v * lax.rsqrt(jnp.mean(v * v, axis=-1, keepdims=True) + epsilon)
-    a2[...] = (n2 * gfull[3:4, :]).astype(low)
+    abuf[0] = (n2 * gfull[3:4, :]).astype(low)
+    in_copies = {}
+
+    def in_send(s, bit):
+        in_copies[s | bit] = links.send(abuf.at[s], abuf.at[s | bit], fsdp=z ^ bit)
+
+    for bit in steps:
+        in_send(0, bit)
     links.move(r1, r1_out)
-    links.move(a2, a2_out)
+    dispatch(0, abuf, in_rows)
+    forward(in_copies, in_send)
+    for s in range(1, nz):
+        experts_in.append(links.send(dp_ref.at[z ^ s], down_full.at[z], fsdp=z ^ s))
     links.move(rbuf, r_all)
     links.move(gfull, g_all)
     links.move(tbuf, t_all)
+    for s in range(1, nz):
+        links.arrived(in_copies[s])
+        dispatch(s, abuf, in_rows)
+    links.move(abuf, in_near)
     for copy in experts_in + rows_sent:
         links.arrived(copy)
     links.close()
 
 
-def front(cfg, x, w_query, w_key, w_value, w_out, gains, router, routes, cot, gate_pieces, up_pieces, cosine, sine):
+def front(cfg, x, w_query, w_key, w_value, w_out, gains, router, routes, cot, gate_pieces, up_pieces, down_pieces, cosine, sine):
     nc, nz, tokens, width = cfg["nc"], cfg["nz"], cfg["tokens"], cfg["width"]
     cols, rows_w, length, cap = cfg["cols"], cfg["rows_w"], cfg["length"], cfg["cap"]
     rows, part = gate_pieces.shape[1:]
+    rows_d = down_pieces.shape[1]
     shape = jax.ShapeDtypeStruct
     any_, vmem = pl.BlockSpec(memory_space=pl.ANY), pl.BlockSpec(memory_space=pltpu.VMEM)
     top_rows = routes.shape[0]
@@ -562,12 +558,14 @@
         shape((length, cols), low),
         shape((nc, nz, rows_w, width), low),
         shape((tokens, width), exact),
-        shape((tokens, width), low),
         shape((nc, nz, rows_w, 128), low),
         shape((8, width), exact),
         shape((nc, nz, top_rows, tokens), jnp.int32),
         shape((nz, rows, part), low),
         shape((nz, rows, part), low),
+        shape((nz, rows_d, width), low),
+        shape((nz, nc, cap, width), low),
+        shape((nz, tokens, width), low),
         shape((nz, nc, cap, width), low),
         shape((nz, tokens, width), low),
     ]
@@ -591,6 +589,7 @@
         pltpu.VMEM((tokens, width), exact),
         pltpu.VMEM((tokens, width), low),
         pltpu.VMEM((nz, tokens, width), low),
+        pltpu.VMEM((nz, tokens, width), low),
         pltpu.VMEM((nc * cap, tokens), low),
         pltpu.VMEM((2, nc * cap, width), low),
         pltpu.SemaphoreType.DMA((cfg["copies"],)),
@@ -600,14 +599,378 @@
     return pl.pallas_call(
         functools.partial(front_kernel, cfg),
         out_shape=outs,
-        in_specs=[any_] * 11 + [vmem] * 2,
+        in_specs=[any_] * 12 + [vmem] * 2,
         out_specs=[any_] * len(outs),
         scratch_shapes=scratch,
         compiler_params=pltpu.CompilerParams(
             collective_id=0, has_side_effects=True, vmem_limit_bytes=cfg["vmem"]
         ),
         name="front",
-    )(x, w_query, w_key, w_value, w_out, gains, router, routes, cot, gate_pieces, up_pieces, cosine, sine)
+    )(x, w_query, w_key, w_value, w_out, gains, router, routes, cot, gate_pieces, up_pieces, down_pieces, cosine, sine)
+
+
+def expert_kernel(
+    cfg,
+    rows_ref, cotr_ref, rt_ref, tb_ref, wg_ref, wu_ref, wd_ref, near_ref, cotn_ref, r1_ref, gain_ref,
+    hidden_out, dr1_out, datt_out, dlog_out, fgain_out, gd_land, gg_land, gu_out,
+    back, in_back, out_land, in_land, ebh, rbh,
+    wg, wu, wd, rows, cotb, gin, dg, du, eb, rb, tile, ranks, hot, metab, dgs, dgl,
+    sends, recvs, locals_,
+):
+    nc, nz, tokens, width = cfg["nc"], cfg["nz"], cfg["tokens"], cfg["width"]
+    cap, part, split, exp_local = cfg["cap"], cfg["part"], cfg["split"], cfg["exp_local"]
+    ch = nc * cap
+    total = nz * ch
+    c, z = lax.axis_index("ctx"), lax.axis_index("fsdp")
+    links = Links(sends, recvs, locals_)
+    ds = pl.ds
+    expert = c * exp_local + z // split
+    best = lax.Precision.HIGHEST
+    peers = list(range(1, nc))
+
+    loads = [links.move(wg_ref, wg), links.move(wu_ref, wu), links.move(wd_ref, wd)]
+    loads.append(links.move(rows_ref, rows))
+    cot_base = links.local_count
+    links.local_count += nz
+    send_base = links.count
+    links.count += 2 * nz * (nc - 1)
+    keep_base = links.local_count
+    links.local_count += 2 * nz
+    off_base = links.local_count
+    links.local_count += 2 * nz
+
+    def cot_load(s, slot):
+        return pltpu.make_async_copy(
+            cotr_ref.at[ds(s * ch, ch)], cotb.at[slot], locals_.at[cot_base + s]
+        )
+
+    def chunk_copies(s, which):
+        buf, landing = ((ebh, back), (rbh, in_back))[which]
+        base = send_base + which * nz * (nc - 1) + s * (nc - 1)
+        out = []
+        for d in peers:
+            out.append(
+                pltpu.make_async_remote_copy(
+                    src_ref=buf.at[s, ds((c ^ d) * cap, cap)],
+                    dst_ref=landing.at[s, c],
+                    send_sem=sends.at[base + d - 1],
+                    recv_sem=recvs.at[base + d - 1],
+                    device_id={"ctx": c ^ d},
+                    device_id_type=pl.DeviceIdType.MESH,
+                )
+            )
+        return out
+
+    def keep_copy(s, which):
+        landing = (back, in_back)[which]
+        return pltpu.make_async_copy(
+            (ebh, rbh)[which].at[s, ds(c * cap, cap)],
+            landing.at[s, c],
+            locals_.at[keep_base + which * nz + s],
+        )
+
+    def off_copy(s, which):
+        return pltpu.make_async_copy(
+            (eb, rb)[which], (ebh, rbh)[which].at[s], locals_.at[off_base + which * nz + s]
+        )
+
+    cot_load(nz - 1, 0).start()
+    greet(c, z, nc, nz)
+    for copy in loads:
+        links.left(copy)
+
+    expert_rows = lax.broadcasted_iota(jnp.int32, (128, tokens), 0)
+    upper = jnp.where(
+        lax.broadcasted_iota(jnp.int32, (tokens, tokens), 0)
+        <= lax.broadcasted_iota(jnp.int32, (tokens, tokens), 1),
+        1.0,
+        0.0,
+    ).astype(low)
+
+    def routed(block):
+        chosen = jnp.zeros((128, tokens), exact)
+        for k in range(cfg["top"]):
+            chosen = jnp.where(block[k : k + 1, :] == expert_rows, 1.0, chosen)
+        return chosen
+
+    sub = min(256, ch)
+    lane = lax.broadcasted_iota(jnp.int32, (sub, 128), 1)
+
+    def work(i, _):
+        s = nz - 1 - i
+        slot = lax.rem(i, 2)
+
+        @pl.when(i + 1 < nz)
+        def _():
+            cot_load(s - 1, 1 - slot).start()
+
+        for k in range(nc):
+            block = tb_ref[k, z ^ s]
+            found = jnp.where(block == expert, 1.0, 0.0)
+            ranks[k : k + 1, :] = jnp.max(found, axis=0, keepdims=True)
+        ranks[...] = slots_of(cfg, ranks[...], upper)
+        fill_hot(cfg, ranks[...], hot)
+        for k in range(nc):
+            chosen = routed(tb_ref[k, z ^ s]).astype(low)
+            metab[k * cap : (k + 1) * cap, :] = kdot(
+                hot[k * cap : (k + 1) * cap, :], chosen, ((1,), (1,))
+            )
+        cot_load(s, slot).wait()
+
+        def some_rows(j, _):
+            here = pl.multiple_of(j * sub, sub)
+            at = pl.multiple_of(s * ch + j * sub, sub)
+            span, to = ds(here, sub), ds(at, sub)
+            block = rows[to, :]
+            logits = kdot(block, rt_ref[...], ((1,), (1,)))
+            logits = jnp.where(metab[span, :] > 0.5, logits, neg_large)
+            weight = jnp.exp(logits - jnp.max(logits, axis=-1, keepdims=True))
+            gate = jnp.sum(jnp.where(lane == expert, weight, 0.0), axis=-1, keepdims=True)
+            gate = gate / jnp.sum(weight, axis=-1, keepdims=True)
+            g = kdot(block, wg[...])
+            u = kdot(block, wu[...])
+            sg = 1.0 / (1.0 + jnp.exp(-g))
+            act = g * sg
+            inner = (act * u).astype(low)
+            gin[to, :] = (inner.astype(exact) * gate).astype(low)
+            eb[span, :] = kdot(inner, wd[...]).astype(low)
+            dinner = kdot(cotb[slot, span, :], wd[...], ((1,), (1,))) * gate
+            dg_low = (dinner * u * sg * (1.0 + g * (1.0 - sg))).astype(low)
+            du_low = (dinner * act).astype(low)
+            dg[to, :] = dg_low
+            du[to, :] = du_low
+            rb[span, :] = (
+                kdot(dg_low, wg[...], ((1,), (1,))) + kdot(du_low, wu[...], ((1,), (1,)))
+            ).astype(low)
+            return 0
+
+        lax.fori_loop(0, ch // sub, some_rows, 0)
+        for which in (0, 1):
+            off_copy(s, which).start()
+        for which in (0, 1):
+            off_copy(s, which).wait()
+            for copy in chunk_copies(s, which):
+                copy.start()
+            keep_copy(s, which).start()
+        return 0
+
+    lax.fori_loop(0, nz, work, 0)
+
+    rows_d = part // nz
+    step = 256 if nz * ch <= 2048 else 128
+    tile_base = links.local_count
+    links.local_count += width // step
+
+    def tile_load(k):
+        return pltpu.make_async_copy(
+            cotr_ref.at[:, ds(k * step, step)], tile.at[lax.rem(k, 2)], locals_.at[tile_base + k]
+        )
+
+    tile_load(0).start()
+
+    def down_tile(k, _):
+        @pl.when(k + 1 < width // step)
+        def _():
+            tile_load(k + 1).start()
+
+        tile_load(k).wait()
+        at = pl.multiple_of(k * step, step)
+        wd[:, ds(at, step)] = kdot(gin[...], tile[lax.rem(k, 2)], ((0,), (0,))).astype(low)
+        return 0
+
+    lax.fori_loop(0, width // step, down_tile, 0)
+    grads_out = []
+    for s in range(1, nz):
+        src = wd.at[ds(pl.multiple_of((z ^ s) * rows_d, rows_d), rows_d)]
+        grads_out.append(links.send(src, gd_land.at[z], fsdp=z ^ s))
+    links.move(wd.at[ds(pl.multiple_of(z * rows_d, rows_d), rows_d)], gd_land.at[z])
+    rows_g = width // nz
+
+    def rows_tile(left, dst):
+        def one(k, _):
+            at = pl.multiple_of(k * step, step)
+            dst[ds(at, step), :] = kdot(rows[:, ds(at, step)], left[...], ((0,), (0,))).astype(low)
+            return 0
+
+        lax.fori_loop(0, width // step, one, 0)
+
+    rows_tile(dg, wg)
+    for s in range(1, nz):
+        src = wg.at[ds(pl.multiple_of((z ^ s) * rows_g, rows_g), rows_g)]
+        grads_out.append(links.send(src, gg_land.at[z], fsdp=z ^ s))
+    links.move(wg.at[ds(pl.multiple_of(z * rows_g, rows_g), rows_g)], gg_land.at[z])
+    rows_tile(du, wu)
+    links.move(wu, gu_out)
+
+    spare = {}
+    at = 0
+    for name, count in (
+        ("back", ch), ("in_back", ch), ("near", tokens), ("cot", tokens), ("out0", tokens),
+        ("in0", tokens),
+    ):
+        spare[name] = rows.at[at : at + count]
+        at += count
+    stage = {0: (spare["out0"], spare["in0"]), 1: (cotb.at[0, 0:tokens], cotb.at[1, 0:tokens])}
+    extra = (cotb.at[0, tokens : 2 * tokens], cotb.at[1, tokens : 2 * tokens])
+    pick_rows = lax.broadcasted_iota(jnp.int32, (nc, 128), 0)
+    pick_lane = lax.broadcasted_iota(jnp.int32, (nc, 128), 1)
+    homeward = {}
+    gate_home = {}
+    busy = {0: [], 1: []}
+    gates_own = None
+    sums = None
+    for s in range(nz - 1, -1, -1):
+        for which in (0, 1):
+            out = chunk_copies(s, which)
+            for copy in out:
+                copy.wait_recv()
+            keep_copy(s, which).wait()
+        fetch = []
+        for k in range(nc):
+            fetch.append(links.move(back.at[s, k], rows.at[k * cap : (k + 1) * cap]))
+            fetch.append(links.move(in_back.at[s, k], rows.at[ch + k * cap : ch + (k + 1) * cap]))
+        fetch.append(links.move(near_ref.at[s], spare["near"]))
+        fetch.append(links.move(cotn_ref.at[s], spare["cot"]))
+        block = tb_ref[c, z ^ s]
+        fill_hot(cfg, plane_ranks(cfg, block, z), hot)
+        chosen = routed(block)
+        for copy in fetch:
+            links.left(copy)
+        logits = kdot(rt_ref[...], spare["near"][...], ((1,), (1,)))
+        logits = jnp.where(chosen > 0.5, logits, neg_large)
+        weight = jnp.exp(logits - jnp.max(logits, axis=0, keepdims=True))
+        gates = weight / jnp.sum(weight, axis=0, keepdims=True)
+        sel = jnp.where(pick_lane == pick_rows * exp_local + z // split, 1.0, 0.0)
+        plane = kdot(sel, gates, ((1,), (0,)), best)
+        slot_grad = kdot(spare["back"][...], spare["cot"][...], ((1,), (1,)))
+        for k in range(nc):
+            span = slice(k * cap, (k + 1) * cap)
+            hit = hot[span, :].astype(exact)
+            dgs[s, k : k + 1, :] = jnp.sum(hit * slot_grad[span, :], axis=0, keepdims=True)
+        in_part = kdot(hot[...], spare["in_back"][...], ((0,), (0,)))
+        for k in range(nc):
+            span = slice(k * cap, (k + 1) * cap)
+            hot[span, :] = (hot[span, :].astype(exact) * plane[k : k + 1, :]).astype(low)
+        out_part = kdot(hot[...], spare["back"][...], ((0,), (0,)))
+        lowest = s & -s
+        bit = 1
+        while bit < nz and (s == 0 or bit < lowest):
+            for copy in homeward[s | bit]:
+                links.arrived(copy)
+            got = [links.move(out_land.at[s | bit], extra[0]), links.move(in_land.at[s | bit], extra[1])]
+            for copy in got:
+                links.left(copy)
+            out_part += extra[0][...].astype(exact)
+            in_part += extra[1][...].astype(exact)
+            bit *= 2
+        if s:
+            slot = s % 2
+            for copy in busy[slot]:
+                links.left(copy)
+            stage[slot][0][...] = out_part.astype(low)
+            stage[slot][1][...] = in_part.astype(low)
+            homeward[s] = [
+                links.send(stage[slot][0], out_land.at[s], fsdp=z ^ lowest),
+                links.send(stage[slot][1], in_land.at[s], fsdp=z ^ lowest),
+            ]
+            busy[slot] = homeward[s]
+            gate_home[s] = links.send(dgs.at[s], dgl.at[s], fsdp=z ^ s)
+        else:
+            gates_own = gates
+            sums = (out_part, in_part)
+
+    dgate = jnp.zeros((128, tokens), exact)
+    for s in range(nz):
+        if s:
+            links.arrived(gate_home[s])
+        here = dgl[s] if s else dgs[0]
+        sel = jnp.where(pick_lane == pick_rows * exp_local + (z ^ s) // split, 1.0, 0.0)
+        dgate += kdot(sel, here, ((0,), (0,)), best)
+    dchosen = gates_own * (dgate - jnp.sum(gates_own * dgate, axis=0, keepdims=True))
+    dlog = dchosen.astype(low)
+    hot[0:128, :] = dlog
+    dlog_copy = links.move(hot.at[0:128], dlog_out)
+    out_part, in_part = sums
+    da2 = in_part + kdot(dlog, rt_ref[...], ((0,), (0,)))
+    r1 = r1_ref[...]
+    for copies in busy.values():
+        for copy in copies:
+            links.left(copy)
+    stage[0][0][...] = (r1 + out_part).astype(low)
+    links.move(stage[0][0], hidden_out)
+    rs = lax.rsqrt(jnp.mean(r1 * r1, axis=-1, keepdims=True) + epsilon)
+    n2 = r1 * rs
+    dm = da2 * gain_ref[3:4, :]
+    fgain_out[...] = jnp.broadcast_to(jnp.sum(da2 * n2, axis=0, keepdims=True), (8, width))
+    inner_mean = jnp.mean(dm * n2, axis=-1, keepdims=True)
+    dr1 = spare["cot"][...].astype(exact) + rs * (dm - n2 * inner_mean)
+    dr1_out[...] = dr1
+    datt_out[...] = dr1.astype(low)
+    for s in range(nz):
+        for which in (0, 1):
+            out = chunk_copies(s, which)
+            for copy in out:
+                copy.wait_send()
+    for copy in grads_out:
+        links.arrived(copy)
+    links.close()
+
+
+def run_experts(cfg, rows, cot_rows, router_t, routes, wg, wu, wd, near, cot_near, r1, gains):
+    nc, nz, tokens, width = cfg["nc"], cfg["nz"], cfg["tokens"], cfg["width"]
+    cap, part = cfg["cap"], cfg["part"]
+    ch = nc * cap
+    shape = jax.ShapeDtypeStruct
+    any_, vmem = pl.BlockSpec(memory_space=pl.ANY), pl.BlockSpec(memory_space=pltpu.VMEM)
+    outs = [
+        (shape((tokens, width), low), any_),
+        (shape((tokens, width), exact), vmem),
+        (shape((tokens, width), low), vmem),
+        (shape((128, tokens), low), any_),
+        (shape((8, width), exact), vmem),
+        (shape((nz, part // nz, width), low), any_),
+        (shape((nz, width // nz, part), low), any_),
+        (shape((width, part), low), any_),
+        (shape((nz, nc, cap, width), low), any_),
+        (shape((nz, nc, cap, width), low), any_),
+        (shape((nz, tokens, width), low), any_),
+        (shape((nz, tokens, width), low), any_),
+        (shape((nz, ch, width), low), any_),
+        (shape((nz, ch, width), low), any_),
+    ]
+    step = 256 if nz * ch <= 2048 else 128
+    scratch = [
+        pltpu.VMEM((width, part), low),
+        pltpu.VMEM((width, part), low),
+        pltpu.VMEM((part, width), low),
+        pltpu.VMEM((nz * ch, width), low),
+        pltpu.VMEM((2, ch, width), low),
+        pltpu.VMEM((nz * ch, part), low),
+        pltpu.VMEM((nz * ch, part), low),
+        pltpu.VMEM((nz * ch, part), low),
+        pltpu.VMEM((ch, width), low),
+        pltpu.VMEM((ch, width), low),
+        pltpu.VMEM((2, nz * ch, step), low),
+        pltpu.VMEM((nc, tokens), exact),
+        pltpu.VMEM((ch, tokens), low),
+        pltpu.VMEM((ch, 128), exact),
+        pltpu.VMEM((nz, nc, tokens), exact),
+        pltpu.VMEM((nz, nc, tokens), exact),
+        pltpu.SemaphoreType.DMA((2 * nz * nc + 8 * nz,)),
+        pltpu.SemaphoreType.DMA((2 * nz * nc + 8 * nz,)),
+        pltpu.SemaphoreType.DMA((2 * nz * nc + 16 * nz + width // step + 16,)),
+    ]
+    return pl.pallas_call(
+        functools.partial(expert_kernel, cfg),
+        out_shape=[o[0] for o in outs],
+        in_specs=[any_, any_, vmem, vmem, any_, any_, any_, any_, any_, vmem, vmem],
+        out_specs=[o[1] for o in outs],
+        scratch_shapes=scratch,
+        compiler_params=pltpu.CompilerParams(
+            collective_id=1, has_side_effects=True, vmem_limit_bytes=cfg["vmem"]
+        ),
+        name="experts",
+    )(rows, cot_rows, router_t, routes, wg, wu, wd, near, cot_near, r1, gains)
 
 
 def tables(nc, tokens, head_size):
@@ -674,11 +1037,11 @@
         top=top,
         exp_local=exp_local,
         split=split,
-        block=math.gcd(length, 256),
+        block=math.gcd(length, 256 if length <= 2048 else 128),
         chunk=math.gcd(length, 64),
-        copies=(ctx_count - 1) * (8 + z_count) + (z_count - 1) * 8 + 2 * ctx_count + 8,
-        carry_up=True,
-        vmem=60 * 2**20,
+        copies=(ctx_count - 1) * (8 + 2 * z_count) + (z_count - 1) * 12 + 2 * ctx_count + 8,
+        part=part,
+        vmem=62 * 2**20,
     )
     index = c_index * z_count + z_index
     per = 128 // rows_w
@@ -695,63 +1058,44 @@
         return weight.transpose(0, 3, 1, 2, 4).reshape(z_count, rows, part)
 
     (
-        attn_all, w_full, raw, squares, rot, out_heads, wo_full, resid_one, ffn_input,
-        router_full, gains, routes_all, gate_full, up_full, cot_rows, cot_near,
+        attn_all, w_full, raw, squares, rot, out_heads, wo_full, resid_one,
+        router_full, gains, routes_all, gate_full, up_full, down_full, cot_rows, cot_near,
+        input_rows, input_near,
     ) = front(
         cfg, hidden_in[0], w_query, w_key, w_value, w_out, gains, router_tile, route_tile,
-        cotangent[0], pieces_of(w_gate), pieces_of(w_up), *tables(ctx_count, tokens, head_size),
+        cotangent[0], pieces_of(w_gate), pieces_of(w_up),
+        w_down.reshape(z_count, -1, width), *tables(ctx_count, tokens, head_size),
     )
     gate_full = gate_full.reshape(-1, part)
     up_full = up_full.reshape(-1, part)
+    down_full = down_full.reshape(-1, width)
+    ffn_input = input_near[0]
+    router_t = router_full.reshape(width, 128).T
+    (
+        resid_two, grad_one, attn_grad_low, logit_grad, ffn_gain_grad, down_land, gate_land,
+        up_grad, *_,
+    ) = run_experts(
+        cfg, input_rows.reshape(-1, width), cot_rows.reshape(-1, width), router_t, routes_all,
+        gate_full, up_full, down_full, input_near, cot_near, resid_one, gains,
+    )
+    out_hidden = resid_two[None]
+    ffn_gain_grad = ffn_gain_grad[0]
+    router_grad = lax.dot_general(
+        ffn_input, logit_grad[:experts], (((0,), (1,)), ((), ())), preferred_element_type=exact
+    )
+
+    def whole_out(grad):
+        grad = grad.reshape(exp_local, split, -1, z_count, part // z_count)
+        return grad.transpose(0, 2, 3, 1, 4).reshape(exp_local, -1, hidden).astype(exact)
+
+    grad_down = down_land.reshape(exp_local, -1, width).astype(exact)
+    grad_gate = whole_out(gate_land)
+    grad_up = whole_out(spread(up_grad.reshape(z_count, -1, part)))
     w_full = w_full.reshape(3, width, cols)
     out_full = wo_full.reshape(width, width)
-    router_full = router_full.reshape(width, 128)[:, :experts]
-    cot_rows = cot_rows.reshape(-1, width)
-    attn_scale, ffn_scale = gains[0], gains[3]
+    attn_scale = gains[0]
     query_scale = lax.dynamic_slice_in_dim(gains[1], c_index * cols, cols)
     key_scale = lax.dynamic_slice_in_dim(gains[2], c_index * cols, cols)
-    routes_all = routes_all[:, :, :top].swapaxes(2, 3)
-
-    multi_all = jnp.sum(
-        (routes_all[..., None] == jnp.arange(experts, dtype=jnp.int32)).astype(exact), axis=-2
-    ).reshape(ctx_count, z_count, tokens, experts)
-    own_expert = c_index * exp_local + z_index // split
-    lower = (
-        jnp.arange(tokens)[:, None] >= jnp.arange(tokens)[None, :]
-    ).astype(low)
-
-    def slots(mask):
-        rank = jnp.einsum("ts,bs->bt", lower, mask.astype(low), preferred_element_type=exact)
-        rank = rank.astype(jnp.int32) - 1
-        hit = rank[:, None, :] == jnp.arange(capacity, dtype=jnp.int32)[None, :, None]
-        return (hit & (mask[:, None, :] > 0)).astype(low)
-
-    multi_own = lax.dynamic_index_in_dim(multi_all, c_index, 0, False)
-    sends = []
-    metas = []
-    for step in range(z_count):
-        source = z_index ^ step
-        multi = lax.dynamic_index_in_dim(multi_own, source, 0, False)
-        plane = multi.reshape(tokens, ctx_count, exp_local)
-        plane = lax.dynamic_index_in_dim(plane, z_index // split, 2, False)
-        sends.append(slots(plane.T))
-        there = lax.dynamic_index_in_dim(multi_all, source, 1, False)
-        mine = lax.dynamic_index_in_dim(there, own_expert, 2, False)
-        metas.append(
-            jnp.einsum(
-                "crt,cte->cre", slots(mine), there.astype(low), preferred_element_type=exact
-            )
-        )
-    meta = jnp.stack(metas).reshape(-1, experts)
-
-    def pick(hot, block):
-        rows = jnp.einsum("crt,td->crd", hot, block, preferred_element_type=exact)
-        return rows.astype(low)
-
-    cot_sent = [pick(hot, cot_near[step]) for step, hot in enumerate(sends)]
-    rows_d = w_down.shape[1]
-    down_full = spread(w_down.reshape(z_count, rows_d // split, width)).reshape(part, width)
-
     def total_over_ctx(one, two):
         both_sums = jnp.stack([one, two])
         return jnp.sum(lax.all_gather(both_sums, "ctx", axis=0), axis=0)
@@ -781,98 +1125,6 @@
     probs = jnp.exp(scores - log_total)
     probs_low = probs.astype(low)
     rows_in = hidden_in[0].astype(exact)
-    scale_two = lax.rsqrt(jnp.mean(resid_one * resid_one, axis=-1, keepdims=True) + epsilon)
-    normed_two = resid_one * scale_two
-
-    input_near = near_first(ffn_input)
-    input_rows = jnp.stack(
-        [exchange(pick(hot, block), "ctx") for hot, block in zip(sends, input_near)]
-    ).reshape(-1, width)
-
-    def routed_softmax(rows, multi):
-        logits = jnp.where(multi > 0, dot(rows, router_full), neg_large)
-        top_value = jnp.max(logits, axis=-1, keepdims=True)
-        weight = jnp.exp(logits - top_value)
-        return weight / jnp.sum(weight, axis=-1, keepdims=True)
-
-    row_gates = routed_softmax(input_rows, meta)
-    row_gate = lax.dynamic_slice_in_dim(row_gates, own_expert, 1, 1)
-    deout = (row_gate * cot_rows.astype(exact)).astype(low)
-    gate_pre = dot(input_rows, gate_full)
-    up_pre = dot(input_rows, up_full)
-    sigmoid_gate = jax.nn.sigmoid(gate_pre)
-    activated = gate_pre * sigmoid_gate
-    inner_low = (activated * up_pre).astype(low)
-    produced = dot(inner_low, down_full).astype(low)
-    inner_grad = contract_cols(deout, down_full)
-    gate_pre_grad = (
-        inner_grad * up_pre * sigmoid_gate * (1.0 + gate_pre * (1.0 - sigmoid_gate))
-    ).astype(low)
-    up_pre_grad = (inner_grad * activated).astype(low)
-    droute = (
-        contract_cols(gate_pre_grad, gate_full) + contract_cols(up_pre_grad, up_full)
-    ).astype(low)
-    down_grad = contract_rows(inner_low, deout).astype(low)
-    gate_grad = contract_rows(input_rows, gate_pre_grad).astype(low)
-    up_grad = contract_rows(input_rows, up_pre_grad).astype(low)
-
-    def whole_out(grad):
-        rows = grad.shape[0] // z_count
-        grad = spread(grad.reshape(z_count, rows, part))
-        grad = grad.reshape(exp_local, split, rows, z_count, part // z_count)
-        return grad.transpose(0, 2, 3, 1, 4).reshape(exp_local, rows, hidden).astype(exact)
-
-    grad_down = (
-        spread(down_grad.reshape(z_count, rows_d // split, width))
-        .reshape(exp_local, rows_d, width)
-        .astype(exact)
-    )
-    grad_gate = whole_out(gate_grad)
-    grad_up = whole_out(up_grad)
-
-    shape = (z_count, ctx_count, capacity, width)
-    produced = produced.reshape(shape)
-    droute = droute.reshape(shape)
-    out_parts = []
-    in_parts = []
-    gate_sums = []
-    for step in range(z_count):
-        source = z_index ^ step
-        hot = sends[step]
-        multi = lax.dynamic_index_in_dim(multi_own, source, 0, False)
-        gates = routed_softmax(input_near[step], multi)
-        if step == 0:
-            gates_own, multi_here = gates, multi
-        plane = gates.reshape(tokens, ctx_count, exp_local)
-        plane = lax.dynamic_index_in_dim(plane, z_index // split, 2, False)
-        back = exchange(produced[step], "ctx")
-        weighted = (hot * plane.T[:, None, :]).astype(low)
-        out_parts.append(
-            jnp.einsum("crt,crd->td", weighted, back, preferred_element_type=exact)
-        )
-        slot_grad = jnp.sum(cot_sent[step].astype(exact) * back.astype(exact), axis=-1)
-        gate_sums.append(jnp.sum(hot.astype(exact) * slot_grad[:, :, None], axis=1).T)
-        in_back = exchange(droute[step], "ctx")
-        in_parts.append(
-            jnp.einsum("crt,crd->td", hot, in_back, preferred_element_type=exact)
-        )
-    resid_two = resid_one + back_home(out_parts)
-    out_hidden = resid_two.astype(low)[None]
-    gate_grads = jnp.zeros((tokens, ctx_count, exp_local), exact)
-    for step in range(z_count):
-        got = swap(gate_sums[step], "fsdp", step) if step else gate_sums[step]
-        place = ((z_index ^ step) // split) == jnp.arange(exp_local)
-        gate_grads = gate_grads + got[:, :, None] * place.astype(exact)
-    gate_grads = gate_grads.reshape(tokens, experts)
-    weighted_sum = jnp.sum(gates_own * gate_grads, axis=-1, keepdims=True)
-    logit_grad = (gates_own * (gate_grads - weighted_sum)).astype(low)
-    input_grad = contract_cols(logit_grad, router_full) + back_home(in_parts)
-    router_grad = contract_rows(ffn_input, logit_grad)
-    grad_two = cotangent[0].astype(exact)
-    resid_norm_grad, ffn_gain_grad = rms_back(input_grad, normed_two, scale_two, ffn_scale)
-    grad_one = grad_two + resid_norm_grad
-
-    attn_grad_low = grad_one.astype(low)
     attn_grad_all = gather_ctx(attn_grad_low).reshape(length, width)
     out_weight_grad = contract_rows(out_heads, attn_grad_all)
     grad_heads = contract_cols(attn_grad_low, out_full).astype(low)

time: 1490 us -> 1200 us (0.81)
  Pallas kernels: 379 us -> 779 us
  waiting for transfers between devices: 380 us -> 102 us
  matrix products: 258 us -> 73.2 us
  starting transfers between devices: 220 us -> 60.2 us
  local copies, waits for them, and re-layouts: 113 us -> 69.3 us
  other arithmetic: 121 us -> 98.3 us
    pallas_call x0 -> x1, Pallas kernels: none -> 351 us  [run_experts(): pl.pallas_call(functools.partial(expert_kernel, cfg), out_shape=[o[0] for...]
    ppermute x40 -> x19, waiting for transfers between devices: 304 us -> 87.4 us  [swap(): return lax.ppermute(x, axis, [(i, i ^ bit) for i in range(length)])]
    ppermute x40 -> x19, starting transfers between devices: 148 us -> 40.1 us  [swap(): return lax.ppermute(x, axis, [(i, i ^ bit) for i in range(length)])]
    dot_general x36 -> x1, matrix products: 94.3 us -> 1.62 us  [body(): lax.dot_general(ffn_input, logit_grad[:experts], (((0,), (1,)), ((), ()))...]
    all_to_all x17 -> x5, waiting for transfers between devices: 75.9 us -> 14.8 us  [exchange(): return lax.all_to_all(x, axis, split_axis=0, concat_axis=0, tiled=True)]
    dot_general x8 -> x4, matrix products: 80.4 us -> 25.7 us  [contract_cols(): lax.dot_general(left, right, (((1,), (1,)), ((), ())), preferred_element_...]
    all_to_all x17 -> x5, starting transfers between devices: 72.2 us -> 20.1 us  [exchange(): return lax.all_to_all(x, axis, split_axis=0, concat_axis=0, tiled=True)]
    pallas_call x1, Pallas kernels: 379 us -> 428 us  [front(): pl.pallas_call(functools.partial(front_kernel, cfg), out_shape=outs, in_s...]
  transfers between devices with their start and end apart: 57 -> 24, of which waited for: 21 -> 7; matrix products, arithmetic and copies ran while one was open for 25% -> 18% of each run, Pallas kernels for 0% -> 0%
where the time goes in v3:
time: 1200 us; the launch traced here: 1190 us
  Pallas kernels  779 us (65%)
  waiting for transfers between devices  102 us (8%)
  other arithmetic  98.3 us (8%)
  matrix products  73.2 us (6%)
  local copies, waits for them, and re-layouts  69.3 us (6%)
  starting transfers between devices  60.2 us (5%)
    pallas_call x1, Pallas kernels, front(): pl.pallas_call(functools.partial(front_kernel, cfg), out_shape=outs, in_s...  428 us
    pallas_call x1, Pallas kernels, run_experts(): pl.pallas_call(functools.partial(expert_kernel, cfg), out_shape=[o[0] for...  351 us
    ppermute x19, waiting for transfers between devices, swap(): return lax.ppermute(x, axis, [(i, i ^ bit) for i in range(length)])  87.4 us
    ppermute x19, starting transfers between devices, swap(): return lax.ppermute(x, axis, [(i, i ^ bit) for i in range(length)])  40.1 us
    dot_general x4, matrix products, contract_cols(): lax.dot_general(left, right, (((1,), (1,)), ((), ())), preferred_element_...  25.7 us
  transfers between devices with their start and end apart: 24, of which 7 were waited for; matrix products, arithmetic and copies ran while one was open for 18% of the time, Pallas kernels for 0%

profile of v3, /device:TPU:0, one launch (start us, length us, event | category | flops | bytes accessed | tf_op | source)
XLA Modules:
  0.0 1192.7 jit_solution(11877250148984466394)
XLA Ops:
  3.7 427.9 %front.1 = (bf16[1536,2048]{1,0:T(8,128)(2,1)}, bf16[3,8,4,64,256]{4,3,2,1,0:T(8,128)(2,1)}, f32[1536,768]{1,0:T(8,128)}, f32[8,1536]{1,0:T(8,128)}, bf16[3,1536...) custom-call(bf16[192,2048]{1,0:T(8,128)(2,1)} %bitcast.331, ...), custom_call_target="tpu_custom_call" | custom-call | tf_op jit(solution)/shard_map/front/pallas_call | solution.py:599
  431.6 2.0 copy.256
  433.7 351.4 %experts.1 = (bf16[192,2048]{1,0:T(8,128)(2,1)}, f32[192,2048]{1,0:T(8,128)}, bf16[192,2048]{1,0:T(8,128)(2,1)}, bf16[128,192]{1,0:T(8,128)(2,1)}, f32[8,2048]{1...) custom-call(bf16[2048,2048]{1,0:T(8,128)(2,1)} %bitcast.335, ...), custom_call_target="tpu_custom_call" | custom-call | tf_op jit(solution)/shard_map/experts/pallas_call | solution.py:963
  785.1 2.3 constant_dynamic-slice_fusion.2
  795.4 3.4 all-to-all-start.3
  798.8 2.1 iota_compare_fusion
  802.7 6.4 convolution_convert_fusion
  810.8 10.1 fusion.81
  820.9 8.8 exponential_reduce_fusion
  830.6 4.3 multiply_cosine_fusion
  834.9 3.6 fusion.72
  839.1 4.1 all-to-all-start
  845.2 6.8 convert_element_type.198
  852.0 4.4 convert_element_type.200
  858.9 2.0 collective-permute-start.9
  865.9 9.6 fusion.13
  875.5 11.8 multiply_reduce_fusion
  887.3 13.3 %multiply_convert_fusion = bf16[2,1536,1536]{1,2,0:T(8,128)(2,1)S(1)} fusion(f32[2,1536,1536]{1,2,0:T(8,128)} %get-tuple-element.204, f32[2,1536,1536]{1,2,0:T(8,128)} %get-tuple-element.202, f32[2,1536]{1,0:T(2,128)S(1)} %get-tuple-element.203, f32[2,1536]{1,0:T(2,128)S(1)} %log_add_fusion), kind=kLoop, calls=%fused_computation | loop fusion | flops 18874368 | bytes 47210496 | tf_op jit(solution)/shard_map/convert_element_type | solution.py:1136
  902.1 3.2 fusion.9
  927.7 2.1 fusion.36
  929.9 8.3 all-gather.1
  938.3 4.3 multiply_convert_fusion.1
  942.6 8.0 fusion.16
  951.3 1.9 copy-done.1
  958.2 4.2 all-to-all-start.2
  964.3 6.4 fusion.82
  970.7 11.0 add_add_fusion
  981.7 9.3 fusion.71
  991.0 6.6 fusion.32
  1000.3 3.3 constant_dynamic-slice_fusion
  1003.7 2.9 collective-permute-start.17
  1014.7 60.9 %collective-permute-done.17 = bf16[1,512,1024]{2,1,0:T(8,128)(2,1)S(1)} collective-permute-done((bf16[1,512,1024]{2,1,0:T(8,128)(2,1)S(1)}, bf16[1,512,1024]{2,1,0:T(8,128)(2,1)S(1)}, u32[]{:S(2)}, u32[]{:S(2)}) %collective-permute-start.17) | collective-permute-done | bytes 1048608 | tf_op jit(solution)/shard_map/ppermute | solution.py:23
  1076.4 5.2 convert_element_type.199
  1081.7 2.2 bitcast_add_fusion
  1084.1 22.8 %collective-permute-start.7 = (bf16[8,64,768]{2,1,0:T(8,128)(2,1)S(1)}, bf16[8,64,768]{2,1,0:T(8,128)(2,1)S(1)}, u32[]{:S(2)}, u32[]{:S(2)}) collective-permute-start(bf16[8,64,768]{2,1,0:T(8,128)(2,1)S(1)} %fusion.45), channel_id=1, source_target_pairs={{0,2},{1,3},{2,0},{3,1},{4,6},{5,7},{6,4},{7,5},{8,10},{9,11},{10,... | collective-permute-start | bytes 2359304 | tf_op jit(solution)/shard_map/ppermute | solution.py:23
  1106.9 2.6 bitcast_add_fusion.2
  1111.4 2.6 bitcast_add_fusion.1
  1115.1 2.2 select_bitcast_fusion.1
  1121.5 8.1 collective-permute-done.1
  1131.6 3.0 collective-permute-done.4
  1135.4 6.7 collective-permute-done.7
  1143.2 8.6 collective-permute-done.14
  1155.3 4.2 all-to-all-start.1
  1159.5 7.5 all-to-all-done.1
  1167.0 4.2 all-to-all-start.4
  1171.2 3.0 fusion.29
  1176.5 7.3 all-to-all-done.4
  1183.8 2.5 reshape.348
  (274 shorter events, 90.9 us)
Async XLA Ops:
  787.4 212.9 %collective-permute-start.16 = (bf16[1,512,1024]{2,1,0:T(8,128)(2,1)}, bf16[1,512,1024]{2,1,0:T(8,128)(2,1)}, u32[]{:S(2)}, u32[]{:S(2)}) collective-permute-start(bf16[1,512,1024]{2,1,0:T(8,128)(2,1)} %constant_dynamic-slice_fusion.2), channel_id=1, source_target_pairs={{0,1},{1,0},{2,3},{3,2},{4,5},{5,4},{6,7},{7,6},{8,9},{9,8},{10,11... | collective-permute-start | bytes 3145736 | tf_op jit(solution)/shard_map/ppermute | solution.py:23
  788.3 68.2 %collective-permute-start.11 = (bf16[192,1024]{1,0:T(8,128)(2,1)}, bf16[192,1024]{1,0:T(8,128)(2,1)}, u32[]{:S(2)}, u32[]{:S(2)}) collective-permute-start(bf16[192,1024]{1,0:T(8,128)(2,1)} %get-tuple-element.189), channel_id=1, source_target_pairs={{0,16},{4,20},{8,24},{12,28},{16,0},{20,4},{24,8},{28,12},{1,17},{... | collective-permute-start | bytes 1179656 | tf_op jit(solution)/shard_map/ppermute | solution.py:23
  790.0 66.6 %collective-permute-start.8 = (bf16[192,1024]{1,0:T(8,128)(2,1)}, bf16[192,1024]{1,0:T(8,128)(2,1)}, u32[]{:S(2)}, u32[]{:S(2)}) collective-permute-start(bf16[192,1024]{1,0:T(8,128)(2,1)} %get-tuple-element.188), channel_id=1, source_target_pairs={{0,8},{4,12},{8,0},{12,4},{16,24},{20,28},{24,16},{28,20},{1,9},{5... | collective-permute-start | bytes 1179656 | tf_op jit(solution)/shard_map/ppermute | solution.py:23
  795.4 7.1 copy-start.7
  795.4 43.7 %all-to-all-start.3 = ((f32[32,1,2112]{2,1,0:T(1,128)}), f32[32,1,2112]{2,1,0:T(1,128)S(1)}, u32[]{:S(2)}, u32[]{:S(2)}) async-start(f32[32,1,2112]{2,1,0:T(1,128)} %copy.291), calls=%async_computation.3 | async-start | bytes 557056 | tf_op jit(solution)/shard_map/all_to_all | solution.py:87
  802.7 7.4 copy-start.39
  810.8 10.1 copy-start.31
  838.5 5.4 copy-start.42
  839.1 25.8 %all-to-all-start = ((bf16[8,192,256]{2,1,0:T(8,128)(2,1)}), bf16[8,192,256]{2,1,0:T(8,128)(2,1)S(1)}, u32[]{:S(2)}, u32[]{:S(2)}) async-start(bf16[8,192,256]{2,1,0:T(8,128)(2,1)} %bitcast.305), calls=%async_computation | async-start | bytes 1572864 | tf_op jit(solution)/shard_map/all_to_all | solution.py:87
  845.2 6.8 copy-start.13
  858.9 149.7 %collective-permute-start.9 = (bf16[2,192,1024]{2,1,0:T(8,128)(2,1)}, bf16[2,192,1024]{2,1,0:T(8,128)(2,1)}, u32[]{:S(2)}, u32[]{:S(2)}) collective-permute-start(bf16[2,192,1024]{2,1,0:T(8,128)(2,1)} %pad_maximum_fusion.7), channel_id=1, source_target_pairs={{0,16},{4,20},{8,24},{12,28},{16,0},{20,4},{24,8},{28,12},{1,17},{... | collective-permute-start | bytes 2359304 | tf_op jit(solution)/shard_map/ppermute | solution.py:23
  861.9 149.4 %collective-permute-start.12 = (bf16[2,192,1024]{2,1,0:T(8,128)(2,1)}, bf16[2,192,1024]{2,1,0:T(8,128)(2,1)}, u32[]{:S(2)}, u32[]{:S(2)}) collective-permute-start(bf16[2,192,1024]{2,1,0:T(8,128)(2,1)} %pad_maximum_fusion.8), channel_id=1, source_target_pairs={{0,8},{4,12},{8,0},{12,4},{16,24},{20,28},{24,16},{28,20},{1,9},{5... | collective-permute-start | bytes 2359304 | tf_op jit(solution)/shard_map/ppermute | solution.py:23
  942.6 8.0 copy-start.17
  942.6 8.0 copy-start.19
  951.3 4.5 copy-start.2
  953.3 9.1 copy-start.16
  953.3 9.1 copy-start.20
  955.9 125.8 %collective-permute-start.6 = (bf16[2,8,64,768]{3,2,1,0:T(8,128)(2,1)}, bf16[2,8,64,768]{3,2,1,0:T(8,128)(2,1)}, u32[]{:S(2)}, u32[]{:S(2)}) collective-permute-start(bf16[2,8,64,768]{3,2,1,0:T(8,128)(2,1)} %fusion.34), channel_id=1, source_target_pairs={{0,1},{1,0},{2,3},{3,2},{4,5},{5,4},{6,7},{7,6},{8,9},{9,8},{10,11... | collective-permute-start | bytes 4718600 | tf_op jit(solution)/shard_map/ppermute | solution.py:23
  958.2 40.9 %all-to-all-start.2 = ((f32[4,1,128]{2,1,0:T(1,128)}), f32[4,1,128]{2,1,0:T(1,128)S(1)}, u32[]{:S(2)}, u32[]{:S(2)}) async-start(f32[4,1,128]{2,1,0:T(1,128)} %reshape.365), calls=%async_computation.2 | async-start | bytes 4096 | tf_op jit(solution)/shard_map/all_to_all | solution.py:87
  964.2 6.4 copy-start.12
  964.3 6.4 copy-start.14
  991.0 6.6 copy-start
  1000.3 8.3 copy-start.26
  1000.3 8.3 copy-start.28
  1000.3 81.3 %slice-start.6 = ((s8[6291456]{0:T(1024)(128)(4,1)}), s8[4194304]{0:T(1024)(128)(4,1)S(1)}, s32[]{:S(2)}) async-start(s8[6291456]{0:T(1024)(128)(4,1)} %bitcast.322), calls=%async_computation.11 | async-start | bytes 8388608
  1003.7 71.9 %collective-permute-start.17 = (bf16[1,512,1024]{2,1,0:T(8,128)(2,1)S(1)}, bf16[1,512,1024]{2,1,0:T(8,128)(2,1)S(1)}, u32[]{:S(2)}, u32[]{:S(2)}) collective-permute-start(bf16[1,512,1024]{2,1,0:T(8,128)(2,1)S(1)} %get-tuple-element.153), channel_id=1, source_target_pairs={{0,2},{1,3},{2,0},{3,1},{4,6},{5,7},{6,4},{7,5},{8,10},{9,11},{10,... | collective-permute-start | bytes 3145736 | tf_op jit(solution)/shard_map/ppermute | solution.py:23
  1006.6 69.1 %collective-permute-start.18 = (bf16[1,512,1024]{2,1,0:T(8,128)(2,1)S(1)}, bf16[1,512,1024]{2,1,0:T(8,128)(2,1)S(1)}, u32[]{:S(2)}, u32[]{:S(2)}) collective-permute-start(bf16[1,512,1024]{2,1,0:T(8,128)(2,1)S(1)} %get-tuple-element.152), channel_id=1, source_target_pairs={{0,3},{1,2},{2,1},{3,0},{4,7},{5,6},{6,5},{7,4},{8,11},{9,10},{10,... | collective-permute-start | bytes 3145736 | tf_op jit(solution)/shard_map/ppermute | solution.py:23
  1008.6 98.3 %collective-permute-start = (bf16[2,2,192,1024]{3,2,1,0:T(8,128)(2,1)}, bf16[2,2,192,1024]{3,2,1,0:T(8,128)(2,1)}, u32[]{:S(2)}, u32[]{:S(2)}) collective-permute-start(bf16[2,2,192,1024]{3,2,1,0:T(8,128)(2,1)} %fusion.32), channel_id=1, source_target_pairs={{0,4},{4,0},{8,12},{12,8},{16,20},{20,16},{24,28},{28,24},{1,5},{5... | collective-permute-start | bytes 4718600 | tf_op jit(solution)/shard_map/ppermute | solution.py:23
  1011.3 100.1 %collective-permute-start.3 = (bf16[2,2,192,1024]{3,2,1,0:T(8,128)(2,1)}, bf16[2,2,192,1024]{3,2,1,0:T(8,128)(2,1)}, u32[]{:S(2)}, u32[]{:S(2)}) collective-permute-start(bf16[2,2,192,1024]{3,2,1,0:T(8,128)(2,1)} %fusion.33), channel_id=1, source_target_pairs={{0,4},{4,0},{8,12},{12,8},{16,20},{20,16},{24,28},{28,24},{1,5},{5... | collective-permute-start | bytes 4718600 | tf_op jit(solution)/shard_map/ppermute | solution.py:23
  1011.8 63.8 %copy-start.6 = (bf16[4,512,1024]{2,1,0:T(8,128)(2,1)S(1)}, bf16[4,512,1024]{2,1,0:T(8,128)(2,1)}, u32[]{:S(2)}) copy-start(bf16[4,512,1024]{2,1,0:T(8,128)(2,1)} %get-tuple-element.154) | copy-start | bytes 12582916
  1013.3 68.4 %slice-start.7 = ((s8[6291456]{0:T(1024)(128)(4,1)}), s8[2097152]{0:T(1024)(128)(4,1)S(1)}, s32[]{:S(2)}) async-start(s8[6291456]{0:T(1024)(128)(4,1)} %bitcast.322), calls=%async_computation.12 | async-start | bytes 4194304
  1075.6 39.2 %collective-permute-start.10 = (bf16[2,2,192,1024]{3,2,1,0:T(8,128)(2,1)}, bf16[2,2,192,1024]{3,2,1,0:T(8,128)(2,1)}, u32[]{:S(2)}, u32[]{:S(2)}) collective-permute-start(bf16[2,2,192,1024]{3,2,1,0:T(8,128)(2,1)} %pad_maximum_fusion.3), channel_id=1, source_target_pairs={{0,4},{4,0},{8,12},{12,8},{16,20},{20,16},{24,28},{28,24},{1,5},{5... | collective-permute-start | bytes 4718600 | tf_op jit(solution)/shard_map/ppermute | solution.py:23
  1075.6 6.1 slice-start.4
  1075.7 39.1 %collective-permute-start.13 = (bf16[2,2,192,1024]{3,2,1,0:T(8,128)(2,1)}, bf16[2,2,192,1024]{3,2,1,0:T(8,128)(2,1)}, u32[]{:S(2)}, u32[]{:S(2)}) collective-permute-start(bf16[2,2,192,1024]{3,2,1,0:T(8,128)(2,1)} %pad_maximum_fusion.4), channel_id=1, source_target_pairs={{0,4},{4,0},{8,12},{12,8},{16,20},{20,16},{24,28},{28,24},{1,5},{5... | collective-permute-start | bytes 4718600 | tf_op jit(solution)/shard_map/ppermute | solution.py:23
  1076.4 5.3 slice-start.5
  1076.4 30.5 %slice-start.2 = ((s8[6291456]{0:T(1024)(128)(4,1)}), s8[4194304]{0:T(1024)(128)(4,1)S(1)}, s32[]{:S(2)}) async-start(s8[6291456]{0:T(1024)(128)(4,1)} %bitcast.313), calls=%async_computation.7 | async-start | bytes 8388608
  1081.7 25.2 %slice-start.3 = ((s8[6291456]{0:T(1024)(128)(4,1)}), s8[2097152]{0:T(1024)(128)(4,1)S(1)}, s32[]{:S(2)}) async-start(s8[6291456]{0:T(1024)(128)(4,1)} %bitcast.313), calls=%async_computation.8 | async-start | bytes 4194304
  1083.9 27.4 %slice-start = ((s8[6291456]{0:T(1024)(128)(4,1)}), s8[4194304]{0:T(1024)(128)(4,1)S(1)}, s32[]{:S(2)}) async-start(s8[6291456]{0:T(1024)(128)(4,1)} %bitcast.309), calls=%async_computation.5 | async-start | bytes 8388608
  1084.1 27.3 %slice-start.1 = ((s8[6291456]{0:T(1024)(128)(4,1)}), s8[2097152]{0:T(1024)(128)(4,1)S(1)}, s32[]{:S(2)}) async-start(s8[6291456]{0:T(1024)(128)(4,1)} %bitcast.309), calls=%async_computation.6 | async-start | bytes 4194304
  1084.1 57.9 %collective-permute-start.7 = (bf16[8,64,768]{2,1,0:T(8,128)(2,1)S(1)}, bf16[8,64,768]{2,1,0:T(8,128)(2,1)S(1)}, u32[]{:S(2)}, u32[]{:S(2)}) collective-permute-start(bf16[8,64,768]{2,1,0:T(8,128)(2,1)S(1)} %fusion.45), channel_id=1, source_target_pairs={{0,2},{1,3},{2,0},{3,1},{4,6},{5,7},{6,4},{7,5},{8,10},{9,11},{10,... | collective-permute-start | bytes 2359304 | tf_op jit(solution)/shard_map/ppermute | solution.py:23
  1109.8 19.7 %collective-permute-start.1 = (bf16[2,192,1024]{2,1,0:T(8,128)(2,1)S(1)}, bf16[2,192,1024]{2,1,0:T(8,128)(2,1)S(1)}, u32[]{:S(2)}, u32[]{:S(2)}) collective-permute-start(bf16[2,192,1024]{2,1,0:T(8,128)(2,1)S(1)} %fusion.43), channel_id=1, source_target_pairs={{0,8},{4,12},{8,0},{12,4},{16,24},{20,28},{24,16},{28,20},{1,9},{5... | collective-permute-start | bytes 2359304 | tf_op jit(solution)/shard_map/ppermute | solution.py:23
  1114.2 20.5 %collective-permute-start.4 = (bf16[2,192,1024]{2,1,0:T(8,128)(2,1)S(1)}, bf16[2,192,1024]{2,1,0:T(8,128)(2,1)S(1)}, u32[]{:S(2)}, u32[]{:S(2)}) collective-permute-start(bf16[2,192,1024]{2,1,0:T(8,128)(2,1)S(1)} %fusion.44), channel_id=1, source_target_pairs={{0,16},{4,20},{8,24},{12,28},{16,0},{20,4},{24,8},{28,12},{1,17},{... | collective-permute-start | bytes 2359304 | tf_op jit(solution)/shard_map/ppermute | solution.py:23
  1121.4 30.4 %collective-permute-start.14 = (bf16[2,64,2048]{2,1,0:T(8,128)(2,1)S(1)}, bf16[2,64,2048]{2,1,0:T(8,128)(2,1)S(1)}, u32[]{:S(2)}, u32[]{:S(2)}) collective-permute-start(bf16[2,64,2048]{2,1,0:T(8,128)(2,1)S(1)} %fusion.51), channel_id=1, source_target_pairs={{0,1},{1,0},{2,3},{3,2},{4,5},{5,4},{6,7},{7,6},{8,9},{9,8},{10,11... | collective-permute-start | bytes 1572872 | tf_op jit(solution)/shard_map/ppermute | solution.py:23
  1130.1 22.7 %collective-permute-start.2 = (bf16[192,1024]{1,0:T(8,128)(2,1)S(1)}, bf16[192,1024]{1,0:T(8,128)(2,1)S(1)}, u32[]{:S(2)}, u32[]{:S(2)}) collective-permute-start(bf16[192,1024]{1,0:T(8,128)(2,1)S(1)} %fusion.52), channel_id=1, source_target_pairs={{0,16},{4,20},{8,24},{12,28},{16,0},{20,4},{24,8},{28,12},{1,17},{... | collective-permute-start | bytes 1179656 | tf_op jit(solution)/shard_map/ppermute | solution.py:23
  1135.3 17.7 %collective-permute-start.5 = (bf16[192,1024]{1,0:T(8,128)(2,1)S(1)}, bf16[192,1024]{1,0:T(8,128)(2,1)S(1)}, u32[]{:S(2)}, u32[]{:S(2)}) collective-permute-start(bf16[192,1024]{1,0:T(8,128)(2,1)S(1)} %fusion.53), channel_id=1, source_target_pairs={{0,8},{4,12},{8,0},{12,4},{16,24},{20,28},{24,16},{28,20},{1,9},{5... | collective-permute-start | bytes 1179656 | tf_op jit(solution)/shard_map/ppermute | solution.py:23
  1152.8 21.9 %collective-permute-start.15 = (bf16[64,2048]{1,0:T(8,128)(2,1)}, bf16[64,2048]{1,0:T(8,128)(2,1)}, u32[]{:S(2)}, u32[]{:S(2)}) collective-permute-start(bf16[64,2048]{1,0:T(8,128)(2,1)} %fusion.54), channel_id=1, source_target_pairs={{0,2},{1,3},{2,0},{3,1},{4,6},{5,7},{6,4},{7,5},{8,10},{9,11},{10,... | collective-permute-start | bytes 786440 | tf_op jit(solution)/shard_map/ppermute | solution.py:23
  1155.3 11.7 all-to-all-start.1
  1167.0 16.8 %all-to-all-start.4 = ((bf16[8,64,768]{2,1,0:T(8,128)(2,1)}), bf16[8,64,768]{2,1,0:T(8,128)(2,1)}, u32[]{:S(2)}, u32[]{:S(2)}) async-start(bf16[8,64,768]{2,1,0:T(8,128)(2,1)} %fusion.39), calls=%async_computation.4 | async-start | bytes 1572864 | tf_op jit(solution)/shard_map/all_to_all | solution.py:87
  (35 other events, 75.0 us)

commit v4 on v3

--- a/solution.py
+++ b/solution.py
@@ -18,130 +18,8 @@
 exact = jnp.float32
 
 
-def swap(x, axis, bit):
-    length = lax.axis_size(axis)
-    return lax.ppermute(x, axis, [(i, i ^ bit) for i in range(length)])
-
-
-def bits_of(axis):
-    length = lax.axis_size(axis)
-    return [1 << i for i in range(length.bit_length() - 1)]
-
-
-def doubled(x, axis, bits):
-    index = lax.axis_index(axis)
-    for bit in bits:
-        other = swap(x, axis, bit)
-        high = (index & bit) != 0
-        x = jnp.stack([jnp.where(high, other, x), jnp.where(high, x, other)])
-    count = len(bits)
-    order = sorted(range(count), key=lambda i: -bits[count - 1 - i])
-    x = x.transpose(order + list(range(count, x.ndim)))
-    return x.reshape((1 << count,) + x.shape[count:])
-
-
-def gather_ctx(x):
-    bits = bits_of("ctx")
-    half = x.shape[-1] // 2
-    far = bits[1:]
-    one = doubled(x[..., :half], "ctx", far + bits[:1])
-    two = doubled(x[..., half:], "ctx", far[::-1] + bits[:1])
-    return jnp.concatenate([one, two], axis=-1)
-
-
-def spread(x):
-    index = lax.axis_index("fsdp")
-    out = x
-    for step in range(1, x.shape[0]):
-        piece = lax.dynamic_index_in_dim(x, index ^ step, 0, True)
-        out = lax.dynamic_update_slice_in_dim(out, swap(piece, "fsdp", step), index ^ step, 0)
-    return out
-
-
-def halved(x, axis, bits):
-    index = lax.axis_index(axis)
-    count = len(bits)
-    x = x.reshape((2,) * count + x.shape[1:])
-    left = sorted(bits, reverse=True)
-    for bit in bits:
-        at = left.index(bit)
-        left.remove(bit)
-        zero = lax.index_in_dim(x, 0, at, keepdims=False)
-        one = lax.index_in_dim(x, 1, at, keepdims=False)
-        high = (index & bit) != 0
-        got = swap(jnp.where(high, zero, one).astype(low), axis, bit)
-        x = jnp.where(high, one, zero).astype(exact) + got.astype(exact)
-    return x
-
-
-def scatter_ctx(x):
-    bits = bits_of("ctx")
-    half = x.shape[-1] // 2
-    far = bits[1:]
-    one = halved(x[..., :half], "ctx", bits[:1] + far)
-    two = halved(x[..., half:], "ctx", bits[:1] + far[::-1])
-    return jnp.concatenate([one, two], axis=-1)
-
-
 def exchange(x, axis):
     return lax.all_to_all(x, axis, split_axis=0, concat_axis=0, tiled=True)
-
-
-def rms_apply(vector, gain):
-    scale = lax.rsqrt(jnp.mean(vector * vector, axis=-1, keepdims=True) + epsilon)
-    normed = vector * scale
-    return (normed * gain, normed, scale)
-
-
-def rms_back(grad, normed, scale, gain):
-    dnormed = grad * gain
-    gain_grad = jnp.sum(grad * normed, axis=0)
-    inner = jnp.mean(dnormed * normed, axis=-1, keepdims=True)
-    return (scale * (dnormed - normed * inner), gain_grad)
-
-
-def rotation(positions, head_size):
-    half = head_size // 2
-    freq = 10000.0 ** (-jnp.arange(half, dtype=jnp.float32) * (2.0 / head_size))
-    angle = positions.astype(jnp.float32)[:, None] * freq[None, :]
-    return (jnp.cos(angle)[:, None, :], jnp.sin(angle)[:, None, :])
-
-
-def rotate(vector, cosine, sine):
-    half = vector.shape[-1] // 2
-    first = vector[..., :half]
-    second = vector[..., half:]
-    return jnp.concatenate(
-        [first * cosine - second * sine, second * cosine + first * sine], axis=-1
-    )
-
-
-def dot(left, right):
-    return jnp.dot(left, right, preferred_element_type=exact)
-
-
-def contract_rows(left, right):
-    return lax.dot_general(
-        left, right, (((0,), (0,)), ((), ())), preferred_element_type=exact
-    )
-
-
-def contract_cols(left, right):
-    return lax.dot_general(
-        left, right, (((1,), (1,)), ((), ())), preferred_element_type=exact
-    )
-
-
-def ordered(x, ctx_count):
-    x = x.reshape((ctx_count, 2, -1) + x.shape[1:])
-    x = jnp.concatenate([x[:, 0], x[::-1, 1]], axis=0)
-    return x.reshape((-1,) + x.shape[2:])
-
-
-def placed(x, ctx_count):
-    x = x.reshape((2 * ctx_count, -1) + x.shape[1:])
-    x = jnp.stack([x[:ctx_count], x[ctx_count:][::-1]], axis=1)
-    return x.reshape((-1,) + x.shape[3:])
 
 
 def bits_down(count):
@@ -973,6 +851,391 @@
     )(rows, cot_rows, router_t, routes, wg, wu, wd, near, cot_near, r1, gains)
 
 
+def back_kernel(
+    cfg,
+    x_ref, dr1_ref, datt_ref, a1_ref, w_ref, raw_ref, stat_ref, rot_ref, ob_ref, wo_ref, gain_ref, fgain_ref,
+    gu_ref, cos_ref, sin_ref,
+    hidden_out, w_out, wo_out, gains_out, gu_land, pair_land, chip_land, wz_land, oz_land,
+    wo, datt, a1, w, raw, rot, ob, dland, aq, ak, av, rq, rk, cq, ck, stat, total, dqkv, gw, go, gsum,
+    wtemp, otemp, wsum, wl, xrow, xtemp, small_z, small_c,
+    sends, recvs, locals_,
+):
+    nc, nz, tokens, width = cfg["nc"], cfg["nz"], cfg["tokens"], cfg["width"]
+    cols, rows_w, length = cfg["cols"], cfg["rows_w"], cfg["length"]
+    hs = 128
+    heads = cols // hs
+    half = tokens // 2
+    block = cfg["block"]
+    blocks = length // block
+    c, z = lax.axis_index("ctx"), lax.axis_index("fsdp")
+    links = Links(sends, recvs, locals_)
+    ds = pl.ds
+    best = lax.Precision.HIGHEST
+    same = [d for d in range(2, nc, 2)]
+    own_rows = ds(pl.multiple_of(c * tokens, tokens), tokens)
+
+    wo_in = links.move(wo_ref, wo)
+    datt_in = links.move(datt_ref, datt.at[own_rows])
+    first = [links.move(rot_ref, rot), links.move(raw_ref.at[:, 0 : 2 * cols], raw), links.move(ob_ref, ob)]
+    later = [links.move(w_ref, w), links.move(x_ref, xrow)]
+    up_own = links.move(gu_ref.at[z], gu_land.at[z])
+    greet(c, z, nc, nz)
+    up_sends = [links.send(gu_ref.at[z ^ s], gu_land.at[z], fsdp=z ^ s) for s in range(1, nz)]
+    links.left(datt_in)
+    links.left(wo_in)
+
+    heads_sent = []
+    for d in range(1, nc):
+        at = pl.multiple_of((c ^ d) * cols, cols)
+        spot = dqkv.at[d * tokens : (d + 1) * tokens, 0:cols]
+        spot[...] = kdot(datt[own_rows, :], wo[ds(at, cols), :], ((1,), (1,))).astype(low)
+        heads_sent.append(links.send(spot, dland.at[c], ctx=c ^ d))
+    at = pl.multiple_of(c * cols, cols)
+    dland[c] = kdot(datt[own_rows, :], wo[ds(at, cols), :], ((1,), (1,))).astype(low)
+    rows_same = {d: links.send(datt.at[own_rows], datt.at[own_rows], ctx=c ^ d) for d in same}
+    rows_side = [links.send(datt.at[own_rows], datt.at[own_rows], ctx=c ^ 1)]
+    for copy in first:
+        links.left(copy)
+
+    row8 = lax.broadcasted_iota(jnp.int32, (8, hs), 0)
+
+    def columns(src, one, two, finish):
+        def step(i, _):
+            at = pl.multiple_of(i * block, block)
+            part = src[:, ds(at, block)]
+            for row, dst in ((0, one), (1, two)):
+                sel = jnp.where(row8 == row, 1.0, 0.0)
+                dst[ds(at, block), :] = finish(kdot(part, sel, ((0,), (0,)), best) / width)
+            return 0
+
+        lax.fori_loop(0, blocks, step, 0)
+
+    columns(stat_ref, rq, rk, lambda v: lax.rsqrt(v + epsilon))
+    ak[...] = jnp.zeros_like(ak)
+    av[...] = jnp.zeros_like(av)
+    gsum[...] = jnp.zeros_like(gsum)
+    for copy in heads_sent:
+        links.arrived(copy)
+    for copy in heads_sent:
+        links.left(copy)
+
+    def place(i, _):
+        d, side = i // 2, i % 2
+        at = pl.multiple_of(side * half, half)
+        to = pl.multiple_of(jnp.where(side == 0, d, 2 * nc - 1 - d) * half, half)
+        aq[ds(to, half), :] = dland[d, ds(at, half), :].astype(exact)
+        return 0
+
+    lax.fori_loop(0, 2 * nc, place, 0)
+    for d in same:
+        links.arrived(rows_same[d])
+        there = datt.at[ds(pl.multiple_of((c ^ d) * tokens, tokens), tokens)]
+        rows_side.append(links.send(there, there, ctx=c ^ 1))
+
+    scale = hs ** -0.5
+    for h in range(heads):
+        lanes = slice(h * hs, (h + 1) * hs)
+        for i in range(blocks):
+            count = (i + 1) * block
+            here = slice(i * block, count)
+            q, k, v = rot[0, here, lanes], rot[1, :count, lanes], rot[2, :count, lanes]
+            do = aq[here, lanes].astype(low)
+            s = kdot(q, k, ((1,), (1,))) * scale
+            row = lax.broadcasted_iota(jnp.int32, (block, count), 0) + i * block
+            col = lax.broadcasted_iota(jnp.int32, (block, count), 1)
+            s = jnp.where(col <= row, s, neg_large)
+            p = jnp.exp(s - jnp.max(s, axis=-1, keepdims=True))
+            p = p * (1.0 / jnp.sum(p, axis=-1, keepdims=True))
+            dp = kdot(do, v, ((1,), (1,)))
+            delta = jnp.sum(p * dp, axis=-1, keepdims=True)
+            dscore = (p * (dp - delta)).astype(low)
+            av[:count, lanes] += kdot(p.astype(low), do, ((0,), (0,)))
+            ak[:count, lanes] += kdot(dscore, q, ((0,), (0,))) * scale
+            aq[here, lanes] = kdot(dscore, k) * scale
+
+    def unturn(i, _):
+        d, side = i // 2, i % 2
+        at = pl.multiple_of(d * tokens + side * half, half)
+        to = pl.multiple_of(jnp.where(side == 0, d, 2 * nc - 1 - d) * half, half)
+        cosine, sine = cos_ref[ds(at, half), :], sin_ref[ds(at, half), :]
+        for j, acc, scale_ref, sums in ((0, aq, rq, cq), (1, ak, rk, ck)):
+            row_sum = jnp.zeros((half, 1), exact)
+            for h in range(heads):
+                lanes = slice(h * hs, (h + 1) * hs)
+                lane = j * cols + h * hs
+                v = acc[ds(to, half), lanes]
+                v = v * cosine - pltpu.roll(v, hs // 2, 1) * sine
+                acc[ds(to, half), lanes] = v
+                normed = raw[ds(at, half), lane : lane + hs] * scale_ref[ds(at, half), :]
+                v = v * normed
+                gsum[j : j + 1, lanes] += jnp.sum(v, axis=0, keepdims=True)
+                gain = gain_ref[1 + j : 2 + j, ds(pl.multiple_of(c * cols + h * hs, hs), hs)]
+                row_sum += jnp.sum(v * gain, axis=-1, keepdims=True)
+            sums[ds(at, half), :] = jnp.broadcast_to(row_sum, (half, hs))
+        return 0
+
+    lax.fori_loop(0, 2 * nc, unturn, 0)
+    lane8 = lax.broadcasted_iota(jnp.int32, (8, hs), 1)
+
+    def gather_sums(i, _):
+        at = pl.multiple_of(i * block, block)
+        part = jnp.zeros((8, block), exact)
+        for row, src in ((0, cq), (1, ck)):
+            sel = jnp.where((row8 == row) & (lane8 == 0), 1.0, 0.0)
+            part += kdot(sel, src[ds(at, block), :], ((1,), (1,)), best)
+        stat[c, :, ds(at, block)] = part
+        return 0
+
+    lax.fori_loop(0, blocks, gather_sums, 0)
+    stats = [links.send(stat.at[c], stat.at[c], ctx=c ^ d) for d in range(1, nc)]
+
+    for copy in rows_side:
+        links.arrived(copy)
+    tile = width // nc
+    tile_base = links.local_count
+    links.local_count += nc
+
+    def tile_load(k):
+        return pltpu.make_async_copy(
+            a1_ref.at[:, ds(k * tile, tile)], a1.at[lax.rem(k, 2)], locals_.at[tile_base + k]
+        )
+
+    tile_load(0).start()
+
+    def out_tile(k, _):
+        at = pl.multiple_of(k * tile, tile)
+        v = kdot(ob[...], datt[:, ds(at, tile)], ((0,), (0,))).astype(low)
+        go[:, :, ds(at, tile)] = v.reshape(nz, rows_w, tile)
+        return 0
+
+    lax.fori_loop(0, nc, out_tile, 0)
+    for copy in stats:
+        links.arrived(copy)
+    summed = stat[0]
+    for k in range(1, nc):
+        summed += stat[k]
+    total[...] = summed
+    columns(total, cq, ck, lambda v: v)
+
+    def finish(i, _):
+        d, side = i // 2, i % 2
+        at = pl.multiple_of(d * tokens + side * half, half)
+        to = pl.multiple_of(jnp.where(side == 0, d, 2 * nc - 1 - d) * half, half)
+        for j, acc, scale_ref, sums in ((0, aq, rq, cq), (1, ak, rk, ck)):
+            for h in range(heads):
+                lanes = slice(h * hs, (h + 1) * hs)
+                lane = j * cols + h * hs
+                gain = gain_ref[1 + j : 2 + j, ds(pl.multiple_of(c * cols + h * hs, hs), hs)]
+                normed = raw[ds(at, half), lane : lane + hs] * scale_ref[ds(at, half), :]
+                v = acc[ds(to, half), lanes] * gain - normed * sums[ds(at, half), :]
+                dqkv[ds(at, half), lane : lane + hs] = (v * scale_ref[ds(at, half), :]).astype(low)
+        dqkv[ds(at, half), 2 * cols : 3 * cols] = av[ds(to, half), :].astype(low)
+        return 0
+
+    lax.fori_loop(0, 2 * nc, finish, 0)
+    for copy in later:
+        links.left(copy)
+    for copy in list(rows_same.values()) + rows_side:
+        links.left(copy)
+
+    def w_tile(k, _):
+        @pl.when(k + 1 < nc)
+        def _():
+            tile_load(k + 1).start()
+
+        tile_load(k).wait()
+        v = kdot(a1[lax.rem(k, 2)], dqkv[...], ((0,), (0,))).astype(low)
+        for j in range(3):
+            gw[j, k] = v[:, j * cols : (j + 1) * cols].reshape(nz, rows_w, cols)
+        return 0
+
+    lax.fori_loop(0, nc, w_tile, 0)
+    home = {}
+
+    def send_home(s):
+        peer = z ^ (s & -s)
+        home[s] = (
+            links.send(gw.at[:, :, z ^ s], wz_land.at[s], fsdp=peer),
+            links.send(go.at[z ^ s], oz_land.at[s], fsdp=peer),
+        )
+
+    def taken(s):
+        w_sum = gw[:, :, z ^ s].astype(exact)
+        o_sum = go[z ^ s].astype(exact)
+        bit = 1
+        while bit < nz and (s == 0 or bit < (s & -s)):
+            for copy in home[s | bit]:
+                links.arrived(copy)
+            got = [links.move(wz_land.at[s | bit], wtemp), links.move(oz_land.at[s | bit], otemp)]
+            for copy in got:
+                links.left(copy)
+            w_sum += wtemp[...].astype(exact)
+            o_sum += otemp[...].astype(exact)
+            bit *= 2
+        return w_sum, o_sum
+
+    for s in range(nz - 1, 0, -1):
+        if s & 1:
+            send_home(s)
+
+    def partial(k):
+        at = pl.multiple_of(k * tokens, tokens)
+        v = jnp.zeros((tokens, width), exact)
+        for j in range(3):
+            v += kdot(dqkv[ds(at, tokens), j * cols : (j + 1) * cols], w[j], ((1,), (1,)))
+        datt[ds(at, tokens), :] = v.astype(low)
+
+    def rows_of(k):
+        return datt.at[ds(pl.multiple_of(k * tokens, tokens), tokens)]
+
+    evens = [0] + same
+    pair, chip = {}, {}
+
+    def other_core(m, _):
+        partial(2 * m + 1 - lax.rem(c, 2))
+        return 0
+
+    def this_core(m, _):
+        partial(2 * m + lax.rem(c, 2))
+        return 0
+
+    lax.fori_loop(0, nc // 2, other_core, 0)
+    for m, d in enumerate(evens):
+        pair[d] = links.send(rows_of((c ^ 1) ^ d), pair_land.at[m], ctx=c ^ 1)
+    lax.fori_loop(0, nc // 2, this_core, 0)
+    for m, d in list(enumerate(evens))[::-1]:
+        links.arrived(pair[d])
+        got = links.move(pair_land.at[m], xtemp)
+        links.left(got)
+        mine = rows_of(c ^ d)
+        if d:
+            mine[...] = (mine[...].astype(exact) + xtemp[...].astype(exact)).astype(low)
+            chip[d] = links.send(mine, chip_land.at[m], ctx=c ^ d)
+        else:
+            grad_in = mine[...].astype(exact) + xtemp[...].astype(exact)
+            hidden_out[...] = grad_in
+
+    for s in range(nz - 2, 0, -1):
+        if not s & 1:
+            w_sum, o_sum = taken(s)
+            gw[:, :, z ^ s] = w_sum.astype(low)
+            go[z ^ s] = o_sum.astype(low)
+            send_home(s)
+
+    for m, d in enumerate(evens):
+        if d:
+            links.arrived(chip[d])
+            got = links.move(chip_land.at[m], xtemp)
+            links.left(got)
+            hidden_out[...] += xtemp[...].astype(exact)
+    x = xrow[...].astype(exact)
+    rs = lax.rsqrt(jnp.mean(x * x, axis=-1, keepdims=True) + epsilon)
+    n1 = x * rs
+    grad_in = hidden_out[...]
+    gains_out[...] = jnp.zeros_like(gains_out)
+    gains_out[0:1, :] = jnp.sum(grad_in * n1, axis=0, keepdims=True)
+    for j in range(2):
+        own_lanes = ds(pl.multiple_of(c * cols, cols), cols)
+        gains_out[1 + j : 2 + j, own_lanes] = gsum[j : j + 1, :]
+    gains_out[3:4, :] = fgain_ref[0:1, :]
+    dn = grad_in * gain_ref[0:1, :]
+    hidden_out[...] = dr1_ref[...] + rs * (dn - n1 * jnp.mean(dn * n1, axis=-1, keepdims=True))
+
+    small_z[0] = gains_out[...]
+    z_sums = [links.send(small_z.at[0], small_z.at[s], fsdp=z ^ s) for s in range(1, nz)]
+    for copy in z_sums:
+        links.arrived(copy)
+    v = small_z[0]
+    for s in range(1, nz):
+        v += small_z[s]
+    small_c[0] = v
+    c_sums = [links.send(small_c.at[0], small_c.at[d], ctx=c ^ d) for d in range(1, nc)]
+    for copy in c_sums:
+        links.arrived(copy)
+    v = small_c[0]
+    for d in range(1, nc):
+        v += small_c[d]
+    gains_out[...] = v
+
+    w_sum, o_sum = taken(0)
+    wo_out[...] = o_sum
+    wsum[...] = w_sum.astype(low)
+    w_home = [links.send(wsum.at[:, c ^ d], wl.at[:, c], ctx=c ^ d) for d in range(1, nc)]
+    w_own = links.move(wsum.at[:, c], wl.at[:, c])
+    for copy in w_home:
+        links.arrived(copy)
+    links.left(w_own)
+    for j in range(3):
+        for k in range(nc):
+            w_out[j, :, k * cols : (k + 1) * cols] = wl[j, k].astype(exact)
+    for copy in up_sends:
+        links.arrived(copy)
+    links.close()
+
+
+def run_back(cfg, x, dr1, datt, a1, w, raw, stat, rot, ob, wo, gains, fgain, gu, cosine, sine):
+    nc, nz, tokens, width = cfg["nc"], cfg["nz"], cfg["tokens"], cfg["width"]
+    cols, rows_w, length = cfg["cols"], cfg["rows_w"], cfg["length"]
+    shape = jax.ShapeDtypeStruct
+    any_, vmem = pl.BlockSpec(memory_space=pl.ANY), pl.BlockSpec(memory_space=pltpu.VMEM)
+    outs = [
+        (shape((tokens, width), exact), vmem),
+        (shape((3, rows_w, width), exact), vmem),
+        (shape((rows_w, width), exact), vmem),
+        (shape((8, width), exact), vmem),
+        (shape(gu.shape, low), any_),
+        (shape((nc // 2, tokens, width), low), any_),
+        (shape((nc // 2, tokens, width), low), any_),
+        (shape((nz, 3, nc, rows_w, cols), low), any_),
+        (shape((nz, rows_w, width), low), any_),
+    ]
+    scratch = [
+        pltpu.VMEM((width, width), low),
+        pltpu.VMEM((length, width), low),
+        pltpu.VMEM((2, length, width // nc), low),
+        pltpu.VMEM((3, width, cols), low),
+        pltpu.VMEM((length, 2 * cols), exact),
+        pltpu.VMEM((3, length, cols), low),
+        pltpu.VMEM((length, cols), low),
+        pltpu.VMEM((nc, tokens, cols), low),
+        pltpu.VMEM((length, cols), exact),
+        pltpu.VMEM((length, cols), exact),
+        pltpu.VMEM((length, cols), exact),
+        pltpu.VMEM((length, 128), exact),
+        pltpu.VMEM((length, 128), exact),
+        pltpu.VMEM((length, 128), exact),
+        pltpu.VMEM((length, 128), exact),
+        pltpu.VMEM((nc, 8, length), exact),
+        pltpu.VMEM((8, length), exact),
+        pltpu.VMEM((length, 3 * cols), low),
+        pltpu.VMEM((3, nc, nz, rows_w, cols), low),
+        pltpu.VMEM((nz, rows_w, width), low),
+        pltpu.VMEM((8, cols), exact),
+        pltpu.VMEM((3, nc, rows_w, cols), low),
+        pltpu.VMEM((rows_w, width), low),
+        pltpu.VMEM((3, nc, rows_w, cols), low),
+        pltpu.VMEM((3, nc, rows_w, cols), low),
+        pltpu.VMEM((tokens, width), low),
+        pltpu.VMEM((tokens, width), low),
+        pltpu.VMEM((nz, 8, width), exact),
+        pltpu.VMEM((nc, 8, width), exact),
+        pltpu.SemaphoreType.DMA((8 * nc + 8 * nz,)),
+        pltpu.SemaphoreType.DMA((8 * nc + 8 * nz,)),
+        pltpu.SemaphoreType.DMA((4 * nc + 8 * nz + 16,)),
+    ]
+    return pl.pallas_call(
+        functools.partial(back_kernel, cfg),
+        out_shape=[o[0] for o in outs],
+        in_specs=[any_, vmem, any_, any_, any_, any_, vmem, any_, any_, any_, vmem, vmem, any_, vmem, vmem],
+        out_specs=[o[1] for o in outs],
+        scratch_shapes=scratch,
+        compiler_params=pltpu.CompilerParams(
+            collective_id=2, has_side_effects=True, vmem_limit_bytes=cfg["vmem"]
+        ),
+        name="back",
+    )(x, dr1, datt, a1, w, raw, stat, rot, ob, wo, gains, fgain, gu, cosine, sine)
+
+
 def tables(nc, tokens, head_size):
     half = tokens // 2
     local = np.arange(tokens)
@@ -1017,10 +1280,8 @@
     part = hidden // split
     experts = exp_local * ctx_count
     capacity = tokens * top * 4 // (3 * experts)
-    heads = HEADS // ctx_count
-    cols = heads * head_size
+    cols = HEADS // ctx_count * head_size
     length = tokens * ctx_count
-    scale = head_size ** (-0.5)
     c_index = lax.axis_index("ctx")
     z_index = lax.axis_index("fsdp")
     rows_w = w_query.shape[0]
@@ -1057,6 +1318,7 @@
         weight = weight.reshape(exp_local, rows, z_count, split, part // z_count)
         return weight.transpose(0, 3, 1, 2, 4).reshape(z_count, rows, part)
 
+    cosine, sine = tables(ctx_count, tokens, head_size)
     (
         attn_all, w_full, raw, squares, rot, out_heads, wo_full, resid_one,
         router_full, gains, routes_all, gate_full, up_full, down_full, cot_rows, cot_near,
@@ -1064,7 +1326,7 @@
     ) = front(
         cfg, hidden_in[0], w_query, w_key, w_value, w_out, gains, router_tile, route_tile,
         cotangent[0], pieces_of(w_gate), pieces_of(w_up),
-        w_down.reshape(z_count, -1, width), *tables(ctx_count, tokens, head_size),
+        w_down.reshape(z_count, -1, width), cosine, sine,
     )
     gate_full = gate_full.reshape(-1, part)
     up_full = up_full.reshape(-1, part)
@@ -1079,7 +1341,6 @@
         gate_full, up_full, down_full, input_near, cot_near, resid_one, gains,
     )
     out_hidden = resid_two[None]
-    ffn_gain_grad = ffn_gain_grad[0]
     router_grad = lax.dot_general(
         ffn_input, logit_grad[:experts], (((0,), (1,)), ((), ())), preferred_element_type=exact
     )
@@ -1090,113 +1351,27 @@
 
     grad_down = down_land.reshape(exp_local, -1, width).astype(exact)
     grad_gate = whole_out(gate_land)
-    grad_up = whole_out(spread(up_grad.reshape(z_count, -1, part)))
-    w_full = w_full.reshape(3, width, cols)
-    out_full = wo_full.reshape(width, width)
-    attn_scale = gains[0]
-    query_scale = lax.dynamic_slice_in_dim(gains[1], c_index * cols, cols)
-    key_scale = lax.dynamic_slice_in_dim(gains[2], c_index * cols, cols)
-    def total_over_ctx(one, two):
-        both_sums = jnp.stack([one, two])
-        return jnp.sum(lax.all_gather(both_sums, "ctx", axis=0), axis=0)
-
-    queries, keys = raw[:, :cols], raw[:, cols : 2 * cols]
-    rms_two = lax.rsqrt(squares[:2] / width + epsilon)
-    query_rms, key_rms = rms_two[0][:, None], rms_two[1][:, None]
-    query_normed, key_normed = queries * query_rms, keys * key_rms
-    half = tokens // 2
-    row = jnp.arange(length, dtype=jnp.int32)
-    device, local = row // tokens, row % tokens
-    positions = jnp.where(
-        local < half, device * half + local, (2 * ctx_count - 1 - device) * half + local - half
+    grad_hidden, w_grads, grad_out, gain_grads, up_land, *_ = run_back(
+        cfg, hidden_in[0], grad_one, attn_grad_low, attn_all, w_full.reshape(3, width, cols), raw,
+        squares, rot, out_heads, wo_full.reshape(width, width), gains, ffn_gain_grad,
+        up_grad.reshape(z_count, -1, part), cosine, sine,
     )
-    cosine, sine = rotation(positions, head_size)
-
-    def by_head(x):
-        return x.reshape(length, heads, head_size)
-
-    query_rot, key_rot, value_low = by_head(rot[0]), by_head(rot[1]), by_head(rot[2])
-    allowed = (row[None, :] <= row[:, None])[None]
-    scores = (
-        jnp.einsum("qhd,khd->hqk", query_rot, key_rot, preferred_element_type=exact) * scale
-    )
-    scores = jnp.where(allowed, scores, neg_large)
-    log_total = jax.nn.logsumexp(scores, axis=-1, keepdims=True)
-    probs = jnp.exp(scores - log_total)
-    probs_low = probs.astype(low)
-    rows_in = hidden_in[0].astype(exact)
-    attn_grad_all = gather_ctx(attn_grad_low).reshape(length, width)
-    out_weight_grad = contract_rows(out_heads, attn_grad_all)
-    grad_heads = contract_cols(attn_grad_low, out_full).astype(low)
-    grad_heads = exchange(grad_heads.reshape(tokens, ctx_count, cols).transpose(1, 0, 2), "ctx")
-    grad_heads = ordered(by_head(grad_heads), ctx_count)
-    value_grad = jnp.einsum("hqk,qhd->khd", probs_low, grad_heads, preferred_element_type=exact)
-    prob_grad = jnp.einsum("qhd,khd->hqk", grad_heads, value_low, preferred_element_type=exact)
-    delta = jnp.sum(probs * prob_grad, axis=-1, keepdims=True)
-    score_grad = (probs * (prob_grad - delta)).astype(low)
-    query_rot_grad = scale * jnp.einsum(
-        "hqk,khd->qhd", score_grad, key_rot, preferred_element_type=exact
-    )
-    key_rot_grad = scale * jnp.einsum(
-        "hqk,qhd->khd", score_grad, query_rot, preferred_element_type=exact
-    )
-    query_back = rotate(placed(query_rot_grad, ctx_count), cosine, -sine).reshape(length, cols)
-    key_back = rotate(placed(key_rot_grad, ctx_count), cosine, -sine).reshape(length, cols)
-    value_grad_low = placed(value_grad.astype(low), ctx_count).reshape(length, cols)
-    query_gain_grad = jnp.sum(query_back * query_normed, axis=0)
-    key_gain_grad = jnp.sum(key_back * key_normed, axis=0)
-    query_d, key_d = query_back * query_scale, key_back * key_scale
-    inner_two = total_over_ctx(
-        jnp.sum(query_d * query_normed, -1), jnp.sum(key_d * key_normed, -1)
-    ) / width
-    query_grad_low = (query_rms * (query_d - query_normed * inner_two[0][:, None])).astype(low)
-    key_grad_low = (key_rms * (key_d - key_normed * inner_two[1][:, None])).astype(low)
-    qkv_grad_low = jnp.concatenate([query_grad_low, key_grad_low, value_grad_low], axis=1)
-    attn_input_grad = (
-        contract_cols(query_grad_low, w_full[0])
-        + contract_cols(key_grad_low, w_full[1])
-        + contract_cols(value_grad_low, w_full[2])
-    )
-    qkv_weight_grad = contract_rows(attn_all, qkv_grad_low)
-    attn_input_grad = scatter_ctx(attn_input_grad.reshape(ctx_count, tokens, width))
-    _, normed_one, scale_one = rms_apply(rows_in, attn_scale)
-    input_norm_grad, attn_gain_grad = rms_back(
-        attn_input_grad, normed_one, scale_one, attn_scale
-    )
-    grad_hidden = (grad_one + input_norm_grad)[None]
-
-    z_bits = bits_of("fsdp")
-    pieces = qkv_weight_grad.reshape(ctx_count, z_count, rows_w, 3 * cols).transpose(1, 0, 2, 3)
-    pieces = halved(pieces, "fsdp", z_bits).astype(low)
-    pieces = exchange(pieces, "ctx").reshape(ctx_count, rows_w, 3, cols).astype(exact)
-    pieces = pieces.transpose(2, 1, 0, 3).reshape(3, rows_w, width)
-    grad_out = halved(out_weight_grad.reshape(z_count, rows_w, width), "fsdp", z_bits)
-    sums = jnp.concatenate(
-        [
-            router_grad.reshape(ctx_count * z_count, rows_w * experts),
-            ffn_gain_grad.reshape(-1, rows_w),
-        ],
-        axis=1,
-    )
+    grad_up = whole_out(up_land)
+    gain_grads = lax.dynamic_slice_in_dim(gain_grads, index * rows_w, rows_w, 1)
+    sums = router_grad.reshape(ctx_count * z_count, rows_w * experts)
     sums = jnp.sum(exchange(sums, both), axis=0)
-    grad_router = sums[: rows_w * experts].reshape(rows_w, experts)
-    grad_ffn_gain = sums[rows_w * experts :]
-    grad_attn_gain = jnp.sum(exchange(attn_gain_grad.reshape(-1, rows_w), both), axis=0)
-    head_gains = jnp.stack([query_gain_grad, key_gain_grad], axis=1)
-    head_gains = head_gains.reshape(z_count, rows_w, 2)
-    head_gains = jnp.sum(exchange(head_gains, "fsdp"), axis=0)
     return (
         out_hidden,
-        grad_hidden,
-        grad_attn_gain,
-        head_gains[:, 0],
-        head_gains[:, 1],
-        grad_ffn_gain,
-        pieces[0],
-        pieces[1],
-        pieces[2],
+        grad_hidden[None],
+        gain_grads[0],
+        gain_grads[1],
+        gain_grads[2],
+        gain_grads[3],
+        w_grads[0],
+        w_grads[1],
+        w_grads[2],
         grad_out,
-        grad_router,
+        sums.reshape(rows_w, experts),
         grad_gate,
         grad_up,
         grad_down,

time: 1200 us -> 1020 us (0.85)
  Pallas kernels: 779 us -> 974 us
  waiting for transfers between devices: 102 us -> 0.01 us
  other arithmetic: 98.3 us -> 16.6 us
  matrix products: 73.2 us -> 1.62 us
  local copies, waits for them, and re-layouts: 69.3 us -> 11.6 us
  starting transfers between devices: 60.2 us -> 3.48 us
    pallas_call x0 -> x1, Pallas kernels: none -> 194 us  [run_back(): pl.pallas_call(functools.partial(back_kernel, cfg), out_shape=[o[0] for o...]
    ppermute x19 -> x0, waiting for transfers between devices: 87.4 us -> none  [swap(): return lax.ppermute(x, axis, [(i, i ^ bit) for i in range(length)])]
    dot_general x11 -> x0, matrix products: 71.6 us -> none  [the longest x4 25.7 us: contract_cols(): lax.dot_general(left, right, (((1,), (1,)), ((), ())), preferred_element_...]
    ppermute x19 -> x0, starting transfers between devices: 40.1 us -> none  [swap(): return lax.ppermute(x, axis, [(i, i ^ bit) for i in range(length)])]
    slice x24 -> x0, local copies, waits for them, and re-layouts: 31.2 us -> none  [the longest x9 11.1 us: placed(): x = jnp.stack([x[:ctx_count], x[ctx_count:][::-1]], axis=1)]
    convert_element_type x14 -> x0, other arithmetic: 30 us -> none  [the longest x1 13.3 us: body(): score_grad = (probs * (prob_grad - delta)).astype(low)]
    all_to_all x5 -> x1, starting transfers between devices: 20.1 us -> 3.48 us  [exchange(): return lax.all_to_all(x, axis, split_axis=0, concat_axis=0, tiled=True)]
    all_to_all x5 -> x1, waiting for transfers between devices: 14.8 us -> 0.01 us  [exchange(): return lax.all_to_all(x, axis, split_axis=0, concat_axis=0, tiled=True)]
  transfers between devices with their start and end apart: 24 -> 1, of which waited for: 7 -> 0; matrix products, arithmetic and copies ran while one was open for 18% -> 2% of each run, Pallas kernels for 0% -> 19%
where the time goes in v4:
time: 1020 us; the launch traced here: 1010 us
  Pallas kernels  974 us (95%)
  other arithmetic  16.6 us (2%)
  local copies, waits for them, and re-layouts  11.6 us (1%)
    pallas_call x1, Pallas kernels, front(): pl.pallas_call(functools.partial(front_kernel, cfg), out_shape=outs, in_s...  428 us
    pallas_call x1, Pallas kernels, run_experts(): pl.pallas_call(functools.partial(expert_kernel, cfg), out_shape=[o[0] for...  352 us
    pallas_call x1, Pallas kernels, run_back(): pl.pallas_call(functools.partial(back_kernel, cfg), out_shape=[o[0] for o...  194 us
  transfers between devices with their start and end apart: 1, of which 0 were waited for; matrix products, arithmetic and copies ran while one was open for 2% of the time, Pallas kernels for 19%

profile of v4, /device:TPU:0, one launch (start us, length us, event | category | flops | bytes accessed | tf_op | source)
XLA Modules:
  0.0 1008.1 jit_solution(8175349182840476252)
XLA Ops:
  0.7 0.8 copy.37
  1.4 0.6 pad.4.rt_ref
  2.1 0.7 maximum_convert_fusion
  2.8 0.3 dynamic_update_slice.3.gt_ref
  3.1 0.0 copy-start.6
  3.1 0.6 copy-done.6
  3.7 427.9 %front.1 = (bf16[1536,2048]{1,0:T(8,128)(2,1)}, bf16[3,8,4,64,256]{4,3,2,1,0:T(8,128)(2,1)}, f32[1536,768]{1,0:T(8,128)}, f32[8,1536]{1,0:T(8,128)}, bf16[3,1536...) custom-call(bf16[192,2048]{1,0:T(8,128)(2,1)} %bitcast.46, ...), custom_call_target="tpu_custom_call" | custom-call | tf_op jit(solution)/shard_map/front/pallas_call | solution.py:477
  431.6 2.0 copy.38
  433.7 351.6 %experts.1 = (bf16[192,2048]{1,0:T(8,128)(2,1)}, f32[192,2048]{1,0:T(8,128)}, bf16[192,2048]{1,0:T(8,128)(2,1)}, bf16[128,192]{1,0:T(8,128)(2,1)}, f32[8,2048]{1...) custom-call(bf16[2048,2048]{1,0:T(8,128)(2,1)} %bitcast.40, ...), custom_call_target="tpu_custom_call" | custom-call | tf_op jit(solution)/shard_map/experts/pallas_call | solution.py:841
  785.3 1.6 fusion
  786.9 1.2 all_to_all.8
  788.1 3.5 all-to-all-start
  791.6 194.4 %back.1 = (f32[192,2048]{1,0:T(8,128)}, f32[3,64,2048]{2,1,0:T(8,128)}, f32[64,2048]{1,0:T(8,128)}, f32[8,2048]{1,0:T(8,128)}, bf16[4,512,1024]{2,1,0:T(8,128)(2...) custom-call(bf16[192,2048]{1,0:T(8,128)(2,1)} %bitcast.47, ...), custom_call_target="tpu_custom_call" | custom-call | tf_op jit(solution)/shard_map/back/pallas_call | solution.py:1226
  985.9 0.8 constant_dynamic-slice_fusion
  986.7 0.5 slice_bitcast_fusion.3
  987.2 0.0 copy-start.1
  987.2 6.8 convert_element_type.16
  994.0 0.0 copy-done.1
  994.0 0.0 copy-start
  994.0 4.4 convert_element_type.15
  998.5 0.0 copy-done
  998.5 0.0 copy-start.3
  998.5 0.0 copy-start.4
  998.5 4.4 convert_element_type.17
  1002.9 0.0 copy-start.2
  1002.9 0.0 copy-start.5
  1002.9 0.0 copy-done.3
  1002.9 1.2 slice_bitcast_fusion
  1004.1 0.0 all-to-all-done
  1004.1 0.2 reduce_sum.9
  1004.3 0.1 reshape.71
  1004.4 0.7 copy.41
  1005.0 0.0 copy-done.4
  1005.0 0.9 copy.47
  1005.9 0.0 copy-done.2
  1005.9 1.1 copy.48
  1007.1 0.0 copy-done.5
  1007.1 0.8 copy.49
  (1 shorter events, 0.0 us)
Async XLA Ops:
  3.1 0.6 copy-start.6
  788.1 216.0 %all-to-all-start = ((f32[32,1,2048]{2,1,0:T(1,128)}), f32[32,1,2048]{2,1,0:T(1,128)S(1)}, u32[]{:S(2)}, u32[]{:S(2)}) async-start(f32[32,1,2048]{2,1,0:T(1,128)} %all_to_all.8), calls=%async_computation | async-start | bytes 524288 | tf_op jit(solution)/shard_map/all_to_all | solution.py:22
  987.2 6.8 copy-start.1
  994.0 4.4 copy-start
  998.5 4.5 copy-start.3
  998.5 6.6 copy-start.4
  1002.9 3.0 copy-start.2
  1002.9 4.1 copy-start.5

commit v5 on v4

--- a/solution.py
+++ b/solution.py
@@ -136,6 +136,7 @@
     links = Links(sends, recvs, locals_)
     ds = pl.ds
     same = [d for d in range(2, nc, 2)]
+    steps = bits_down(nz)
 
     own = []
     own.append(links.move(x_ref, xbuf.at[ds(c * tokens, tokens)]))
@@ -162,11 +163,24 @@
     for s in range(1, nz):
         for src, dst in ((gt_ref, gbuf), (rt_ref, rbuf), (ro_ref, tbuf)):
             small_z.append(links.send(src, dst.at[c, z], fsdp=z ^ s))
+    wo_near, cot_copies = {}, {}
+
+    def wo_send(s, bit):
+        place = obw.at[c, z ^ s]
+        wo_near[s | bit] = links.send(place, place, fsdp=z ^ bit)
+
+    def cot_send(s, bit):
+        cot_copies[s | bit] = links.send(cbuf.at[s], cbuf.at[s | bit], fsdp=z ^ bit)
+
     x_at = xbuf.at[ds(c * tokens, tokens)]
     x_same = {d: links.send(x_ref, x_at, ctx=c ^ d) for d in same}
     x_side = [links.send(x_ref, x_at, ctx=c ^ 1)]
     for copy in own:
         links.left(copy)
+    for bit in steps:
+        wo_send(0, bit)
+    for bit in steps:
+        cot_send(0, bit)
 
     for copy in slices:
         links.arrived(copy)
@@ -176,18 +190,8 @@
         place = wbuf.at[:, :, z ^ s]
         w_near[s | bit] = links.send(place, place, fsdp=z ^ bit)
 
-    steps = bits_down(nz)
     for bit in steps:
         w_send(0, bit)
-    wo_near, cot_copies = {}, {}
-
-    def wo_send(s, bit):
-        place = obw.at[c, z ^ s]
-        wo_near[s | bit] = links.send(place, place, fsdp=z ^ bit)
-
-    def cot_send(s, bit):
-        cot_copies[s | bit] = links.send(cbuf.at[s], cbuf.at[s | bit], fsdp=z ^ bit)
-
     for copy in small_z:
         links.arrived(copy)
     small_c = []
@@ -209,10 +213,6 @@
                 send(s, bit)
 
     forward(w_near, w_send)
-    for bit in steps:
-        wo_send(0, bit)
-    for bit in steps:
-        cot_send(0, bit)
     for copy in small_c:
         links.arrived(copy)
     per = 128 // rows_w
@@ -492,7 +492,7 @@
     rows_ref, cotr_ref, rt_ref, tb_ref, wg_ref, wu_ref, wd_ref, near_ref, cotn_ref, r1_ref, gain_ref,
     hidden_out, dr1_out, datt_out, dlog_out, fgain_out, gd_land, gg_land, gu_out,
     back, in_back, out_land, in_land, ebh, rbh,
-    wg, wu, wd, rows, cotb, gin, dg, du, eb, rb, tile, ranks, hot, metab, dgs, dgl,
+    wg, wu, wd, rows, cotb, gin, gdb, du, eb, rb, tile, ranks, hot, metab, gate_rows, dgs, dgl,
     sends, recvs, locals_,
 ):
     nc, nz, tokens, width = cfg["nc"], cfg["nz"], cfg["tokens"], cfg["width"]
@@ -574,14 +574,14 @@
     sub = min(256, ch)
     lane = lax.broadcasted_iota(jnp.int32, (sub, 128), 1)
 
-    def work(i, _):
-        s = nz - 1 - i
-        slot = lax.rem(i, 2)
-
-        @pl.when(i + 1 < nz)
-        def _():
-            cot_load(s - 1, 1 - slot).start()
-
+    def gate_of(block, picked):
+        logits = kdot(block, rt_ref[...], ((1,), (1,)))
+        logits = jnp.where(picked > 0.5, logits, neg_large)
+        weight = jnp.exp(logits - jnp.max(logits, axis=-1, keepdims=True))
+        gate = jnp.sum(jnp.where(lane == expert, weight, 0.0), axis=-1, keepdims=True)
+        return gate / jnp.sum(weight, axis=-1, keepdims=True)
+
+    def first_work(s, _):
         for k in range(nc):
             block = tb_ref[k, z ^ s]
             found = jnp.where(block == expert, 1.0, 0.0)
@@ -593,29 +593,79 @@
             metab[k * cap : (k + 1) * cap, :] = kdot(
                 hot[k * cap : (k + 1) * cap, :], chosen, ((1,), (1,))
             )
-        cot_load(s, slot).wait()
 
         def some_rows(j, _):
             here = pl.multiple_of(j * sub, sub)
             at = pl.multiple_of(s * ch + j * sub, sub)
             span, to = ds(here, sub), ds(at, sub)
             block = rows[to, :]
-            logits = kdot(block, rt_ref[...], ((1,), (1,)))
-            logits = jnp.where(metab[span, :] > 0.5, logits, neg_large)
-            weight = jnp.exp(logits - jnp.max(logits, axis=-1, keepdims=True))
-            gate = jnp.sum(jnp.where(lane == expert, weight, 0.0), axis=-1, keepdims=True)
-            gate = gate / jnp.sum(weight, axis=-1, keepdims=True)
+            gate = gate_of(block, metab[span, :])
+            g = kdot(block, wg[...])
+            u = kdot(block, wu[...])
+            inner = (g * (1.0 / (1.0 + jnp.exp(-g))) * u).astype(low)
+            gin[to, :] = (inner.astype(exact) * gate).astype(low)
+            gate_rows[to, :] = jnp.broadcast_to(gate, (sub, 128))
+            return 0
+
+        lax.fori_loop(0, ch // sub, some_rows, 0)
+        return 0
+
+    lax.fori_loop(0, nz, first_work, 0)
+
+    rows_d = part // nz
+    step = 256 if nz * ch <= 2048 else 128
+    tile_base = links.local_count
+    links.local_count += width // step
+
+    def tile_load(k):
+        return pltpu.make_async_copy(
+            cotr_ref.at[:, ds(k * step, step)], tile.at[lax.rem(k, 2)], locals_.at[tile_base + k]
+        )
+
+    tile_load(0).start()
+
+    def down_tile(k, _):
+        @pl.when(k + 1 < width // step)
+        def _():
+            tile_load(k + 1).start()
+
+        tile_load(k).wait()
+        at = pl.multiple_of(k * step, step)
+        gdb[:, ds(at, step)] = kdot(gin[...], tile[lax.rem(k, 2)], ((0,), (0,))).astype(low)
+        return 0
+
+    lax.fori_loop(0, width // step, down_tile, 0)
+    grads_out = []
+    for s in range(1, nz):
+        src = gdb.at[ds(pl.multiple_of((z ^ s) * rows_d, rows_d), rows_d)]
+        grads_out.append(links.send(src, gd_land.at[z], fsdp=z ^ s))
+    links.move(gdb.at[ds(pl.multiple_of(z * rows_d, rows_d), rows_d)], gd_land.at[z])
+    def work(i, _):
+        s = nz - 1 - i
+        slot = lax.rem(i, 2)
+
+        @pl.when(i + 1 < nz)
+        def _():
+            cot_load(s - 1, 1 - slot).start()
+
+        cot_load(s, slot).wait()
+
+        def some_rows(j, _):
+            here = pl.multiple_of(j * sub, sub)
+            at = pl.multiple_of(s * ch + j * sub, sub)
+            span, to = ds(here, sub), ds(at, sub)
+            block = rows[to, :]
+            gate = gate_rows[to, 0:1]
             g = kdot(block, wg[...])
             u = kdot(block, wu[...])
             sg = 1.0 / (1.0 + jnp.exp(-g))
             act = g * sg
             inner = (act * u).astype(low)
-            gin[to, :] = (inner.astype(exact) * gate).astype(low)
             eb[span, :] = kdot(inner, wd[...]).astype(low)
             dinner = kdot(cotb[slot, span, :], wd[...], ((1,), (1,))) * gate
             dg_low = (dinner * u * sg * (1.0 + g * (1.0 - sg))).astype(low)
             du_low = (dinner * act).astype(low)
-            dg[to, :] = dg_low
+            gin[to, :] = dg_low
             du[to, :] = du_low
             rb[span, :] = (
                 kdot(dg_low, wg[...], ((1,), (1,))) + kdot(du_low, wu[...], ((1,), (1,)))
@@ -634,34 +684,6 @@
 
     lax.fori_loop(0, nz, work, 0)
 
-    rows_d = part // nz
-    step = 256 if nz * ch <= 2048 else 128
-    tile_base = links.local_count
-    links.local_count += width // step
-
-    def tile_load(k):
-        return pltpu.make_async_copy(
-            cotr_ref.at[:, ds(k * step, step)], tile.at[lax.rem(k, 2)], locals_.at[tile_base + k]
-        )
-
-    tile_load(0).start()
-
-    def down_tile(k, _):
-        @pl.when(k + 1 < width // step)
-        def _():
-            tile_load(k + 1).start()
-
-        tile_load(k).wait()
-        at = pl.multiple_of(k * step, step)
-        wd[:, ds(at, step)] = kdot(gin[...], tile[lax.rem(k, 2)], ((0,), (0,))).astype(low)
-        return 0
-
-    lax.fori_loop(0, width // step, down_tile, 0)
-    grads_out = []
-    for s in range(1, nz):
-        src = wd.at[ds(pl.multiple_of((z ^ s) * rows_d, rows_d), rows_d)]
-        grads_out.append(links.send(src, gd_land.at[z], fsdp=z ^ s))
-    links.move(wd.at[ds(pl.multiple_of(z * rows_d, rows_d), rows_d)], gd_land.at[z])
     rows_g = width // nz
 
     def rows_tile(left, dst):
@@ -672,7 +694,7 @@
 
         lax.fori_loop(0, width // step, one, 0)
 
-    rows_tile(dg, wg)
+    rows_tile(gin, wg)
     for s in range(1, nz):
         src = wg.at[ds(pl.multiple_of((z ^ s) * rows_g, rows_g), rows_g)]
         grads_out.append(links.send(src, gg_land.at[z], fsdp=z ^ s))
@@ -824,7 +846,7 @@
         pltpu.VMEM((nz * ch, width), low),
         pltpu.VMEM((2, ch, width), low),
         pltpu.VMEM((nz * ch, part), low),
-        pltpu.VMEM((nz * ch, part), low),
+        pltpu.VMEM((part, width), low),
         pltpu.VMEM((nz * ch, part), low),
         pltpu.VMEM((ch, width), low),
         pltpu.VMEM((ch, width), low),
@@ -832,6 +854,7 @@
         pltpu.VMEM((nc, tokens), exact),
         pltpu.VMEM((ch, tokens), low),
         pltpu.VMEM((ch, 128), exact),
+        pltpu.VMEM((nz * ch, 128), exact),
         pltpu.VMEM((nz, nc, tokens), exact),
         pltpu.VMEM((nz, nc, tokens), exact),
         pltpu.SemaphoreType.DMA((2 * nz * nc + 8 * nz,)),

time: 1020 us -> 968 us (0.949)
  Pallas kernels: 974 us -> 927 us
    pallas_call x1, Pallas kernels: 352 us -> 312 us  [run_experts(): pl.pallas_call(functools.partial(expert_kernel, cfg), out_shape=[o[0] for...]
  transfers between devices with their start and end apart: 1 -> 1, of which waited for: 0 -> 0; matrix products, arithmetic and copies ran while one was open for 2% -> 2% of each run, Pallas kernels for 19% -> 20%
where the time goes in v5:
time: 968 us; the launch traced here: 961 us
  Pallas kernels  927 us (96%)
  other arithmetic  16.6 us (2%)
  local copies, waits for them, and re-layouts  11.6 us (1%)
    pallas_call x1, Pallas kernels, front(): pl.pallas_call(functools.partial(front_kernel, cfg), out_shape=outs, in_s...  420 us
    pallas_call x1, Pallas kernels, run_experts(): pl.pallas_call(functools.partial(expert_kernel, cfg), out_shape=[o[0] for...  312 us
    pallas_call x1, Pallas kernels, run_back(): pl.pallas_call(functools.partial(back_kernel, cfg), out_shape=[o[0] for o...  194 us
  transfers between devices with their start and end apart: 1, of which 0 were waited for; matrix products, arithmetic and copies ran while one was open for 2% of the time, Pallas kernels for 20%

profile of v5, /device:TPU:0, one launch (start us, length us, event | category | flops | bytes accessed | tf_op | source)
XLA Modules:
  0.0 960.6 jit_solution(11832846062916115334)
XLA Ops:
  0.7 0.8 copy.37
  1.4 0.6 pad.4.rt_ref
  2.1 0.7 maximum_convert_fusion
  2.8 0.3 dynamic_update_slice.3.gt_ref
  3.1 0.0 copy-start.6
  3.1 0.6 copy-done.6
  3.7 420.1 %front.1 = (bf16[1536,2048]{1,0:T(8,128)(2,1)}, bf16[3,8,4,64,256]{4,3,2,1,0:T(8,128)(2,1)}, f32[1536,768]{1,0:T(8,128)}, f32[8,1536]{1,0:T(8,128)}, bf16[3,1536...) custom-call(bf16[192,2048]{1,0:T(8,128)(2,1)} %bitcast.46, ...), custom_call_target="tpu_custom_call" | custom-call | tf_op jit(solution)/shard_map/front/pallas_call | solution.py:477
  423.8 2.0 copy.38
  425.8 312.4 %experts.1 = (bf16[192,2048]{1,0:T(8,128)(2,1)}, f32[192,2048]{1,0:T(8,128)}, bf16[192,2048]{1,0:T(8,128)(2,1)}, bf16[128,192]{1,0:T(8,128)(2,1)}, f32[8,2048]{1...) custom-call(bf16[2048,2048]{1,0:T(8,128)(2,1)} %bitcast.40, ...), custom_call_target="tpu_custom_call" | custom-call | tf_op jit(solution)/shard_map/experts/pallas_call | solution.py:864
  738.3 1.6 fusion
  739.9 1.2 all_to_all.8
  741.1 3.1 all-to-all-start
  744.2 194.4 %back.1 = (f32[192,2048]{1,0:T(8,128)}, f32[3,64,2048]{2,1,0:T(8,128)}, f32[64,2048]{1,0:T(8,128)}, f32[8,2048]{1,0:T(8,128)}, bf16[4,512,1024]{2,1,0:T(8,128)(2...) custom-call(bf16[192,2048]{1,0:T(8,128)(2,1)} %bitcast.47, ...), custom_call_target="tpu_custom_call" | custom-call | tf_op jit(solution)/shard_map/back/pallas_call | solution.py:1249
  938.5 0.8 constant_dynamic-slice_fusion
  939.3 0.5 slice_bitcast_fusion.3
  939.8 0.0 copy-start.1
  939.8 6.8 convert_element_type.16
  946.6 0.0 copy-done.1
  946.6 0.0 copy-start
  946.6 4.4 convert_element_type.15
  951.1 0.0 copy-done
  951.1 0.0 copy-start.3
  951.1 0.0 copy-start.4
  951.1 4.4 convert_element_type.17
  955.5 0.0 copy-start.2
  955.5 0.0 copy-start.5
  955.5 0.0 copy-done.3
  955.5 1.2 slice_bitcast_fusion
  956.7 0.0 all-to-all-done
  956.7 0.2 reduce_sum.9
  956.9 0.1 reshape.71
  956.9 0.7 copy.41
  957.6 0.0 copy-done.4
  957.6 0.9 copy.47
  958.5 0.0 copy-done.2
  958.5 1.1 copy.48
  959.7 0.0 copy-done.5
  959.7 0.8 copy.49
  (1 shorter events, 0.0 us)
Async XLA Ops:
  3.1 0.6 copy-start.6
  741.1 215.6 %all-to-all-start = ((f32[32,1,2048]{2,1,0:T(1,128)}), f32[32,1,2048]{2,1,0:T(1,128)S(1)}, u32[]{:S(2)}, u32[]{:S(2)}) async-start(f32[32,1,2048]{2,1,0:T(1,128)} %all_to_all.8), calls=%async_computation | async-start | bytes 524288 | tf_op jit(solution)/shard_map/all_to_all | solution.py:22
  939.8 6.8 copy-start.1
  946.6 4.4 copy-start
  951.1 4.5 copy-start.3
  951.1 6.6 copy-start.4
  955.5 3.0 copy-start.2
  955.5 4.1 copy-start.5

commit v6 on v5

--- a/solution.py
+++ b/solution.py
@@ -121,8 +121,8 @@
     cfg,
     x_ref, wq_ref, wk_ref, wv_ref, wo_ref, gt_ref, rt_ref, ro_ref, cot_ref, gp_ref, up_ref, dp_ref, cos_ref, sin_ref,
     a1_out, w_full, raw_out, stat_out, rot_out, ob_out, wo_full, r1_out, r_all, g_all, t_all,
-    gate_full, up_full, down_full, cot_rows, cot_near, in_rows, in_near,
-    xbuf, wbuf, obw, gbuf, gfull, rbuf, tbuf, raw, stat, total, rq, rk, rot, opos, odev, orecv, r1, a2, cbuf, abuf, hot, cs,
+    gate_full, up_full, down_full, cot_rows, cot_near, in_rows, in_near, staged,
+    xbuf, wbuf, obw, gbuf, gfull, rbuf, tbuf, raw, stat, total, rq, rk, rot, opos, odev, orecv, r1, xrow, cbuf, abuf, hot, cs,
     sends, recvs, locals_,
 ):
     nc, nz, tokens, width = cfg["nc"], cfg["nz"], cfg["tokens"], cfg["width"]
@@ -137,20 +137,21 @@
     ds = pl.ds
     same = [d for d in range(2, nc, 2)]
     steps = bits_down(nz)
-
+    last = steps[-1]
+
+    own_wo = links.move(wo_ref, obw.at[c, z])
+    own_cot = links.move(cot_ref, cbuf.at[0])
+    own_route = links.move(ro_ref, tbuf.at[c, z])
     own = []
-    own.append(links.move(x_ref, xbuf.at[ds(c * tokens, tokens)]))
     for j, ref in enumerate((wq_ref, wk_ref, wv_ref)):
         at = pl.multiple_of(c * cols, 128)
         own.append(links.move(ref.at[:, ds(at, cols)], wbuf.at[j, c, z]))
-    own.append(links.move(wo_ref, obw.at[c, z]))
     own.append(links.move(gt_ref, gbuf.at[c, z]))
     own.append(links.move(rt_ref, rbuf.at[c, z]))
-    own.append(links.move(ro_ref, tbuf.at[c, z]))
-    own.append(links.move(cot_ref, cbuf.at[0]))
-    mine = links.move(gp_ref.at[z], gate_full.at[z])
-    mine_up = links.move(up_ref.at[z], up_full.at[z])
-    mine_down = links.move(dp_ref.at[z], down_full.at[z])
+    own.append(links.move(x_ref, xbuf.at[ds(c * tokens, tokens)]))
+    links.move(gp_ref.at[z], gate_full.at[z])
+    links.move(up_ref.at[z], up_full.at[z])
+    links.move(dp_ref.at[z], down_full.at[z])
     greet(c, z, nc, nz)
 
     slices = []
@@ -163,7 +164,7 @@
     for s in range(1, nz):
         for src, dst in ((gt_ref, gbuf), (rt_ref, rbuf), (ro_ref, tbuf)):
             small_z.append(links.send(src, dst.at[c, z], fsdp=z ^ s))
-    wo_near, cot_copies = {}, {}
+    wo_near, cot_copies, w_near = {}, {}, {}
 
     def wo_send(s, bit):
         place = obw.at[c, z ^ s]
@@ -172,36 +173,9 @@
     def cot_send(s, bit):
         cot_copies[s | bit] = links.send(cbuf.at[s], cbuf.at[s | bit], fsdp=z ^ bit)
 
-    x_at = xbuf.at[ds(c * tokens, tokens)]
-    x_same = {d: links.send(x_ref, x_at, ctx=c ^ d) for d in same}
-    x_side = [links.send(x_ref, x_at, ctx=c ^ 1)]
-    for copy in own:
-        links.left(copy)
-    for bit in steps:
-        wo_send(0, bit)
-    for bit in steps:
-        cot_send(0, bit)
-
-    for copy in slices:
-        links.arrived(copy)
-    w_near = {}
-
     def w_send(s, bit):
         place = wbuf.at[:, :, z ^ s]
         w_near[s | bit] = links.send(place, place, fsdp=z ^ bit)
-
-    for bit in steps:
-        w_send(0, bit)
-    for copy in small_z:
-        links.arrived(copy)
-    small_c = []
-    for d in range(1, nc):
-        for buf in (gbuf, rbuf, tbuf):
-            small_c.append(links.send(buf.at[c], buf.at[c], ctx=c ^ d))
-    for d in same:
-        links.arrived(x_same[d])
-        place = xbuf.at[ds((c ^ d) * tokens, tokens)]
-        x_side.append(links.send(place, place, ctx=c ^ 1))
 
     def forward(waits, send):
         for at, bit in enumerate(steps):
@@ -212,7 +186,57 @@
                 links.arrived(waits[s])
                 send(s, bit)
 
-    forward(w_near, w_send)
+    def all_in(waits):
+        for s in range(1, nz):
+            links.arrived(waits[s])
+
+    links.left(own_wo)
+    links.left(own_route)
+    for bit in steps:
+        wo_send(0, bit)
+    x_at = xbuf.at[ds(c * tokens, tokens)]
+    x_same = {d: links.send(x_ref, x_at, ctx=c ^ d) for d in same}
+    x_side = [links.send(x_ref, x_at, ctx=c ^ 1)]
+    rows_sent = []
+    turn_of = [0]
+
+    def dispatch(s, near, landing):
+        number = turn_of[0]
+        turn_of[0] += 1
+        fill_hot(cfg, plane_ranks(cfg, tbuf[c, z ^ s], z), hot)
+        cs[...] = kdot(hot[...], near[s]).astype(low)
+        off = links.move(cs, staged.at[number])
+        links.left(off)
+        for d in range(1, nc):
+            src = staged.at[number, ds((c ^ d) * cap, cap)]
+            rows_sent.append(links.send(src, landing.at[s, c], ctx=c ^ d))
+        links.move(cs.at[ds(c * cap, cap)], landing.at[s, c])
+
+    def settle():
+        for copy, remote in list(links.open.values()):
+            if not remote:
+                links.left(copy)
+
+    for copy in own:
+        links.left(copy)
+
+    for copy in slices:
+        links.arrived(copy)
+    for bit in steps:
+        w_send(0, bit)
+    for copy in small_z:
+        links.arrived(copy)
+    small_c = []
+    for d in range(1, nc):
+        for buf in (gbuf, rbuf, tbuf):
+            small_c.append(links.send(buf.at[c], buf.at[c], ctx=c ^ d))
+    forward(wo_near, wo_send)
+    for d in same:
+        links.arrived(x_same[d])
+        place = xbuf.at[ds((c ^ d) * tokens, tokens)]
+        x_side.append(links.send(place, place, ctx=c ^ 1))
+    links.left(own_cot)
+    dispatch(0, cbuf, cot_rows)
     for copy in small_c:
         links.arrived(copy)
     per = 128 // rows_w
@@ -224,6 +248,9 @@
                 tile = tile + gbuf[k, g * per + p]
             at = (k * groups + g) * 128
             gfull[:, at : at + 128] = tile
+    all_in(wo_near)
+    wo_same = {d: links.send(obw.at[c], obw.at[c], ctx=c ^ d) for d in same}
+    wo_side = [links.send(obw.at[c], obw.at[c], ctx=c ^ 1)]
     for copy in x_side:
         links.arrived(copy)
     for copy in list(x_same.values()) + x_side:
@@ -238,17 +265,16 @@
         xbuf[ds(at, chunk), :] = v.astype(low)
         return 0
 
+    forward(w_near, w_send)
+    for bit in steps:
+        cot_send(0, bit)
     lax.fori_loop(0, length // chunk, norm_rows, 0)
-    a1_copy = links.move(xbuf, a1_out)
-
-    last = steps[-1]
-    for s in range(1, nz):
-        if s & last:
-            links.arrived(w_near[s])
+    links.move(xbuf, a1_out)
+    all_in(w_near)
     experts_in = []
     for s in range(1, nz):
         experts_in.append(links.send(gp_ref.at[z ^ s], gate_full.at[z], fsdp=z ^ s))
-    w_copy = links.move(wbuf, w_full)
+    links.move(wbuf, w_full)
 
     one_row = lax.broadcasted_iota(jnp.int32, (8, cols), 0)
     pick_q = jnp.where(one_row == 0, 1.0, 0.0)
@@ -269,14 +295,12 @@
         return 0
 
     lax.fori_loop(0, blocks, project, 0)
-    raw_copy = links.move(raw, raw_out)
     stats = [links.send(stat.at[c], stat.at[c], ctx=c ^ d) for d in range(1, nc)]
-    forward(wo_near, wo_send)
-    for s in range(1, nz):
-        if s & last:
-            links.arrived(wo_near[s])
-    wo_same = {d: links.send(obw.at[c], obw.at[c], ctx=c ^ d) for d in same}
-    wo_side = [links.send(obw.at[c], obw.at[c], ctx=c ^ 1)]
+    links.move(raw, raw_out)
+    for d in same:
+        links.arrived(wo_same[d])
+        place_at = obw.at[c ^ d]
+        wo_side.append(links.send(place_at, place_at, ctx=c ^ 1))
     for copy in stats:
         links.arrived(copy)
     summed = stat[0]
@@ -295,7 +319,10 @@
         return 0
 
     lax.fori_loop(0, blocks, columns, 0)
-    stat_copy = links.move(total, stat_out)
+    links.move(total, stat_out)
+    forward(cot_copies, cot_send)
+    for s in range(1, nz):
+        experts_in.append(links.send(up_ref.at[z ^ s], up_full.at[z], fsdp=z ^ s))
 
     def turn(i, _):
         d, side = i // 2, i % 2
@@ -313,10 +340,12 @@
         return 0
 
     lax.fori_loop(0, 2 * nc, turn, 0)
-    rot_copy = links.move(rot, rot_out)
-    forward(cot_copies, cot_send)
-    for s in range(1, nz):
-        experts_in.append(links.send(up_ref.at[z ^ s], up_full.at[z], fsdp=z ^ s))
+    links.move(rot, rot_out)
+    settle()
+    for bit in steps:
+        links.arrived(cot_copies[bit])
+        dispatch(bit, cbuf, cot_rows)
+        settle()
 
     scale = hs ** -0.5
     for h in range(heads):
@@ -340,58 +369,28 @@
         return 0
 
     lax.fori_loop(0, 2 * nc, place, 0)
-    ob_copy = links.move(odev, ob_out)
     mixed = []
     for d in range(1, nc):
         src = odev.at[ds((c ^ d) * tokens, tokens)]
         mixed.append(links.send(src, orecv.at[c], ctx=c ^ d))
     own_mixed = links.move(odev.at[ds(c * tokens, tokens)], orecv.at[c])
-    for d in same:
-        links.arrived(wo_same[d])
-        place_at = obw.at[c ^ d]
-        wo_side.append(links.send(place_at, place_at, ctx=c ^ 1))
-
-    for s in range(1, nz):
-        if s & last:
-            links.arrived(cot_copies[s])
-    near_copy = links.move(cbuf, cot_near)
-    rows_sent = []
-    slot_busy = [[], []]
-
-    def dispatch(s, near, landing):
-        slot = s % 2
-        for copy in slot_busy[slot]:
-            links.left(copy)
-        fill_hot(cfg, plane_ranks(cfg, tbuf[c, z ^ s], z), hot)
-        cs[slot] = kdot(hot[...], near[s]).astype(low)
-        busy = []
-        for d in range(1, nc):
-            src = cs.at[slot, ds((c ^ d) * cap, cap)]
-            copy = links.send(src, landing.at[s, c], ctx=c ^ d)
-            rows_sent.append(copy)
-            busy.append(copy)
-        busy.append(links.move(cs.at[slot, ds(c * cap, cap)], landing.at[s, c]))
-        slot_busy[slot] = busy
-
-    for s in range(nz):
-        dispatch(s, cbuf, cot_rows)
-
+    links.move(odev, ob_out)
+    x_in = links.move(x_ref, xrow)
     for copy in wo_side:
         links.arrived(copy)
-    wo_copy = links.move(obw, wo_full)
+    links.move(obw, wo_full)
+    r1[...] = jnp.zeros_like(r1)
     for copy in mixed:
         links.arrived(copy)
     links.left(own_mixed)
-    r1[...] = jnp.zeros_like(r1)
 
     def mix(k, _):
         r1[...] += kdot(orecv[k], obw[k].reshape(cols, width))
         return 0
 
     lax.fori_loop(0, nc, mix, 0)
-    xin = links.move(x_ref, a2)
-    links.left(xin)
-    v = r1[...] + a2[...].astype(exact)
+    links.left(x_in)
+    v = r1[...] + xrow[...].astype(exact)
     r1[...] = v
     n2 = v * lax.rsqrt(jnp.mean(v * v, axis=-1, keepdims=True) + epsilon)
     abuf[0] = (n2 * gfull[3:4, :]).astype(low)
@@ -402,16 +401,24 @@
 
     for bit in steps:
         in_send(0, bit)
+    settle()
+    dispatch(0, abuf, in_rows)
     links.move(r1, r1_out)
-    dispatch(0, abuf, in_rows)
-    forward(in_copies, in_send)
-    for s in range(1, nz):
-        experts_in.append(links.send(dp_ref.at[z ^ s], down_full.at[z], fsdp=z ^ s))
     links.move(rbuf, r_all)
     links.move(gfull, g_all)
     links.move(tbuf, t_all)
+    all_in(cot_copies)
+    links.move(cbuf, cot_near)
     for s in range(1, nz):
+        if s & (s - 1):
+            settle()
+            dispatch(s, cbuf, cot_rows)
+    forward(in_copies, in_send)
+    for s in range(1, nz - 1):
+        experts_in.append(links.send(dp_ref.at[z ^ s], down_full.at[z], fsdp=z ^ s))
+    for s in list(steps) + [s for s in range(1, nz) if s & (s - 1)]:
         links.arrived(in_copies[s])
+        settle()
         dispatch(s, abuf, in_rows)
     links.move(abuf, in_near)
     for copy in experts_in + rows_sent:
@@ -423,7 +430,6 @@
     nc, nz, tokens, width = cfg["nc"], cfg["nz"], cfg["tokens"], cfg["width"]
     cols, rows_w, length, cap = cfg["cols"], cfg["rows_w"], cfg["length"], cfg["cap"]
     rows, part = gate_pieces.shape[1:]
-    rows_d = down_pieces.shape[1]
     shape = jax.ShapeDtypeStruct
     any_, vmem = pl.BlockSpec(memory_space=pl.ANY), pl.BlockSpec(memory_space=pltpu.VMEM)
     top_rows = routes.shape[0]
@@ -441,11 +447,12 @@
         shape((nc, nz, top_rows, tokens), jnp.int32),
         shape((nz, rows, part), low),
         shape((nz, rows, part), low),
-        shape((nz, rows_d, width), low),
+        shape(down_pieces.shape, low),
         shape((nz, nc, cap, width), low),
         shape((nz, tokens, width), low),
         shape((nz, nc, cap, width), low),
         shape((nz, tokens, width), low),
+        shape((2 * nz, nc * cap, width), low),
     ]
     scratch = [
         pltpu.VMEM((length, width), low),
@@ -469,10 +476,10 @@
         pltpu.VMEM((nz, tokens, width), low),
         pltpu.VMEM((nz, tokens, width), low),
         pltpu.VMEM((nc * cap, tokens), low),
-        pltpu.VMEM((2, nc * cap, width), low),
+        pltpu.VMEM((nc * cap, width), low),
         pltpu.SemaphoreType.DMA((cfg["copies"],)),
         pltpu.SemaphoreType.DMA((cfg["copies"],)),
-        pltpu.SemaphoreType.DMA((64,)),
+        pltpu.SemaphoreType.DMA((32 + 4 * cfg["nz"],)),
     ]
     return pl.pallas_call(
         functools.partial(front_kernel, cfg),
@@ -489,7 +496,7 @@
 
 def expert_kernel(
     cfg,
-    rows_ref, cotr_ref, rt_ref, tb_ref, wg_ref, wu_ref, wd_ref, near_ref, cotn_ref, r1_ref, gain_ref,
+    rows_ref, cotr_ref, rt_ref, tb_ref, wg_ref, wu_ref, wd_ref, dp_ref, near_ref, cotn_ref, r1_ref, gain_ref,
     hidden_out, dr1_out, datt_out, dlog_out, fgain_out, gd_land, gg_land, gu_out,
     back, in_back, out_land, in_land, ebh, rbh,
     wg, wu, wd, rows, cotb, gin, gdb, du, eb, rb, tile, ranks, hot, metab, gate_rows, dgs, dgl,
@@ -506,8 +513,13 @@
     best = lax.Precision.HIGHEST
     peers = list(range(1, nc))
 
-    loads = [links.move(wg_ref, wg), links.move(wu_ref, wu), links.move(wd_ref, wd)]
-    loads.append(links.move(rows_ref, rows))
+    loads = [links.move(wg_ref, wg), links.move(wu_ref, wu), links.move(rows_ref, rows)]
+    rows_d = part // nz
+
+    def down_place(owner):
+        return wd.at[ds(pl.multiple_of(owner * rows_d, rows_d), rows_d)]
+
+    down_here = [links.move(wd_ref.at[z ^ s], down_place(z ^ s)) for s in range(nz - 1)]
     cot_base = links.local_count
     links.local_count += nz
     send_base = links.count
@@ -554,6 +566,8 @@
 
     cot_load(nz - 1, 0).start()
     greet(c, z, nc, nz)
+    far = z ^ (nz - 1)
+    down_in = [links.send(dp_ref.at[far], down_place(z), fsdp=far)]
     for copy in loads:
         links.left(copy)
 
@@ -612,7 +626,6 @@
 
     lax.fori_loop(0, nz, first_work, 0)
 
-    rows_d = part // nz
     step = 256 if nz * ch <= 2048 else 128
     tile_base = links.local_count
     links.local_count += width // step
@@ -640,6 +653,11 @@
         src = gdb.at[ds(pl.multiple_of((z ^ s) * rows_d, rows_d), rows_d)]
         grads_out.append(links.send(src, gd_land.at[z], fsdp=z ^ s))
     links.move(gdb.at[ds(pl.multiple_of(z * rows_d, rows_d), rows_d)], gd_land.at[z])
+    for copy in down_here:
+        links.left(copy)
+    for copy in down_in:
+        links.arrived(copy)
+
     def work(i, _):
         s = nz - 1 - i
         slot = lax.rem(i, 2)
@@ -816,7 +834,7 @@
     links.close()
 
 
-def run_experts(cfg, rows, cot_rows, router_t, routes, wg, wu, wd, near, cot_near, r1, gains):
+def run_experts(cfg, rows, cot_rows, router_t, routes, wg, wu, wd, down_pieces, near, cot_near, r1, gains):
     nc, nz, tokens, width = cfg["nc"], cfg["nz"], cfg["tokens"], cfg["width"]
     cap, part = cfg["cap"], cfg["part"]
     ch = nc * cap
@@ -864,14 +882,14 @@
     return pl.pallas_call(
         functools.partial(expert_kernel, cfg),
         out_shape=[o[0] for o in outs],
-        in_specs=[any_, any_, vmem, vmem, any_, any_, any_, any_, any_, vmem, vmem],
+        in_specs=[any_, any_, vmem, vmem, any_, any_, any_, any_, any_, any_, vmem, vmem],
         out_specs=[o[1] for o in outs],
         scratch_shapes=scratch,
         compiler_params=pltpu.CompilerParams(
             collective_id=1, has_side_effects=True, vmem_limit_bytes=cfg["vmem"]
         ),
         name="experts",
-    )(rows, cot_rows, router_t, routes, wg, wu, wd, near, cot_near, r1, gains)
+    )(rows, cot_rows, router_t, routes, wg, wu, wd, down_pieces, near, cot_near, r1, gains)
 
 
 def back_kernel(
@@ -1341,19 +1359,19 @@
         weight = weight.reshape(exp_local, rows, z_count, split, part // z_count)
         return weight.transpose(0, 3, 1, 2, 4).reshape(z_count, rows, part)
 
+    down_pieces = w_down.reshape(z_count, -1, width)
     cosine, sine = tables(ctx_count, tokens, head_size)
     (
         attn_all, w_full, raw, squares, rot, out_heads, wo_full, resid_one,
         router_full, gains, routes_all, gate_full, up_full, down_full, cot_rows, cot_near,
-        input_rows, input_near,
+        input_rows, input_near, *_,
     ) = front(
         cfg, hidden_in[0], w_query, w_key, w_value, w_out, gains, router_tile, route_tile,
-        cotangent[0], pieces_of(w_gate), pieces_of(w_up),
-        w_down.reshape(z_count, -1, width), cosine, sine,
+        cotangent[0], pieces_of(w_gate), pieces_of(w_up), down_pieces,
+        cosine, sine,
     )
     gate_full = gate_full.reshape(-1, part)
     up_full = up_full.reshape(-1, part)
-    down_full = down_full.reshape(-1, width)
     ffn_input = input_near[0]
     router_t = router_full.reshape(width, 128).T
     (
@@ -1361,7 +1379,7 @@
         up_grad, *_,
     ) = run_experts(
         cfg, input_rows.reshape(-1, width), cot_rows.reshape(-1, width), router_t, routes_all,
-        gate_full, up_full, down_full, input_near, cot_near, resid_one, gains,
+        gate_full, up_full, down_full, down_pieces, input_near, cot_near, resid_one, gains,
     )
     out_hidden = resid_two[None]
     router_grad = lax.dot_general(

time: 968 us -> 935 us (0.966)
  Pallas kernels: 927 us -> 891 us
    pallas_call x1, Pallas kernels: 420 us -> 388 us  [front(): pl.pallas_call(functools.partial(front_kernel, cfg), out_shape=outs, in_s...]
  transfers between devices with their start and end apart: 1 -> 1, of which waited for: 0 -> 0; matrix products, arithmetic and copies ran while one was open for 2% -> 2% of each run, Pallas kernels for 20% -> 21%
where the time goes in v6:
time: 935 us; the launch traced here: 926 us
  Pallas kernels  891 us (95%)
  other arithmetic  16.6 us (2%)
  local copies, waits for them, and re-layouts  11.6 us (1%)
    pallas_call x1, Pallas kernels, front(): pl.pallas_call(functools.partial(front_kernel, cfg), out_shape=outs, in_s...  388 us
    pallas_call x1, Pallas kernels, run_experts(): pl.pallas_call(functools.partial(expert_kernel, cfg), out_shape=[o[0] for...  309 us
    pallas_call x1, Pallas kernels, run_back(): pl.pallas_call(functools.partial(back_kernel, cfg), out_shape=[o[0] for o...  194 us
  transfers between devices with their start and end apart: 1, of which 0 were waited for; matrix products, arithmetic and copies ran while one was open for 2% of the time, Pallas kernels for 21%

profile of v6, /device:TPU:0, one launch (start us, length us, event | category | flops | bytes accessed | tf_op | source)
XLA Modules:
  0.0 926.0 jit_solution(16502513114169947273)
XLA Ops:
  0.7 0.8 copy.37
  1.4 0.6 pad.4.rt_ref
  2.1 0.7 maximum_convert_fusion
  2.8 0.3 dynamic_update_slice.3.gt_ref
  3.1 0.0 copy-start.6
  3.1 0.6 copy-done.6
  3.7 387.9 %front.1 = (bf16[1536,2048]{1,0:T(8,128)(2,1)}, bf16[3,8,4,64,256]{4,3,2,1,0:T(8,128)(2,1)}, f32[1536,768]{1,0:T(8,128)}, f32[8,1536]{1,0:T(8,128)}, bf16[3,1536...) custom-call(bf16[192,2048]{1,0:T(8,128)(2,1)} %bitcast.44, ...), custom_call_target="tpu_custom_call" | custom-call | tf_op jit(solution)/shard_map/front/pallas_call | solution.py:484
  391.6 2.0 copy.38
  393.7 308.9 %experts.1 = (bf16[192,2048]{1,0:T(8,128)(2,1)}, f32[192,2048]{1,0:T(8,128)}, bf16[192,2048]{1,0:T(8,128)(2,1)}, bf16[128,192]{1,0:T(8,128)(2,1)}, f32[8,2048]{1...) custom-call(bf16[2048,2048]{1,0:T(8,128)(2,1)} %bitcast.39, ...), custom_call_target="tpu_custom_call" | custom-call | tf_op jit(solution)/shard_map/experts/pallas_call | solution.py:882
  702.6 1.6 fusion
  704.2 1.2 all_to_all.8
  705.3 4.2 all-to-all-start
  709.5 194.3 %back.1 = (f32[192,2048]{1,0:T(8,128)}, f32[3,64,2048]{2,1,0:T(8,128)}, f32[64,2048]{1,0:T(8,128)}, f32[8,2048]{1,0:T(8,128)}, bf16[4,512,1024]{2,1,0:T(8,128)(2...) custom-call(bf16[192,2048]{1,0:T(8,128)(2,1)} %bitcast.45, ...), custom_call_target="tpu_custom_call" | custom-call | tf_op jit(solution)/shard_map/back/pallas_call | solution.py:1267
  903.9 0.8 constant_dynamic-slice_fusion
  904.6 0.5 slice_bitcast_fusion.3
  905.2 0.0 copy-start.1
  905.2 6.8 convert_element_type.16
  912.0 0.0 copy-done.1
  912.0 0.0 copy-start
  912.0 4.4 convert_element_type.15
  916.4 0.0 copy-done
  916.4 0.0 copy-start.3
  916.4 0.0 copy-start.4
  916.4 4.4 convert_element_type.17
  920.9 0.0 copy-start.2
  920.9 0.0 copy-start.5
  920.9 0.0 copy-done.3
  920.9 1.2 slice_bitcast_fusion
  922.0 0.0 all-to-all-done
  922.0 0.2 reduce_sum.9
  922.2 0.1 reshape.67
  922.3 0.7 copy.41
  923.0 0.0 copy-done.4
  923.0 0.9 copy.47
  923.9 0.0 copy-done.2
  923.9 1.1 copy.48
  925.0 0.0 copy-done.5
  925.0 0.8 copy.49
  (1 shorter events, 0.0 us)
Async XLA Ops:
  3.1 0.6 copy-start.6
  705.3 216.7 %all-to-all-start = ((f32[32,1,2048]{2,1,0:T(1,128)}), f32[32,1,2048]{2,1,0:T(1,128)S(1)}, u32[]{:S(2)}, u32[]{:S(2)}) async-start(f32[32,1,2048]{2,1,0:T(1,128)} %all_to_all.8), calls=%async_computation | async-start | bytes 524288 | tf_op jit(solution)/shard_map/all_to_all | solution.py:22
  905.2 6.8 copy-start.1
  912.0 4.4 copy-start
  916.4 4.5 copy-start.3
  916.4 6.6 copy-start.4
  920.9 3.0 copy-start.2
  920.9 4.1 copy-start.5

commit v7 on v6

--- a/solution.py
+++ b/solution.py
@@ -1093,31 +1093,34 @@
     lax.fori_loop(0, nc, w_tile, 0)
     home = {}
 
-    def send_home(s):
+    def send_home(j, s):
         peer = z ^ (s & -s)
-        home[s] = (
-            links.send(gw.at[:, :, z ^ s], wz_land.at[s], fsdp=peer),
-            links.send(go.at[z ^ s], oz_land.at[s], fsdp=peer),
-        )
-
-    def taken(s):
-        w_sum = gw[:, :, z ^ s].astype(exact)
-        o_sum = go[z ^ s].astype(exact)
+        home[j, s] = [links.send(gw.at[j, :, z ^ s], wz_land.at[s, j], fsdp=peer)]
+        if j == 2:
+            home[j, s].append(links.send(go.at[z ^ s], oz_land.at[s], fsdp=peer))
+
+    def taken(j, s):
+        w_sum = gw[j, :, z ^ s].astype(exact)
+        o_sum = go[z ^ s].astype(exact) if j == 2 else None
         bit = 1
         while bit < nz and (s == 0 or bit < (s & -s)):
-            for copy in home[s | bit]:
+            for copy in home[j, s | bit]:
                 links.arrived(copy)
-            got = [links.move(wz_land.at[s | bit], wtemp), links.move(oz_land.at[s | bit], otemp)]
+            got = [links.move(wz_land.at[s | bit, j], wtemp.at[j])]
+            if j == 2:
+                got.append(links.move(oz_land.at[s | bit], otemp))
             for copy in got:
                 links.left(copy)
-            w_sum += wtemp[...].astype(exact)
-            o_sum += otemp[...].astype(exact)
+            w_sum += wtemp[j].astype(exact)
+            if j == 2:
+                o_sum += otemp[...].astype(exact)
             bit *= 2
         return w_sum, o_sum
 
-    for s in range(nz - 1, 0, -1):
-        if s & 1:
-            send_home(s)
+    for j in range(3):
+        for s in range(nz - 1, 0, -1):
+            if s & 1:
+                send_home(j, s)
 
     def partial(k):
         at = pl.multiple_of(k * tokens, tokens)
@@ -1156,12 +1159,14 @@
             grad_in = mine[...].astype(exact) + xtemp[...].astype(exact)
             hidden_out[...] = grad_in
 
-    for s in range(nz - 2, 0, -1):
-        if not s & 1:
-            w_sum, o_sum = taken(s)
-            gw[:, :, z ^ s] = w_sum.astype(low)
-            go[z ^ s] = o_sum.astype(low)
-            send_home(s)
+    for j in range(3):
+        for s in range(nz - 2, 0, -1):
+            if not s & 1:
+                w_sum, o_sum = taken(j, s)
+                gw[j, :, z ^ s] = w_sum.astype(low)
+                if j == 2:
+                    go[z ^ s] = o_sum.astype(low)
+                send_home(j, s)
 
     for m, d in enumerate(evens):
         if d:
@@ -1184,6 +1189,13 @@
 
     small_z[0] = gains_out[...]
     z_sums = [links.send(small_z.at[0], small_z.at[s], fsdp=z ^ s) for s in range(1, nz)]
+    for j in range(3):
+        w_sum, o_sum = taken(j, 0)
+        if j == 2:
+            wo_out[...] = o_sum
+        wsum[j] = w_sum.astype(low)
+    w_home = [links.send(wsum.at[:, c ^ d], wl.at[:, c], ctx=c ^ d) for d in range(1, nc)]
+    w_own = links.move(wsum.at[:, c], wl.at[:, c])
     for copy in z_sums:
         links.arrived(copy)
     v = small_z[0]
@@ -1191,24 +1203,18 @@
         v += small_z[s]
     small_c[0] = v
     c_sums = [links.send(small_c.at[0], small_c.at[d], ctx=c ^ d) for d in range(1, nc)]
+    for copy in w_home:
+        links.arrived(copy)
+    links.left(w_own)
+    for j in range(3):
+        for k in range(nc):
+            w_out[j, :, k * cols : (k + 1) * cols] = wl[j, k].astype(exact)
     for copy in c_sums:
         links.arrived(copy)
     v = small_c[0]
     for d in range(1, nc):
         v += small_c[d]
     gains_out[...] = v
-
-    w_sum, o_sum = taken(0)
-    wo_out[...] = o_sum
-    wsum[...] = w_sum.astype(low)
-    w_home = [links.send(wsum.at[:, c ^ d], wl.at[:, c], ctx=c ^ d) for d in range(1, nc)]
-    w_own = links.move(wsum.at[:, c], wl.at[:, c])
-    for copy in w_home:
-        links.arrived(copy)
-    links.left(w_own)
-    for j in range(3):
-        for k in range(nc):
-            w_out[j, :, k * cols : (k + 1) * cols] = wl[j, k].astype(exact)
     for copy in up_sends:
         links.arrived(copy)
     links.close()

time: 935 us -> 930 us (level)
  no operation moved by 1% of the time
where the time goes in v7:
time: 930 us; the launch traced here: 921 us
  Pallas kernels  886 us (95%)
  other arithmetic  16.6 us (2%)
  local copies, waits for them, and re-layouts  11.6 us (1%)
    pallas_call x1, Pallas kernels, front(): pl.pallas_call(functools.partial(front_kernel, cfg), out_shape=outs, in_s...  388 us
    pallas_call x1, Pallas kernels, run_experts(): pl.pallas_call(functools.partial(expert_kernel, cfg), out_shape=[o[0] for...  309 us
    pallas_call x1, Pallas kernels, run_back(): pl.pallas_call(functools.partial(back_kernel, cfg), out_shape=[o[0] for o...  189 us
  transfers between devices with their start and end apart: 1, of which 0 were waited for; matrix products, arithmetic and copies ran while one was open for 2% of the time, Pallas kernels for 21%

profile of v7, /device:TPU:0, one launch (start us, length us, event | category | flops | bytes accessed | tf_op | source)
XLA Modules:
  0.0 920.7 jit_solution(18289449516330879834)
XLA Ops:
  0.7 0.8 copy.37
  1.4 0.6 pad.4.rt_ref
  2.1 0.7 maximum_convert_fusion
  2.8 0.3 dynamic_update_slice.3.gt_ref
  3.1 0.0 copy-start.6
  3.1 0.6 copy-done.6
  3.7 387.9 %front.1 = (bf16[1536,2048]{1,0:T(8,128)(2,1)}, bf16[3,8,4,64,256]{4,3,2,1,0:T(8,128)(2,1)}, f32[1536,768]{1,0:T(8,128)}, f32[8,1536]{1,0:T(8,128)}, bf16[3,1536...) custom-call(bf16[192,2048]{1,0:T(8,128)(2,1)} %bitcast.44, ...), custom_call_target="tpu_custom_call" | custom-call | tf_op jit(solution)/shard_map/front/pallas_call | solution.py:484
  391.6 2.0 copy.38
  393.7 308.9 %experts.1 = (bf16[192,2048]{1,0:T(8,128)(2,1)}, f32[192,2048]{1,0:T(8,128)}, bf16[192,2048]{1,0:T(8,128)(2,1)}, bf16[128,192]{1,0:T(8,128)(2,1)}, f32[8,2048]{1...) custom-call(bf16[2048,2048]{1,0:T(8,128)(2,1)} %bitcast.39, ...), custom_call_target="tpu_custom_call" | custom-call | tf_op jit(solution)/shard_map/experts/pallas_call | solution.py:882
  702.6 1.6 fusion
  704.2 1.2 all_to_all.8
  705.3 4.2 all-to-all-start
  709.5 189.0 %back.1 = (f32[192,2048]{1,0:T(8,128)}, f32[3,64,2048]{2,1,0:T(8,128)}, f32[64,2048]{1,0:T(8,128)}, f32[8,2048]{1,0:T(8,128)}, bf16[4,512,1024]{2,1,0:T(8,128)(2...) custom-call(bf16[192,2048]{1,0:T(8,128)(2,1)} %bitcast.45, ...), custom_call_target="tpu_custom_call" | custom-call | tf_op jit(solution)/shard_map/back/pallas_call | solution.py:1273
  898.6 0.8 constant_dynamic-slice_fusion
  899.3 0.5 slice_bitcast_fusion.3
  899.9 0.0 copy-start.1
  899.9 6.8 convert_element_type.16
  906.6 0.0 copy-done.1
  906.7 0.0 copy-start
  906.7 4.4 convert_element_type.15
  911.1 0.0 copy-done
  911.1 0.0 copy-start.3
  911.1 0.0 copy-start.4
  911.1 4.4 convert_element_type.17
  915.6 0.0 copy-start.2
  915.6 0.0 copy-start.5
  915.6 0.0 copy-done.3
  915.6 1.2 slice_bitcast_fusion
  916.7 0.0 all-to-all-done
  916.7 0.2 reduce_sum.9
  916.9 0.1 reshape.67
  917.0 0.7 copy.41
  917.7 0.0 copy-done.4
  917.7 0.9 copy.47
  918.5 0.0 copy-done.2
  918.6 1.1 copy.48
  919.7 0.0 copy-done.5
  919.7 0.8 copy.49
  (1 shorter events, 0.0 us)
Async XLA Ops:
  3.1 0.6 copy-start.6
  705.3 211.4 %all-to-all-start = ((f32[32,1,2048]{2,1,0:T(1,128)}), f32[32,1,2048]{2,1,0:T(1,128)S(1)}, u32[]{:S(2)}, u32[]{:S(2)}) async-start(f32[32,1,2048]{2,1,0:T(1,128)} %all_to_all.8), calls=%async_computation | async-start | bytes 524288 | tf_op jit(solution)/shard_map/all_to_all | solution.py:22
  899.9 6.8 copy-start.1
  906.7 4.4 copy-start
  911.1 4.5 copy-start.3
  911.1 6.6 copy-start.4
  915.6 3.0 copy-start.2
  915.6 4.1 copy-start.5
